TPU v7x, 32 devices: a whole 2x2x4 slice. The times are simulated.
32 devices in a mesh: gx: 8 (over y, x, core), col: 4 (over z).
Axes of the slice: x: 2, y: 2, z: 4, core: 2. Of those that a mesh axis runs over, the one named last changes fastest.
Arguments:
- resid: float32 [8, 4, 32, 1024], P('gx', 'col'), may hold values from -6 to 6
- direction: float32 [8, 4, 32, 1024], P('gx', 'col'), may hold values from -6 to 6
- rz_prev: float32 [32], replicated, may hold values from 10922 to 49152
- schur: bfloat16 [8, 4, 1024, 1024], P('gx', 'col'), may hold values from -1 to 4
- neumann: bfloat16 [8, 4, 1024, 1024], P('gx', 'col'), may hold values from -1 to 4
- basis: bfloat16 [8, 4, 1024, 20], P('gx', 'col'), may hold values from -0.375 to 0.375
- coarse_inv: bfloat16 [4, 8, 20, 8, 4, 20], P('col', None, None, 'gx'), may hold values from -1 to 4
- conduct: float32 [8, 4], replicated, may hold values from 0.01 to 100
- face_perm: int32 [8, 4, 8], P('gx', 'col'), may hold values from 0 to 7, each once within a row
Outputs:
- resid_next: float32 [8, 4, 32, 1024], P('gx', 'col')
- direction_next: float32 [8, 4, 32, 1024], P('gx', 'col')
- rz_next: float32 [32], replicated
All inputs are finite; a program needn't handle non-finite values.
Results may differ from a plain program's by a relative error of at most 0.018.
Values may be sent and summed in bfloat16 or wider, within the bound.
No kernel may reach another device: no remote copies, remote signals or barrier semaphores. Data moves between devices by JAX's collectives and lax.ppermute only.
A program may use at most 64 MiB of HBM per device.

v0:
```python
import jax
import jax.numpy as jnp
from jax import lax
from jax.sharding import PartitionSpec as P


def passed_along(value, axis, steps):
    count = lax.axis_size(axis)
    initial, last = (max(0, -steps), min(count, count - steps))
    return lax.ppermute(value, axis, [(source, source + steps) for source in range(initial, last)])


def passed_along_2(shard, axis, by):
    count = lax.axis_size(axis)
    return lax.ppermute(shard, axis, [(i, (i + by) % count) for i in range(count)])


def face_sum(values, face_order, inverse, per_face):
    row_count = values.shape[0]
    block_count = face_order.shape[0]
    blocks = values.reshape(row_count, block_count, values.shape[1] // block_count)
    slotted = jnp.take(blocks, face_order, axis=1)
    lower_face = slotted[:, 0:per_face]
    upper_face = slotted[:, per_face : 2 * per_face]
    prev_face = slotted[:, 2 * per_face : 3 * per_face]
    next_face = slotted[:, 3 * per_face :]
    from_below = passed_along(upper_face.astype(jnp.bfloat16), "gx", 1).astype(upper_face.dtype)
    from_above = passed_along(lower_face.astype(jnp.bfloat16), "gx", -1).astype(lower_face.dtype)
    from_left = passed_along_2(next_face.astype(jnp.bfloat16), "col", 1).astype(next_face.dtype)
    from_right = passed_along_2(prev_face, "col", -1)
    received = jnp.concatenate([from_below, from_above, from_left, from_right], axis=1)
    returned = jnp.take(received, inverse, axis=1)
    return values + returned.reshape(values.shape)


def body(resid, direction, rz_prev, schur, neumann, basis, coarse_inv, conduct, face_perm):
    width = resid.shape[3]
    block_count = face_perm.shape[2]
    block_len = width // block_count
    per_face = block_count // 4
    prim_count = basis.shape[3]
    slab_index = lax.axis_index("gx")
    sector_index = lax.axis_index("col")
    slab_count = lax.axis_size("gx")
    sector_count = lax.axis_size("col")
    face_order = face_perm[0, 0]
    positions = jnp.arange(block_count, dtype=jnp.int32)
    matches = face_order[:, None] == positions[None, :]
    inverse = jnp.sum(jnp.where(matches, positions[:, None], 0), axis=0)
    own_rho = conduct[slab_index, sector_index]
    below_rho = jnp.where(
        slab_index > 0, conduct[jnp.maximum(slab_index - 1, 0), sector_index], 0.0
    )
    above_rho = jnp.where(
        slab_index < slab_count - 1,
        conduct[jnp.minimum(slab_index + 1, slab_count - 1), sector_index],
        0.0,
    )
    left_rho = conduct[slab_index, (sector_index + sector_count - 1) % sector_count]
    right_rho = conduct[slab_index, (sector_index + 1) % sector_count]
    others = jnp.stack([below_rho, above_rho, left_rho, right_rho])
    face_weight = own_rho / (own_rho + others)
    slot_weight = jnp.repeat(face_weight, per_face)
    weight = jnp.repeat(jnp.take(slot_weight, inverse), block_len)[None, :]
    resid_local = resid[0, 0]
    dir_local = direction[0, 0]
    image_part = jnp.dot(
        dir_local.astype(jnp.bfloat16), schur[0, 0], preferred_element_type=jnp.float32
    )
    curvature = lax.psum(jnp.sum(dir_local * image_part, axis=1), ("gx", "col"))
    step_len = rz_prev / curvature
    assembled = face_sum(image_part, face_order, inverse, per_face)
    resid_new = resid_local - step_len[:, None] * assembled
    scaled = weight * resid_new
    scaled_b = scaled.astype(jnp.bfloat16)
    basis_local = basis[0, 0]
    coarse_rhs = lax.dot_general(
        basis_local, scaled_b, (((0,), (1,)), ((), ())), preferred_element_type=jnp.float32
    ).astype(jnp.bfloat16)
    gathered = lax.all_gather(coarse_rhs[None], "col", axis=0, tiled=True)
    rhs_matrix = gathered.reshape(sector_count * prim_count, gathered.shape[2])
    block_matrix = coarse_inv[0, :, :, 0].reshape(
        coarse_inv.shape[1] * prim_count, coarse_inv.shape[4] * prim_count
    )
    partial_all = jnp.dot(block_matrix, rhs_matrix, preferred_element_type=jnp.float32)
    summed_all = lax.psum(partial_all.astype(jnp.bfloat16), "gx").astype(jnp.float32)
    coarse_sol = lax.dynamic_slice_in_dim(summed_all, slab_index * prim_count, prim_count, 0)
    coarse_b = coarse_sol.astype(jnp.bfloat16)
    correction = lax.dot_general(
        coarse_b, basis_local, (((0,), (1,)), ((), ())), preferred_element_type=jnp.float32
    )
    local_sol = jnp.dot(scaled_b, neumann[0, 0], preferred_element_type=jnp.float32) + correction
    rz_next = lax.psum(jnp.sum(scaled * local_sol, axis=1), ("gx", "col"))
    precond = face_sum(weight * local_sol, face_order, inverse, per_face)
    direction_new = precond + (rz_next / rz_prev)[:, None] * dir_local
    return (resid_new[None, None], direction_new[None, None], rz_next)


def solution(mesh):
    placed = (
        P("gx", "col", None, None),
        P("gx", "col", None, None),
        P(),
        P("gx", "col", None, None),
        P("gx", "col", None, None),
        P("gx", "col", None, None),
        P("col", None, None, "gx", None, None),
        P(),
        P("gx", "col", None),
    )
    return jax.shard_map(
        body,
        mesh=mesh,
        in_specs=placed,
        out_specs=(P("gx", "col", None, None), P("gx", "col", None, None), P()),
        check_vma=False,
    )
```

profile of v0, /device:TPU:0, one launch (start us, length us, event | category | flops | bytes accessed | tf_op | source)
XLA Modules:
  0.0 148.7 jit_solution(17916309657454218332)
XLA Ops:
  0.6 0.0 copy-start
  0.6 0.0 copy-start.7
  0.7 0.0 copy-start.6
  0.7 0.0 copy-start.4
  0.7 0.8 compare_select_fusion.1
  1.5 0.7 compare_and_fusion.1
  2.1 0.1 copy-done
  2.2 0.0 copy-start.8
  2.2 0.0 copy-start.5
  2.2 1.6 %fusion.13 = (f32[32]{0:T(128)S(1)}, f32[32,1024]{1,0:T(8,128)S(1)}) fusion(f32[1,1,32,1024]{3,2,1,0:T(8,128)} %param.12, bf16[1,1,1024,1024]{3,2,1,0:T(8,128)(2,1)S(1)} %copy-done), kind=kOutput, calls=%fused_computation.26 | convolution fusion | flops 67207136 | bytes 2359424 | tf_op jit(solution)/shard_map/dot_general | solution.py:67
  3.8 0.0 copy-start.3
  3.9 0.6 gather_fusion.1
  4.4 0.1 fusion.24
  4.5 2.4 %collective-permute-start = (bf16[32,2,128]{2,0,1:T(8,128)(2,1)S(1)}, bf16[32,2,128]{2,0,1:T(8,128)(2,1)S(1)}, u32[]{:S(2)}, u32[]{:S(2)}) collective-permute-start(bf16[32,2,128]{2,0,1:T(8,128)(2,1)S(1)} %get-tuple-element.15), channel_id=1, source_target_pairs={{0,4},{4,8},{8,12},{12,16},{16,20},{20,24},{24,28},{1,5},{5,9},{9,... | collective-permute-start | bytes 49160 | tf_op jit(solution)/shard_map/ppermute | solution.py:10
  6.9 1.3 collective-permute-start.1
  8.2 2.5 %collective-permute-start.2 = (bf16[32,2,128]{2,0,1:T(8,128)(2,1)S(1)}, bf16[32,2,128]{2,0,1:T(8,128)(2,1)S(1)}, u32[]{:S(2)}, u32[]{:S(2)}) collective-permute-start(bf16[32,2,128]{2,0,1:T(8,128)(2,1)S(1)} %get-tuple-element.16), channel_id=1, source_target_pairs={{0,1},{1,2},{2,3},{3,0},{4,5},{5,6},{6,7},{7,4},{8,9},{9,10},{10,1... | collective-permute-start | bytes 49160 | tf_op jit(solution)/shard_map/ppermute | solution.py:15
  10.7 2.1 %collective-permute-start.3 = (f32[32,2,128]{2,0,1:T(8,128)S(1)}, f32[32,2,128]{2,0,1:T(8,128)S(1)}, u32[]{:S(2)}, u32[]{:S(2)}) collective-permute-start(f32[32,2,128]{2,0,1:T(8,128)S(1)} %slice.51), channel_id=1, source_target_pairs={{0,3},{1,0},{2,1},{3,2},{4,7},{5,4},{6,5},{7,6},{8,11},{9,8},{10,9... | collective-permute-start | bytes 98312 | tf_op jit(solution)/shard_map/ppermute | solution.py:15
  12.8 0.0 copy-done.7
  12.8 0.1 select_reduce_fusion
  12.9 0.0 copy-done.6
  12.9 0.7 fusion.27
  14.9 2.0 %fusion.21 = f32[4]{0:T(128)S(1)} fusion(f32[1]{0:T(128)} %bitcast.14, f32[1]{0:T(128)} %bitcast.13, f32[1]{0:T(128)} %bitcast.12, f32[1]{0:T(128)} %bitcast.10, f32[]{:T(128)} %bitcast.8), kind=kLoop, calls=%fused_computation.54 | loop fusion | flops 20 | bytes 36 | tf_op jit(solution)/shard_map/div | solution.py:62
  16.9 0.1 broadcast_in_dim.45
  17.0 0.1 reshape.54
  17.1 0.6 gather_fusion
  17.7 0.1 broadcast_bitcast_fusion
  17.8 41.4 %psum.21 = f32[32]{0:T(128)S(1)} all-reduce(f32[32]{0:T(128)S(1)} %get-tuple-element.23), channel_id=1, replica_groups=mesh['gx'=8,'col'=4] {'gx','col'}, use_global_device_ids=true, to_apply=%region_1.2 | all-reduce | flops 32 | bytes 256 | tf_op jit(solution)/shard_map/psum | solution.py:70
  59.2 0.0 copy-done.4
  59.2 0.1 reshape_squeeze.3
  59.3 0.0 copy-done.8
  59.4 0.0 collective-permute-done
  59.4 0.0 collective-permute-done.1
  59.4 0.0 collective-permute-done.2
  59.4 0.0 collective-permute-done.3
  59.5 0.6 gather_fusion.2
  60.0 0.0 copy-done.5
  60.0 0.1 fusion.12
  60.1 0.0 copy-done.3
  60.1 0.0 copy-start.1
  60.2 0.1 fusion.8
  60.3 13.1 %all-gather.1 = bf16[4,20,32]{2,1,0:T(8,128)(2,1)S(1)} all-gather(bf16[1,20,32]{2,1,0:T(8,128)(2,1)S(1)} %fusion.8), channel_id=2, replica_groups=mesh['gx'=8,'col'=4] {'col'}, dimensions={0}, use_global_device_ids=true | all-gather | bytes 6400 | tf_op jit(solution)/shard_map/all_gather | solution.py:80
  73.4 0.2 fusion.7
  73.6 22.9 %psum.22 = bf16[160,32]{0,1:T(8,128)(2,1)S(1)} all-reduce(bf16[160,32]{0,1:T(8,128)(2,1)S(1)} %fusion.7), channel_id=1, replica_groups=mesh['gx'=8,'col'=4] {'gx'}, use_global_device_ids=true, to_apply=%region_3.5 | all-reduce | flops 5120 | bytes 20480 | tf_op jit(solution)/shard_map/psum | solution.py:86
  96.5 0.2 fusion.16
  96.7 0.0 copy-start.2
  96.7 2.1 %fusion.4 = f32[32,1024]{1,0:T(8,128)S(1)} fusion(f32[32,1024]{1,0:T(8,128)S(1)} %fusion.16, bf16[1,1,1024,1024]{3,2,1,0:T(8,128)(2,1)} %param.15, f32[32,1024]{1,0:T(8,128)S(1)} %fusion.12, f32[1024]{0:T(1024)S(1)} %broadcast_bitcast_fusion), kind=kOutput, calls=%fused_computation.9 | convolution fusion | flops 67207168 | bytes 2494464 | tf_op jit(solution)/shard_map/dot_general | solution.py:92
  98.8 0.1 multiply_reduce_fusion
  99.0 0.6 gather_fusion.3
  99.5 0.1 fusion.23
  99.6 0.0 copy-done.1
  99.6 2.2 %collective-permute-start.7 = (f32[32,2,128]{2,0,1:T(8,128)S(1)}, f32[32,2,128]{2,0,1:T(8,128)S(1)}, u32[]{:S(2)}, u32[]{:S(2)}) collective-permute-start(f32[32,2,128]{2,0,1:T(8,128)S(1)} %slice.55), channel_id=1, source_target_pairs={{0,3},{1,0},{2,1},{3,2},{4,7},{5,4},{6,5},{7,6},{8,11},{9,8},{10,9... | collective-permute-start | bytes 98312 | tf_op jit(solution)/shard_map/ppermute | solution.py:15
  101.9 1.3 collective-permute-start.4
  103.2 1.3 collective-permute-start.5
  104.5 0.1 collective-permute-start.6
  104.5 42.7 %psum.23 = f32[32]{0:T(128)S(1)} all-reduce(f32[32]{0:T(128)S(1)} %get-tuple-element.10), channel_id=1, replica_groups=mesh['gx'=8,'col'=4] {'gx','col'}, use_global_device_ids=true, to_apply=%region_5.7 | all-reduce | flops 32 | bytes 256 | tf_op jit(solution)/shard_map/psum | solution.py:93
  147.3 0.0 copy-start.9
  147.3 0.0 collective-permute-done.4
  147.3 0.0 collective-permute-done.5
  147.3 0.0 collective-permute-done.6
  147.4 0.0 collective-permute-done.7
  147.4 0.6 gather_fusion.4
  147.9 0.0 copy-done.2
  148.0 0.7 fusion.10
  148.7 0.0 copy-done.9
  (23 shorter events, 0.2 us)
Async XLA Ops:
  0.6 1.6 %copy-start = (bf16[1,1,1024,1024]{3,2,1,0:T(8,128)(2,1)S(1)}, bf16[1,1,1024,1024]{3,2,1,0:T(8,128)(2,1)}, u32[]{:S(2)}) copy-start(bf16[1,1,1024,1024]{3,2,1,0:T(8,128)(2,1)} %param.14) | copy-start | bytes 6291460
  0.6 12.1 %copy-start.7 = (s32[1,1,8]{2,1,0:T(1,128)S(1)}, s32[1,1,8]{2,1,0:T(1,128)}, u32[]{:S(2)}) copy-start(s32[1,1,8]{2,1,0:T(1,128)} %param.19) | copy-start | bytes 100
  0.7 12.2 %copy-start.6 = (f32[8,4]{0,1:T(4,128)S(1)}, f32[8,4]{0,1:T(4,128)}, u32[]{:S(2)}) copy-start(f32[8,4]{0,1:T(4,128)} %param.18) | copy-start | bytes 388
  0.7 58.5 %copy-start.4 = (bf16[1,8,20,1,4,20]{5,4,3,2,1,0:T(4,128)(2,1)S(1)}, bf16[1,8,20,1,4,20]{5,4,3,2,1,0:T(4,128)(2,1)}, u32[]{:S(2)}) copy-start(bf16[1,8,20,1,4,20]{5,4,3,2,1,0:T(4,128)(2,1)} %param.17) | copy-start | bytes 76804
  2.2 57.1 %copy-start.8 = (f32[32]{0:T(128)S(1)}, f32[32]{0:T(128)}, u32[]{:S(2)}) copy-start(f32[32]{0:T(128)} %param.13) | copy-start | bytes 388
  2.2 57.8 %copy-start.5 = (f32[1,1,32,1024]{3,2,1,0:T(8,128)S(1)}, f32[1,1,32,1024]{3,2,1,0:T(8,128)}, u32[]{:S(2)}) copy-start(f32[1,1,32,1024]{3,2,1,0:T(8,128)} %param.11) | copy-start | bytes 393220
  3.8 56.3 %copy-start.3 = (bf16[1,1,1024,20]{2,3,1,0:T(8,128)(2,1)S(1)}, bf16[1,1,1024,20]{2,3,1,0:T(8,128)(2,1)}, u32[]{:S(2)}) copy-start(bf16[1,1,1024,20]{2,3,1,0:T(8,128)(2,1)} %param.16) | copy-start | bytes 122884
  4.5 54.8 %collective-permute-start = (bf16[32,2,128]{2,0,1:T(8,128)(2,1)S(1)}, bf16[32,2,128]{2,0,1:T(8,128)(2,1)S(1)}, u32[]{:S(2)}, u32[]{:S(2)}) collective-permute-start(bf16[32,2,128]{2,0,1:T(8,128)(2,1)S(1)} %get-tuple-element.15), channel_id=1, source_target_pairs={{0,4},{4,8},{8,12},{12,16},{16,20},{20,24},{24,28},{1,5},{5,9},{9,... | collective-permute-start | bytes 49160 | tf_op jit(solution)/shard_map/ppermute | solution.py:10
  6.9 52.5 %collective-permute-start.1 = (bf16[32,2,128]{2,0,1:T(8,128)(2,1)S(1)}, bf16[32,2,128]{2,0,1:T(8,128)(2,1)S(1)}, u32[]{:S(2)}, u32[]{:S(2)}) collective-permute-start(bf16[32,2,128]{2,0,1:T(8,128)(2,1)S(1)} %get-tuple-element.17), channel_id=1, source_target_pairs={{4,0},{8,4},{12,8},{16,12},{20,16},{24,20},{28,24},{5,1},{9,5},{13... | collective-permute-start | bytes 49160 | tf_op jit(solution)/shard_map/ppermute | solution.py:10
  8.2 51.2 %collective-permute-start.2 = (bf16[32,2,128]{2,0,1:T(8,128)(2,1)S(1)}, bf16[32,2,128]{2,0,1:T(8,128)(2,1)S(1)}, u32[]{:S(2)}, u32[]{:S(2)}) collective-permute-start(bf16[32,2,128]{2,0,1:T(8,128)(2,1)S(1)} %get-tuple-element.16), channel_id=1, source_target_pairs={{0,1},{1,2},{2,3},{3,0},{4,5},{5,6},{6,7},{7,4},{8,9},{9,10},{10,1... | collective-permute-start | bytes 49160 | tf_op jit(solution)/shard_map/ppermute | solution.py:15
  10.7 48.8 %collective-permute-start.3 = (f32[32,2,128]{2,0,1:T(8,128)S(1)}, f32[32,2,128]{2,0,1:T(8,128)S(1)}, u32[]{:S(2)}, u32[]{:S(2)}) collective-permute-start(f32[32,2,128]{2,0,1:T(8,128)S(1)} %slice.51), channel_id=1, source_target_pairs={{0,3},{1,0},{2,1},{3,2},{4,7},{5,4},{6,5},{7,6},{8,11},{9,8},{10,9... | collective-permute-start | bytes 98312 | tf_op jit(solution)/shard_map/ppermute | solution.py:15
  60.1 39.5 %copy-start.1 = (f32[32,1024]{1,0:T(8,128)}, f32[32,1024]{1,0:T(8,128)S(1)}, u32[]{:S(2)}) copy-start(f32[32,1024]{1,0:T(8,128)S(1)} %fusion.12) | copy-start | bytes 393220
  96.7 51.3 %copy-start.2 = (f32[1,1,32,1024]{3,2,1,0:T(8,128)S(1)}, f32[1,1,32,1024]{3,2,1,0:T(8,128)}, u32[]{:S(2)}) copy-start(f32[1,1,32,1024]{3,2,1,0:T(8,128)} %param.12) | copy-start | bytes 393220
  99.6 47.7 %collective-permute-start.7 = (f32[32,2,128]{2,0,1:T(8,128)S(1)}, f32[32,2,128]{2,0,1:T(8,128)S(1)}, u32[]{:S(2)}, u32[]{:S(2)}) collective-permute-start(f32[32,2,128]{2,0,1:T(8,128)S(1)} %slice.55), channel_id=1, source_target_pairs={{0,3},{1,0},{2,1},{3,2},{4,7},{5,4},{6,5},{7,6},{8,11},{9,8},{10,9... | collective-permute-start | bytes 98312 | tf_op jit(solution)/shard_map/ppermute | solution.py:15
  101.9 45.4 %collective-permute-start.4 = (bf16[32,2,128]{2,0,1:T(8,128)(2,1)S(1)}, bf16[32,2,128]{2,0,1:T(8,128)(2,1)S(1)}, u32[]{:S(2)}, u32[]{:S(2)}) collective-permute-start(bf16[32,2,128]{2,0,1:T(8,128)(2,1)S(1)} %get-tuple-element.12), channel_id=1, source_target_pairs={{0,4},{4,8},{8,12},{12,16},{16,20},{20,24},{24,28},{1,5},{5,9},{9,... | collective-permute-start | bytes 49160 | tf_op jit(solution)/shard_map/ppermute | solution.py:10
  103.2 44.1 %collective-permute-start.5 = (bf16[32,2,128]{2,0,1:T(8,128)(2,1)S(1)}, bf16[32,2,128]{2,0,1:T(8,128)(2,1)S(1)}, u32[]{:S(2)}, u32[]{:S(2)}) collective-permute-start(bf16[32,2,128]{2,0,1:T(8,128)(2,1)S(1)} %get-tuple-element.14), channel_id=1, source_target_pairs={{4,0},{8,4},{12,8},{16,12},{20,16},{24,20},{28,24},{5,1},{9,5},{13... | collective-permute-start | bytes 49160 | tf_op jit(solution)/shard_map/ppermute | solution.py:10
  104.5 42.9 %collective-permute-start.6 = (bf16[32,2,128]{2,0,1:T(8,128)(2,1)S(1)}, bf16[32,2,128]{2,0,1:T(8,128)(2,1)S(1)}, u32[]{:S(2)}, u32[]{:S(2)}) collective-permute-start(bf16[32,2,128]{2,0,1:T(8,128)(2,1)S(1)} %get-tuple-element.13), channel_id=1, source_target_pairs={{0,1},{1,2},{2,3},{3,0},{4,5},{5,6},{6,7},{7,4},{8,9},{9,10},{10,1... | collective-permute-start | bytes 49160 | tf_op jit(solution)/shard_map/ppermute | solution.py:15
  147.3 1.4 copy-start.9
where the time goes:
time: 150 us; the launch traced here: 149 us
  blocking collectives  120 us (80%)
  starting transfers between devices  13.1 us (9%)
  other arithmetic  4.83 us (3%)
  matrix products  4.17 us (3%)
  local copies, waits for them, and re-layouts  4.12 us (3%)
  between operations  2.35 us (2%)
    psum x1, blocking collectives, body(): rz_next = lax.psum(jnp.sum(scaled * local_sol, axis=1), ('gx', 'col'))  42.7 us
    psum x1, blocking collectives, body(): curvature = lax.psum(jnp.sum(dir_local * image_part, axis=1), ('gx', 'col'))  41.4 us
    psum x1, blocking collectives, body(): lax.psum(partial_all.astype(jnp.bfloat16), 'gx').astype(jnp.float32)  22.9 us
    all_gather x1, blocking collectives, body(): gathered = lax.all_gather(coarse_rhs[None], 'col', axis=0, tiled=True)  13.1 us
    ppermute x4, starting transfers between devices, passed_along_2(): lax.ppermute(shard, axis, [(i, (i + by) % count) for i in range(count)])  6.86 us
    ppermute x4, starting transfers between devices, passed_along(): lax.ppermute(value, axis, [(source, source + steps) for source in range(i...  6.22 us
  transfers between devices with their start and end apart: 8, of which 0 were waited for; matrix products, arithmetic and copies ran while one was open for 3% of the time, Pallas kernels for 0%

commit v1 on v0

v1 whole, which is shorter than its diff:
```python
import functools

import jax
import jax.numpy as jnp
from jax import lax
from jax.experimental import pallas as pl
from jax.experimental.pallas import tpu as pltpu
from jax.sharding import PartitionSpec as P

F32 = jnp.float32
BF16 = jnp.bfloat16
BLK = 128
EXACT = lax.Precision.HIGHEST
SMEM = pltpu.SMEM
VMEM = pltpu.VMEM


def params():
    return pltpu.CompilerParams(vmem_limit_bytes=16 * 1024 * 1024)


def cost(flops, nbytes):
    return pl.CostEstimate(flops=flops, bytes_accessed=nbytes, transcendentals=0)


def swap(value, axis, offset):
    count = lax.axis_size(axis)
    pairs = []
    for low in range(offset, count, 2):
        high = (low + 1) % count
        pairs += [(low, high), (high, low)]
    return lax.ppermute(value, axis, pairs)


def swap_faces(faces):
    return (
        swap(faces[0], "gx", 0),
        swap(faces[1], "gx", 1),
        swap(faces[2], "col", 0),
        swap(faces[3], "col", 1),
    )


def swapped_faces():
    slab = lax.axis_index("gx") % 2
    sector = lax.axis_index("col") % 2
    return (1 - slab, slab, 3 - sector, 2 + sector)


def swap_counts():
    slab = lax.axis_index("gx")
    inside = jnp.logical_and(slab > 0, slab < lax.axis_size("gx") - 1)
    return (None, inside, None, None)


def block_at(perm_ref, slot):
    return pl.ds(pl.multiple_of(perm_ref[slot] * BLK, BLK), BLK)


def put_faces(perm_ref, source, outs):
    for face, out in zip(swapped_faces(), outs):
        for j in range(2):
            out[:, j * BLK : (j + 1) * BLK] = source[:, block_at(perm_ref, 2 * face + j)].astype(BF16)


def add_faces(perm_ref, target, received):
    for face, counts, got in zip(swapped_faces(), swap_counts(), received):
        for j in range(2):
            part = got[:, j * BLK : (j + 1) * BLK].astype(F32)
            if counts is not None:
                part = jnp.where(counts, part, 0.0)
            at = block_at(perm_ref, 2 * face + j)
            target[:, at] = target[:, at] + part


def to_column(row):
    n = row.shape[1]
    at = lax.broadcasted_iota(jnp.int32, (n, n), 0) == lax.broadcasted_iota(jnp.int32, (n, n), 1)
    return jnp.sum(jnp.where(at, row, 0.0), axis=1, keepdims=True)


def to_row(column):
    n = column.shape[0]
    at = lax.broadcasted_iota(jnp.int32, (n, n), 0) == lax.broadcasted_iota(jnp.int32, (n, n), 1)
    return jnp.sum(jnp.where(at, column, 0.0), axis=0, keepdims=True)


def image_kernel(perm_ref, dir_ref, schur_ref, image_ref, *faces):
    image_ref[...] = jnp.dot(dir_ref[...].astype(BF16), schur_ref[...], preferred_element_type=F32)
    put_faces(perm_ref, image_ref, faces)


def early_kernel(perm_ref, conduct_ref, dir_ref, image_ref, resid_ref, basis_ref, neumann_ref,
                 weight_ref, rhs_ref, curv_ref, sol_ref):
    slab, sector = lax.axis_index("gx"), lax.axis_index("col")
    slabs, sectors = lax.axis_size("gx"), lax.axis_size("col")
    own = conduct_ref[slab, sector]
    below = jnp.where(slab > 0, conduct_ref[jnp.maximum(slab - 1, 0), sector], 0.0)
    above = jnp.where(slab < slabs - 1, conduct_ref[jnp.minimum(slab + 1, slabs - 1), sector], 0.0)
    left = conduct_ref[slab, (sector + sectors - 1) % sectors]
    right = conduct_ref[slab, (sector + 1) % sectors]
    for face, other in enumerate((below, above, left, right)):
        across = jnp.full((8, BLK), own, F32) / jnp.full((8, BLK), own + other, F32)
        for j in range(2):
            weight_ref[:, block_at(perm_ref, 2 * face + j)] = across
    scaled = (weight_ref[0:1, :] * resid_ref[...]).astype(BF16)
    rhs_ref[...] = lax.dot_general(
        basis_ref[...], scaled, (((1,), (1,)), ((), ())), preferred_element_type=F32
    )
    curv = to_row(jnp.sum(dir_ref[...] * image_ref[...], axis=1, keepdims=True))
    high = curv.astype(BF16)
    low = (curv - high.astype(F32)).astype(BF16)
    curv_ref[...] = jnp.zeros_like(curv_ref)
    n = curv.shape[1]
    curv_ref[0:1, 0:n] = high.astype(F32)
    curv_ref[0:1, n : 2 * n] = low.astype(F32)
    sol_ref[...] = jnp.dot(scaled, neumann_ref[...], preferred_element_type=F32)


def coarse_rhs_kernel(perm_ref, image_ref, r0, r1, r2, r3, weight_ref, basis_ref, rhs_ref, curv_ref,
                      assembled_ref, scaled_ref, out_ref):
    assembled_ref[...] = image_ref[...]
    add_faces(perm_ref, assembled_ref, (r0, r1, r2, r3))
    scaled = (weight_ref[0:1, :] * assembled_ref[...]).astype(BF16)
    scaled_ref[...] = scaled
    rhs_q = lax.dot_general(
        basis_ref[...], scaled, (((1,), (1,)), ((), ())), preferred_element_type=F32
    )
    rhs_r = rhs_ref[...]
    half = rhs_r.shape[0] // 2
    rows = out_ref.shape[1]
    packed = jnp.concatenate([rhs_r[:half], rhs_q[:half], rhs_r[half:], rhs_q[half:]], axis=1)
    packed = jnp.concatenate(
        [packed, curv_ref[0:1, :], jnp.zeros((rows - half - 1, BLK), F32)], axis=0
    ).astype(BF16)
    for i in range(out_ref.shape[0]):
        out_ref[i] = packed


def neumann_kernel(scaled_ref, neumann_ref, out_ref):
    out_ref[...] = jnp.dot(scaled_ref[...], neumann_ref[...], preferred_element_type=F32)


def solve_kernel(prim, perm_ref, gathered_ref, coarse_ref, rz_ref, resid_ref, assembled_ref,
                 weight_ref, basis_ref, sol_r_ref, sol_q_ref,
                 resid_out, weighted_out, rz_out, *faces):
    blocks, rows, depth = coarse_ref.shape
    total = jnp.zeros((rows, BLK), F32)
    per = gathered_ref.shape[0] // blocks
    for h in range(blocks):
        part = gathered_ref[h * per : (h + 1) * per].reshape(depth, BLK)
        total = total + jnp.dot(coarse_ref[h], part, preferred_element_type=F32)
    n = rz_ref.shape[1]
    second = (rows - 8) // 2
    curvature = total[2 * second : 2 * second + 1, 0:n] + total[2 * second : 2 * second + 1, n : 2 * n]
    step = rz_ref[...] / curvature
    sol_r = total[0:prim, 0:n] + total[second : second + prim, 2 * n : 3 * n]
    sol_q = total[0:prim, n : 2 * n] + total[second : second + prim, 3 * n : 4 * n]
    coarse_sol = (sol_r - step * sol_q).astype(BF16)
    correction = lax.dot_general(
        coarse_sol, basis_ref[...], (((0,), (0,)), ((), ())), preferred_element_type=F32
    )
    step_col = to_column(step)
    weight = weight_ref[0:1, :]
    resid_new = resid_ref[...] - step_col * assembled_ref[...]
    resid_out[...] = resid_new
    local = sol_r_ref[...] - step_col * sol_q_ref[...] + correction
    weighted = weight * local
    weighted_out[...] = weighted
    put_faces(perm_ref, weighted_out, faces)
    partial = to_row(jnp.sum(resid_new * weighted, axis=1, keepdims=True))
    partial = jnp.concatenate([partial, jnp.zeros((1, BLK - n), F32)], axis=1)
    for i in range(rz_out.shape[0]):
        rz_out[i] = partial


def direction_kernel(perm_ref, partials_ref, rz_ref, dir_ref, weighted_ref, r0, r1, r2, r3,
                     out_ref, rz_out):
    n = rz_ref.shape[1]
    rz_next = jnp.sum(partials_ref[...], axis=0)[:, 0:n]
    rz_out[...] = rz_next
    out_ref[...] = weighted_ref[...] + to_column(rz_next / rz_ref[...]) * dir_ref[...]
    add_faces(perm_ref, out_ref, (r0, r1, r2, r3))


def coarse_blocks(coarse_inv, rows):
    slabs, prim, _, sectors, _ = coarse_inv.shape
    half = prim // 2
    up = -(-prim // 8) * 8
    own = coarse_inv[:, :, 0]
    first = jnp.pad(own[..., :half], ((0, 0), (0, up - prim), (0, 0), (0, rows - half)))
    second = jnp.pad(own[..., half:], ((0, 0), (0, up - prim), (0, 0), (0, rows - half)))
    last = jnp.zeros((slabs, 8, sectors, rows), coarse_inv.dtype).at[:, 0, :, half].set(1)
    return jnp.concatenate([first, second, last], axis=1).reshape(slabs, 2 * up + 8, sectors * rows)


def body(resid, direction, rz_prev, schur, neumann, basis, coarse_inv, conduct, face_perm):
    resid, direction, schur, neumann = resid[0, 0], direction[0, 0], schur[0, 0], neumann[0, 0]
    basis_t = basis[0, 0].T
    perm = face_perm[0, 0]
    rhs, width = resid.shape
    prim = basis_t.shape[0]
    count = lax.axis_size("gx") * lax.axis_size("col")
    rows = -(-(prim // 2 + 1) // 16) * 16
    face = jax.ShapeDtypeStruct((rhs, 2 * BLK), BF16)
    full = jax.ShapeDtypeStruct((rhs, width), F32)
    rz_row = rz_prev[None, :]
    smem = pl.BlockSpec(memory_space=SMEM)
    vmem = pl.BlockSpec(memory_space=VMEM)
    flops = 2 * rhs * width * width

    coarse = lax.all_to_all(coarse_blocks(coarse_inv[0], rows), "gx", 0, 0)

    image, *faces = pl.pallas_call(
        image_kernel, out_shape=(full,) + (face,) * 4, in_specs=[smem, vmem, vmem],
        out_specs=(vmem,) * 5, compiler_params=params(), cost_estimate=cost(flops, 2 * width * width),
    )(perm, direction, schur)
    received = swap_faces(faces)
    weight, rhs_r, curv, sol_r = pl.pallas_call(
        early_kernel,
        out_shape=(
            jax.ShapeDtypeStruct((8, width), F32),
            jax.ShapeDtypeStruct((prim, rhs), F32),
            jax.ShapeDtypeStruct((8, BLK), F32),
            full,
        ),
        in_specs=[smem, smem] + [vmem] * 5, out_specs=(vmem,) * 4, compiler_params=params(),
        cost_estimate=cost(flops, 2 * width * width),
    )(perm, conduct, direction, image, resid, basis_t, neumann)
    assembled, scaled_q, packed = pl.pallas_call(
        coarse_rhs_kernel,
        out_shape=(
            full,
            jax.ShapeDtypeStruct((rhs, width), BF16),
            jax.ShapeDtypeStruct((count, rows, BLK), BF16),
        ),
        in_specs=[smem] + [vmem] * 9, out_specs=(vmem,) * 3, compiler_params=params(),
        cost_estimate=cost(2 * rhs * width * prim, 8 * rhs * width),
    )(perm, image, *received, weight, basis_t, rhs_r, curv)
    gathered = lax.all_to_all(packed, ("gx", "col"), 0, 0)
    sol_q = pl.pallas_call(
        neumann_kernel, out_shape=full, in_specs=[vmem] * 2, out_specs=vmem,
        compiler_params=params(), cost_estimate=cost(flops, 2 * width * width),
    )(scaled_q, neumann)
    resid_new, weighted, partial, *faces = pl.pallas_call(
        functools.partial(solve_kernel, prim),
        out_shape=(full, full, jax.ShapeDtypeStruct((count, 1, BLK), F32)) + (face,) * 4,
        in_specs=[smem] + [vmem] * 9, out_specs=(vmem,) * 7, compiler_params=params(),
        cost_estimate=cost(2 * rhs * width * prim, 8 * rhs * width),
    )(perm, gathered, coarse, rz_row, resid, assembled, weight, basis_t, sol_r, sol_q)
    partials = lax.all_to_all(partial, ("gx", "col"), 0, 0)
    received = swap_faces(faces)
    direction_new, rz_next = pl.pallas_call(
        direction_kernel, out_shape=(full, jax.ShapeDtypeStruct((1, rhs), F32)),
        in_specs=[smem] + [vmem] * 8, out_specs=(vmem,) * 2, compiler_params=params(),
        cost_estimate=cost(2 * rhs * width, 8 * rhs * width),
    )(perm, partials, rz_row, direction, weighted, *received)
    return (resid_new[None, None], direction_new[None, None], rz_next[0])


def solution(mesh):
    placed = (
        P("gx", "col", None, None),
        P("gx", "col", None, None),
        P(),
        P("gx", "col", None, None),
        P("gx", "col", None, None),
        P("gx", "col", None, None),
        P("col", None, None, "gx", None, None),
        P(),
        P("gx", "col", None),
    )
    return jax.shard_map(
        body,
        mesh=mesh,
        in_specs=placed,
        out_specs=(P("gx", "col", None, None), P("gx", "col", None, None), P()),
        check_vma=False,
    )
```

time: 150 us -> 55.4 us (0.37)
  blocking collectives: 120 us -> 0 us
  waiting for transfers between devices: 0.02 us -> 12.7 us
  starting transfers between devices: 13.1 us -> 24.4 us
  Pallas kernels: 0 us -> 7.23 us
  matrix products: 4.17 us -> 0 us
  local copies, waits for them, and re-layouts: 4.12 us -> 6.21 us
  other arithmetic: 4.83 us -> 2.97 us
    psum x3 -> x0, blocking collectives: 107 us -> none  [the longest x1 42.7 us: body(): rz_next = lax.psum(jnp.sum(scaled * local_sol, axis=1), ('gx', 'col'))]
    all_gather x1 -> x0, blocking collectives: 13.1 us -> none  [body(): gathered = lax.all_gather(coarse_rhs[None], 'col', axis=0, tiled=True)]
    all_to_all x0 -> x3, starting transfers between devices: none -> 10.6 us  [the longest x1 5.17 us: body(): coarse = lax.all_to_all(coarse_blocks(coarse_inv[0], rows), 'gx', 0, 0)]
    all_to_all x0 -> x3, waiting for transfers between devices: none -> 7.79 us  [the longest x1 7.79 us: body(): gathered = lax.all_to_all(packed, ('gx', 'col'), 0, 0)]
    pallas_call x0 -> x6, Pallas kernels: none -> 7.23 us  [the longest x1 1.77 us: body(): pl.pallas_call(functools.partial(solve_kernel, prim), out_shape=(full, fu...]
    ppermute x8, waiting for transfers between devices: 0.02 us -> 4.92 us  [swap(): return lax.ppermute(value, axis, pairs)]
    dot_general x5 -> x0, matrix products: 4.17 us -> none  [the longest x1 2.09 us: body(): jnp.dot(scaled_b, neumann[0, 0], preferred_element_type=jnp.float32)]
    unnamed x21 -> x20, local copies, waits for them, and re-layouts: 0.16 us -> 3.87 us
  transfers between devices with their start and end apart: 8 -> 11, of which waited for: 0 -> 3; matrix products, arithmetic and copies ran while one was open for 3% -> 0% of each run, Pallas kernels for 0% -> 7%
where the time goes in v1:
time: 55.4 us; the launch traced here: 55 us
  starting transfers between devices  24.4 us (44%)
  waiting for transfers between devices  12.7 us (23%)
  Pallas kernels  7.23 us (13%)
  local copies, waits for them, and re-layouts  6.21 us (11%)
  other arithmetic  2.97 us (5%)
  between operations  1.45 us (3%)
    ppermute x8, starting transfers between devices, swap(): return lax.ppermute(value, axis, pairs)  13.9 us
    all_to_all x1, waiting for transfers between devices, body(): gathered = lax.all_to_all(packed, ('gx', 'col'), 0, 0)  7.79 us
    all_to_all x1, starting transfers between devices, body(): coarse = lax.all_to_all(coarse_blocks(coarse_inv[0], rows), 'gx', 0, 0)  5.17 us
    ppermute x8, waiting for transfers between devices, swap(): return lax.ppermute(value, axis, pairs)  4.92 us
    unnamed x20, local copies, waits for them, and re-layouts  3.87 us
    all_to_all x1, starting transfers between devices, body(): gathered = lax.all_to_all(packed, ('gx', 'col'), 0, 0)  2.84 us
    another operation x2, other arithmetic  2.81 us
    all_to_all x1, starting transfers between devices, body(): partials = lax.all_to_all(partial, ('gx', 'col'), 0, 0)  2.54 us
  transfers between devices with their start and end apart: 11, of which 3 were waited for; matrix products, arithmetic and copies ran while one was open for 0% of the time, Pallas kernels for 7%

profile of v1, /device:TPU:0, one launch (start us, length us, event | category | flops | bytes accessed | tf_op | source)
XLA Modules:
  0.0 55.0 jit_solution(15414266172523892984)
XLA Ops:
  0.6 0.0 copy-start.5
  0.6 0.0 copy-start.2
  0.7 0.6 %fusion.6 = (s32[1]{0:T(128)}, s32[1]{0:T(128)}) fusion(s32[2]{0:T(128)S(1)} %iota_multiply_fusion), kind=kLoop, calls=%fused_computation.11 | loop fusion | bytes 16 | tf_op jit(solution)/shard_map/slice.28
  1.2 0.0 copy-start.7
  1.2 0.0 copy-start.3
  1.2 0.0 copy-start.4
  1.2 1.3 %copy.17 = bf16[1,8,20,1,4,20]{2,5,4,1,3,0:T(8,128)(2,1)S(1)} copy(bf16[1,8,20,1,4,20]{5,4,3,2,1,0:T(4,128)(2,1)} %param.17) | data formatting | bytes 51200 | tf_op args[6]
  2.5 0.0 copy-start
  2.6 2.8 %and_reduce_fusion = pred[]{:T(512)} fusion(s32[4]{0:T(128)} %constant.30.clone.1, s32[1]{0:T(128)} %get-tuple-element.60, s32[1]{0:T(128)} %constant.28.clone.1, s32[1]{0:T(128)} %get-tuple-element.59), kind=kLoop, calls=%fused_computation.8 | loop fusion | flops 27 | bytes 29 | tf_op jit(solution)/shard_map/reduce.1
  6.1 1.6 %scatter.4 = bf16[8,8,4,16]{1,3,2,0:T(8,128)(2,1)S(1)} dynamic-update-slice(bf16[8,8,4,16]{1,3,2,0:T(8,128)(2,1)S(1)} %broadcast_in_dim.13, bf16[8,1,4,1]{1,3,2,0:T(2,128)(2,1)S(1)} %broadcast.39, s32[]{:T(128)} %constant.27.clone.1, s32[]{:T(128)} %bitcast.8, s32[]{:T(128)} %constant.27.clone.1, s32[]{:T(128)} %bitcast.9) | dynamic-update-slice | bytes 132 | tf_op jit(solution)/shard_map/scatter | solution.py:193
  7.6 0.2 fusion.4
  7.8 0.1 copy.18
  7.9 0.8 %reshape.53 = bf16[8,2,1792]{2,1,0:T(2,128)(2,1)} reshape(bf16[8,56,64]{2,1,0:T(8,128)(2,1)S(1)} %copy.18) | data formatting | bytes 114688
  8.7 5.2 %all-to-all-start.1 = ((bf16[8,2,1792]{2,1,0:T(2,128)(2,1)}), bf16[8,2,1792]{2,1,0:T(2,128)(2,1)S(1)}, u32[]{:S(2)}, u32[]{:S(2)}) async-start(bf16[8,2,1792]{2,1,0:T(2,128)(2,1)} %reshape.53), calls=%async_computation.1 | async-start | bytes 114688 | tf_op jit(solution)/shard_map/all_to_all | solution.py:212
  13.9 0.0 copy-done.5
  13.9 0.0 copy-done.2
  13.9 0.0 copy-start.1
  13.9 1.6 %copy-done.1 = bf16[1,1,1024,1024]{3,2,1,0:T(8,128)(2,1)S(1)} copy-done((bf16[1,1,1024,1024]{3,2,1,0:T(8,128)(2,1)S(1)}, bf16[1,1,1024,1024]{3,2,1,0:T(8,128)(2,1)}, u32[]{:S(2)}) %copy-start.1) | copy-done | bytes 2097176
  15.5 1.0 %shard_map.112 = (f32[32,1024]{1,0:T(8,128)S(1)}, bf16[32,256]{1,0:T(8,128)(2,1)S(1)}, bf16[32,256]{1,0:T(8,128)(2,1)S(1)}, bf16[32,256]{1,0:T(8,128)(2,1)S(1)}, bf16[32,256]{1,0:T(8,128)(2,1)S(1)}) custom-call(s32[8]{0:T(128)S(1)} %bitcast.27, f32[32,1024]{1,0:T(8,128)S(1)} %bitcast.19, bf16[1024,1024]{1,0:T(8,128)(2,1)S(1)} %bitcast.18), custom_call_target="tpu_custom_call" | custom-call | flops 67108864 | bytes 2097152 | tf_op jit(solution)/shard_map/pallas_call | solution.py:214
  16.5 0.6 %collective-permute-start = (bf16[32,256]{1,0:T(8,128)(2,1)S(1)}, bf16[32,256]{1,0:T(8,128)(2,1)S(1)}, u32[]{:S(2)}, u32[]{:S(2)}) collective-permute-start(bf16[32,256]{1,0:T(8,128)(2,1)S(1)} %get-tuple-element.37), channel_id=1, source_target_pairs={{0,4},{4,0},{8,12},{12,8},{16,20},{20,16},{24,28},{28,24},{1,5},{5... | collective-permute-start | bytes 49160 | tf_op jit(solution)/shard_map/ppermute | solution.py:32
  17.1 2.5 %collective-permute-start.1 = (bf16[32,256]{1,0:T(8,128)(2,1)S(1)}, bf16[32,256]{1,0:T(8,128)(2,1)S(1)}, u32[]{:S(2)}, u32[]{:S(2)}) collective-permute-start(bf16[32,256]{1,0:T(8,128)(2,1)S(1)} %get-tuple-element.38), channel_id=1, source_target_pairs={{4,8},{8,4},{12,16},{16,12},{20,24},{24,20},{28,0},{0,28},{5,9},{9... | collective-permute-start | bytes 49160 | tf_op jit(solution)/shard_map/ppermute | solution.py:32
  19.6 1.6 %collective-permute-start.2 = (bf16[32,256]{1,0:T(8,128)(2,1)S(1)}, bf16[32,256]{1,0:T(8,128)(2,1)S(1)}, u32[]{:S(2)}, u32[]{:S(2)}) collective-permute-start(bf16[32,256]{1,0:T(8,128)(2,1)S(1)} %get-tuple-element.39), channel_id=1, source_target_pairs={{0,1},{1,0},{2,3},{3,2},{4,5},{5,4},{6,7},{7,6},{8,9},{9,8},{10,11... | collective-permute-start | bytes 49160 | tf_op jit(solution)/shard_map/ppermute | solution.py:32
  21.2 2.5 %collective-permute-start.3 = (bf16[32,256]{1,0:T(8,128)(2,1)S(1)}, bf16[32,256]{1,0:T(8,128)(2,1)S(1)}, u32[]{:S(2)}, u32[]{:S(2)}) collective-permute-start(bf16[32,256]{1,0:T(8,128)(2,1)S(1)} %get-tuple-element.40), channel_id=1, source_target_pairs={{1,2},{2,1},{3,0},{0,3},{5,6},{6,5},{7,4},{4,7},{9,10},{10,9},{11,... | collective-permute-start | bytes 49160 | tf_op jit(solution)/shard_map/ppermute | solution.py:32
  23.7 0.0 copy-done.7
  23.7 0.1 copy.16.conduct_ref
  23.7 0.0 copy-done.3
  23.8 0.0 copy-done.4
  23.8 0.0 copy-done
  23.8 1.1 %shard_map.113 = (f32[8,1024]{1,0:T(8,128)S(1)}, f32[20,32]{1,0:T(8,128)S(1)}, f32[8,128]{1,0:T(8,128)S(1)}, f32[32,1024]{1,0:T(8,128)S(1)}) custom-call(s32[8]{0:T(128)S(1)} %bitcast.28, f32[8,4]{1,0:T(8,128)S(1)} %copy.16.conduct_ref, f32[32,1024]{1,0:T(8,128)S(1)} %bitcast.20, f32[32,1024]{1,0:T(8,128)S(1)} %get-tuple-element.36.image_ref, ...), custom_call_target="tpu_custom_call" | custom-call | flops 67108864 | bytes 2097152 | tf_op jit(solution)/shard_map/pallas_call | solution.py:219
  24.9 0.0 copy-start.6
  24.9 0.0 collective-permute-done.r0
  24.9 0.0 collective-permute-done.1.r1
  24.9 0.0 collective-permute-done.2.r2
  24.9 1.8 %collective-permute-done.3.r3 = bf16[32,256]{1,0:T(8,128)(2,1)S(1)} collective-permute-done((bf16[32,256]{1,0:T(8,128)(2,1)S(1)}, bf16[32,256]{1,0:T(8,128)(2,1)S(1)}, u32[]{:S(2)}, u32[]{:S(2)}) %collective-permute-start.3) | collective-permute-done | bytes 16416 | tf_op jit(solution)/shard_map/ppermute | solution.py:32
  26.7 1.5 %shard_map.114 = (f32[32,1024]{1,0:T(8,128)S(1)}, bf16[32,1024]{1,0:T(8,128)(2,1)S(1)}, bf16[32,16,128]{2,1,0:T(8,128)(2,1)}) custom-call(s32[8]{0:T(128)S(1)} %bitcast.29, f32[32,1024]{1,0:T(8,128)S(1)} %get-tuple-element.36.image_ref, bf16[32,256]{1,0:T(8,128)(2,1)S(1)} %collective-permute-done.r0, bf16[32,256]{1,0:T(8,128)(2,1)S(1)} %collective-permute-done.1.r1, ...), custom_call_target="tpu_custom_call" | custom-call | flops 1310720 | bytes 262144 | tf_op jit(solution)/shard_map/pallas_call | solution.py:230
  28.2 0.0 all-to-all-done.1
  28.2 2.8 %all-to-all-start = ((bf16[32,16,128]{2,1,0:T(8,128)(2,1)}), bf16[32,16,128]{2,1,0:T(8,128)(2,1)S(1)}, u32[]{:S(2)}, u32[]{:S(2)}) async-start(bf16[32,16,128]{2,1,0:T(8,128)(2,1)} %get-tuple-element.44), calls=%async_computation | async-start | bytes 262144 | tf_op jit(solution)/shard_map/all_to_all | solution.py:240
  31.1 0.5 shard_map.115.sol_q_ref
  31.5 0.2 reshape.54.coarse_ref
  31.7 7.8 %all-to-all-done.gathered_ref = bf16[32,16,128]{2,1,0:T(8,128)(2,1)S(1)} async-done(((bf16[32,16,128]{2,1,0:T(8,128)(2,1)}), bf16[32,16,128]{2,1,0:T(8,128)(2,1)S(1)}, u32[]{:S(2)}, u32[]{:S(2)}) %all-to-all-start) | async-done | bytes 131104 | tf_op jit(solution)/shard_map/all_to_all | solution.py:240
  39.5 0.0 copy-done.6
  39.5 1.8 %shard_map.116 = (f32[32,1024]{1,0:T(8,128)}, f32[32,1024]{1,0:T(8,128)S(1)}, f32[32,1,128]{2,1,0:T(1,128)}, bf16[32,256]{1,0:T(8,128)(2,1)S(1)}, bf16[32,256]{1...) custom-call(s32[8]{0:T(128)S(1)} %bitcast.30, ...), custom_call_target="tpu_custom_call" | custom-call | flops 1310720 | bytes 262144 | tf_op jit(solution)/shard_map/pallas_call | solution.py:245
  41.2 2.5 %all-to-all-start.2 = ((f32[32,1,128]{2,1,0:T(1,128)}), f32[32,1,128]{2,1,0:T(1,128)S(1)}, u32[]{:S(2)}, u32[]{:S(2)}) async-start(f32[32,1,128]{2,1,0:T(1,128)} %get-tuple-element.49), calls=%async_computation.2 | async-start | bytes 32768 | tf_op jit(solution)/shard_map/all_to_all | solution.py:251
  43.8 0.2 collective-permute-start.4
  44.0 2.6 %collective-permute-start.5 = (bf16[32,256]{1,0:T(8,128)(2,1)S(1)}, bf16[32,256]{1,0:T(8,128)(2,1)S(1)}, u32[]{:S(2)}, u32[]{:S(2)}) collective-permute-start(bf16[32,256]{1,0:T(8,128)(2,1)S(1)} %get-tuple-element.52), channel_id=1, source_target_pairs={{4,8},{8,4},{12,16},{16,12},{20,24},{24,20},{28,0},{0,28},{5,9},{9... | collective-permute-start | bytes 49160 | tf_op jit(solution)/shard_map/ppermute | solution.py:32
  46.5 1.5 %collective-permute-start.6 = (bf16[32,256]{1,0:T(8,128)(2,1)S(1)}, bf16[32,256]{1,0:T(8,128)(2,1)S(1)}, u32[]{:S(2)}, u32[]{:S(2)}) collective-permute-start(bf16[32,256]{1,0:T(8,128)(2,1)S(1)} %get-tuple-element.53), channel_id=1, source_target_pairs={{0,1},{1,0},{2,3},{3,2},{4,5},{5,4},{6,7},{7,6},{8,9},{9,8},{10,11... | collective-permute-start | bytes 49160 | tf_op jit(solution)/shard_map/ppermute | solution.py:32
  48.1 2.4 %collective-permute-start.7 = (bf16[32,256]{1,0:T(8,128)(2,1)S(1)}, bf16[32,256]{1,0:T(8,128)(2,1)S(1)}, u32[]{:S(2)}, u32[]{:S(2)}) collective-permute-start(bf16[32,256]{1,0:T(8,128)(2,1)S(1)} %get-tuple-element.54), channel_id=1, source_target_pairs={{1,2},{2,1},{3,0},{0,3},{5,6},{6,5},{7,4},{4,7},{9,10},{10,9},{11,... | collective-permute-start | bytes 49160 | tf_op jit(solution)/shard_map/ppermute | solution.py:32
  50.5 0.0 collective-permute-done.4.r0
  50.5 0.0 collective-permute-done.5.r1
  50.5 0.0 collective-permute-done.6.r2
  50.5 3.1 %collective-permute-done.7.r3 = bf16[32,256]{1,0:T(8,128)(2,1)S(1)} collective-permute-done((bf16[32,256]{1,0:T(8,128)(2,1)S(1)}, bf16[32,256]{1,0:T(8,128)(2,1)S(1)}, u32[]{:S(2)}, u32[]{:S(2)}) %collective-permute-start.7) | collective-permute-done | bytes 16416 | tf_op jit(solution)/shard_map/ppermute | solution.py:32
  53.6 0.0 all-to-all-done.2.partials_ref
  53.6 1.4 %shard_map.117 = (f32[32,1024]{1,0:T(8,128)}, f32[1,32]{1,0:T(1,128)}) custom-call(s32[8]{0:T(128)S(1)} %bitcast.31, f32[32,1,128]{2,1,0:T(1,128)S(1)} %all-to-all-done.2.partials_ref, f32[1,32]{1,0:T(1,128)S(1)} %bitcast.33, f32[32,1024]{1,0:T(8,128)S(1)} %bitcast.21, f32[32,1024]{1,0:T(8,128)S(1)} %get-tuple-element.50.weighted_ref, ...), custom_call_target="tpu_custom_call" | custom-call | flops 65536 | bytes 262144 | tf_op jit(solution)/shard_map/pallas_call | solution.py:253
  (4 shorter events, 0.1 us)
Async XLA Ops:
  0.6 13.2 %copy-start.5 = (s32[1,1,8]{2,1,0:T(1,128)S(1)}, s32[1,1,8]{2,1,0:T(1,128)}, u32[]{:S(2)}) copy-start(s32[1,1,8]{2,1,0:T(1,128)} %param.19) | copy-start | bytes 100
  0.6 13.2 %copy-start.2 = (f32[1,1,32,1024]{3,2,1,0:T(8,128)S(1)}, f32[1,1,32,1024]{3,2,1,0:T(8,128)}, u32[]{:S(2)}) copy-start(f32[1,1,32,1024]{3,2,1,0:T(8,128)} %param.12) | copy-start | bytes 393220
  1.2 22.4 %copy-start.7 = (f32[8,4]{0,1:T(4,128)S(1)}, f32[8,4]{0,1:T(4,128)}, u32[]{:S(2)}) copy-start(f32[8,4]{0,1:T(4,128)} %param.18) | copy-start | bytes 388
  1.2 22.5 %copy-start.3 = (f32[1,1,32,1024]{3,2,1,0:T(8,128)S(1)}, f32[1,1,32,1024]{3,2,1,0:T(8,128)}, u32[]{:S(2)}) copy-start(f32[1,1,32,1024]{3,2,1,0:T(8,128)} %param.11) | copy-start | bytes 393220
  1.2 22.5 %copy-start.4 = (bf16[1,1,1024,20]{2,3,1,0:T(8,128)(2,1)S(1)}, bf16[1,1,1024,20]{2,3,1,0:T(8,128)(2,1)}, u32[]{:S(2)}) copy-start(bf16[1,1,1024,20]{2,3,1,0:T(8,128)(2,1)} %param.16) | copy-start | bytes 122884
  2.5 21.2 %copy-start = (bf16[1,1,1024,1024]{3,2,1,0:T(8,128)(2,1)S(1)}, bf16[1,1,1024,1024]{3,2,1,0:T(8,128)(2,1)}, u32[]{:S(2)}) copy-start(bf16[1,1,1024,1024]{3,2,1,0:T(8,128)(2,1)} %param.15) | copy-start | bytes 6291460
  8.7 19.5 %all-to-all-start.1 = ((bf16[8,2,1792]{2,1,0:T(2,128)(2,1)}), bf16[8,2,1792]{2,1,0:T(2,128)(2,1)S(1)}, u32[]{:S(2)}, u32[]{:S(2)}) async-start(bf16[8,2,1792]{2,1,0:T(2,128)(2,1)} %reshape.53), calls=%async_computation.1 | async-start | bytes 114688 | tf_op jit(solution)/shard_map/all_to_all | solution.py:212
  13.9 1.6 %copy-start.1 = (bf16[1,1,1024,1024]{3,2,1,0:T(8,128)(2,1)S(1)}, bf16[1,1,1024,1024]{3,2,1,0:T(8,128)(2,1)}, u32[]{:S(2)}) copy-start(bf16[1,1,1024,1024]{3,2,1,0:T(8,128)(2,1)} %param.14) | copy-start | bytes 6291460
  16.5 8.4 %collective-permute-start = (bf16[32,256]{1,0:T(8,128)(2,1)S(1)}, bf16[32,256]{1,0:T(8,128)(2,1)S(1)}, u32[]{:S(2)}, u32[]{:S(2)}) collective-permute-start(bf16[32,256]{1,0:T(8,128)(2,1)S(1)} %get-tuple-element.37), channel_id=1, source_target_pairs={{0,4},{4,0},{8,12},{12,8},{16,20},{20,16},{24,28},{28,24},{1,5},{5... | collective-permute-start | bytes 49160 | tf_op jit(solution)/shard_map/ppermute | solution.py:32
  17.1 7.8 %collective-permute-start.1 = (bf16[32,256]{1,0:T(8,128)(2,1)S(1)}, bf16[32,256]{1,0:T(8,128)(2,1)S(1)}, u32[]{:S(2)}, u32[]{:S(2)}) collective-permute-start(bf16[32,256]{1,0:T(8,128)(2,1)S(1)} %get-tuple-element.38), channel_id=1, source_target_pairs={{4,8},{8,4},{12,16},{16,12},{20,24},{24,20},{28,0},{0,28},{5,9},{9... | collective-permute-start | bytes 49160 | tf_op jit(solution)/shard_map/ppermute | solution.py:32
  19.6 5.3 %collective-permute-start.2 = (bf16[32,256]{1,0:T(8,128)(2,1)S(1)}, bf16[32,256]{1,0:T(8,128)(2,1)S(1)}, u32[]{:S(2)}, u32[]{:S(2)}) collective-permute-start(bf16[32,256]{1,0:T(8,128)(2,1)S(1)} %get-tuple-element.39), channel_id=1, source_target_pairs={{0,1},{1,0},{2,3},{3,2},{4,5},{5,4},{6,7},{7,6},{8,9},{9,8},{10,11... | collective-permute-start | bytes 49160 | tf_op jit(solution)/shard_map/ppermute | solution.py:32
  21.2 5.5 %collective-permute-start.3 = (bf16[32,256]{1,0:T(8,128)(2,1)S(1)}, bf16[32,256]{1,0:T(8,128)(2,1)S(1)}, u32[]{:S(2)}, u32[]{:S(2)}) collective-permute-start(bf16[32,256]{1,0:T(8,128)(2,1)S(1)} %get-tuple-element.40), channel_id=1, source_target_pairs={{1,2},{2,1},{3,0},{0,3},{5,6},{6,5},{7,4},{4,7},{9,10},{10,9},{11,... | collective-permute-start | bytes 49160 | tf_op jit(solution)/shard_map/ppermute | solution.py:32
  24.9 14.6 %copy-start.6 = (f32[32]{0:T(128)S(1)}, f32[32]{0:T(128)}, u32[]{:S(2)}) copy-start(f32[32]{0:T(128)} %param.13) | copy-start | bytes 388
  28.2 11.2 %all-to-all-start = ((bf16[32,16,128]{2,1,0:T(8,128)(2,1)}), bf16[32,16,128]{2,1,0:T(8,128)(2,1)S(1)}, u32[]{:S(2)}, u32[]{:S(2)}) async-start(bf16[32,16,128]{2,1,0:T(8,128)(2,1)} %get-tuple-element.44), calls=%async_computation | async-start | bytes 262144 | tf_op jit(solution)/shard_map/all_to_all | solution.py:240
  41.2 12.4 %all-to-all-start.2 = ((f32[32,1,128]{2,1,0:T(1,128)}), f32[32,1,128]{2,1,0:T(1,128)S(1)}, u32[]{:S(2)}, u32[]{:S(2)}) async-start(f32[32,1,128]{2,1,0:T(1,128)} %get-tuple-element.49), calls=%async_computation.2 | async-start | bytes 32768 | tf_op jit(solution)/shard_map/all_to_all | solution.py:251
  43.8 6.7 %collective-permute-start.4 = (bf16[32,256]{1,0:T(8,128)(2,1)S(1)}, bf16[32,256]{1,0:T(8,128)(2,1)S(1)}, u32[]{:S(2)}, u32[]{:S(2)}) collective-permute-start(bf16[32,256]{1,0:T(8,128)(2,1)S(1)} %get-tuple-element.51), channel_id=1, source_target_pairs={{0,4},{4,0},{8,12},{12,8},{16,20},{20,16},{24,28},{28,24},{1,5},{5... | collective-permute-start | bytes 49160 | tf_op jit(solution)/shard_map/ppermute | solution.py:32
  44.0 6.5 %collective-permute-start.5 = (bf16[32,256]{1,0:T(8,128)(2,1)S(1)}, bf16[32,256]{1,0:T(8,128)(2,1)S(1)}, u32[]{:S(2)}, u32[]{:S(2)}) collective-permute-start(bf16[32,256]{1,0:T(8,128)(2,1)S(1)} %get-tuple-element.52), channel_id=1, source_target_pairs={{4,8},{8,4},{12,16},{16,12},{20,24},{24,20},{28,0},{0,28},{5,9},{9... | collective-permute-start | bytes 49160 | tf_op jit(solution)/shard_map/ppermute | solution.py:32
  46.5 4.0 %collective-permute-start.6 = (bf16[32,256]{1,0:T(8,128)(2,1)S(1)}, bf16[32,256]{1,0:T(8,128)(2,1)S(1)}, u32[]{:S(2)}, u32[]{:S(2)}) collective-permute-start(bf16[32,256]{1,0:T(8,128)(2,1)S(1)} %get-tuple-element.53), channel_id=1, source_target_pairs={{0,1},{1,0},{2,3},{3,2},{4,5},{5,4},{6,7},{7,6},{8,9},{9,8},{10,11... | collective-permute-start | bytes 49160 | tf_op jit(solution)/shard_map/ppermute | solution.py:32
  48.1 5.5 %collective-permute-start.7 = (bf16[32,256]{1,0:T(8,128)(2,1)S(1)}, bf16[32,256]{1,0:T(8,128)(2,1)S(1)}, u32[]{:S(2)}, u32[]{:S(2)}) collective-permute-start(bf16[32,256]{1,0:T(8,128)(2,1)S(1)} %get-tuple-element.54), channel_id=1, source_target_pairs={{1,2},{2,1},{3,0},{0,3},{5,6},{6,5},{7,4},{4,7},{9,10},{10,9},{11,... | collective-permute-start | bytes 49160 | tf_op jit(solution)/shard_map/ppermute | solution.py:32

commit v2 on v1

v2 whole, which is shorter than its diff:
```python
import functools

import jax
import jax.numpy as jnp
from jax import lax
from jax.experimental import pallas as pl
from jax.experimental.pallas import tpu as pltpu
from jax.sharding import PartitionSpec as P

F32 = jnp.float32
BF16 = jnp.bfloat16
BLK = 128
EXACT = lax.Precision.HIGHEST
VMEM = pltpu.VMEM


def params(limit=16 * 1024 * 1024):
    return pltpu.CompilerParams(vmem_limit_bytes=limit)


def cost(flops, nbytes):
    return pl.CostEstimate(flops=flops, bytes_accessed=nbytes, transcendentals=0)


def swap(value, axis, offset):
    count = lax.axis_size(axis)
    pairs = []
    for low in range(offset, count, 2):
        high = (low + 1) % count
        pairs += [(low, high), (high, low)]
    return lax.ppermute(value, axis, pairs)


def swap_faces(faces):
    return (
        swap(faces[0], "col", 1),
        swap(faces[1], "col", 0),
        swap(faces[2], "gx", 1),
        swap(faces[3], "gx", 0),
    )


def swap_counts():
    slab = lax.axis_index("gx")
    inside = jnp.logical_and(slab > 0, slab < lax.axis_size("gx") - 1)
    return (None, None, inside, None)


def slot_place(perm_ref, slot):
    return jnp.broadcast_to(perm_ref[0:1, slot : slot + 1], (1, BLK))


def swapped_places(perm_ref):
    slab = lax.axis_index("gx") % 2
    sector = lax.axis_index("col") % 2
    places = []
    for parity, even, odd in ((sector, 2, 3), (sector, 3, 2), (slab, 0, 1), (slab, 1, 0)):
        for j in range(2):
            at_even, at_odd = (slot_place(perm_ref, 2 * face + j) for face in (even, odd))
            places.append(jnp.where(parity == 0, at_even, at_odd))
    return places


def put_faces(perm_ref, source, outs):
    blocks = [source[:, b * BLK : (b + 1) * BLK] for b in range(source.shape[1] // BLK)]
    for i, place in enumerate(swapped_places(perm_ref)):
        chosen = blocks[0]
        for b in range(1, len(blocks)):
            chosen = jnp.where(place == b, blocks[b], chosen)
        j = i % 2
        outs[i // 2][:, j * BLK : (j + 1) * BLK] = chosen.astype(BF16)


def received_blocks(perm_ref, received, blocks):
    places = swapped_places(perm_ref)
    parts = []
    for i in range(len(places)):
        j = i % 2
        part = received[i // 2][:, j * BLK : (j + 1) * BLK].astype(F32)
        counts = swap_counts()[i // 2]
        parts.append(part if counts is None else jnp.where(counts, part, 0.0))
    for b in range(blocks):
        chosen = parts[0]
        for place, part in zip(places[1:], parts[1:]):
            chosen = jnp.where(place == b, part, chosen)
        yield slice(b * BLK, (b + 1) * BLK), chosen


def to_column(row):
    n = row.shape[1]
    at = lax.broadcasted_iota(jnp.int32, (n, n), 0) == lax.broadcasted_iota(jnp.int32, (n, n), 1)
    return jnp.sum(jnp.where(at, row, 0.0), axis=1, keepdims=True)


def to_row(column):
    n = column.shape[0]
    at = lax.broadcasted_iota(jnp.int32, (n, n), 0) == lax.broadcasted_iota(jnp.int32, (n, n), 1)
    return jnp.sum(jnp.where(at, column, 0.0), axis=0, keepdims=True)


CHUNKS = 4


def other_block(i, k):
    mine = (lax.axis_index("gx") >> k) % 2
    return ((i >> k) << (k + 1)) + (i & ((1 << k) - 1)) + ((1 - mine) << k)


def swap_bit(value, k):
    count = lax.axis_size("gx")
    return lax.ppermute(value, "gx", [(i, i ^ (1 << k)) for i in range(count)])


def image_kernel(perm_hbm, dir_hbm, schur_hbm, resid_hbm, basis_hbm, coarse_hbm,
                 image_ref, f0, f1, f2, f3, send_ref, dir_ref, resid_ref, basis_ref, coarse_ref, perm_ref,
                 schur_ref, sems):
    rows = schur_ref.shape[0] // CHUNKS
    parts = [pl.ds(i * rows, rows) for i in range(CHUNKS)]
    pairs = [(dir_hbm, dir_ref), (perm_hbm, perm_ref)]
    pairs += [(schur_hbm.at[part], schur_ref.at[part]) for part in parts]
    pairs += [(coarse_hbm.at[other_block(i, 0)], send_ref.at[i]) for i in range(send_ref.shape[0])]
    pairs += [(resid_hbm, resid_ref), (basis_hbm, basis_ref), (coarse_hbm, coarse_ref)]
    copies = [pltpu.make_async_copy(source, target, sems.at[i]) for i, (source, target) in enumerate(pairs)]
    for copy in copies:
        copy.start()
    copies[0].wait()
    total = None
    for i, part in enumerate(parts):
        copies[2 + i].wait()
        term = jnp.dot(dir_ref[:, part].astype(BF16), schur_ref[part], preferred_element_type=F32)
        total = term if total is None else total + term
    image_ref[...] = total
    copies[1].wait()
    put_faces(perm_ref, total, (f0, f1, f2, f3))
    for copy in copies[2 + CHUNKS :]:
        copy.wait()


def merge_kernel(k, last, blocks_ref, got_ref, out_ref, *send_ref):
    out_ref[...] = blocks_ref[...]
    for i in range(got_ref.shape[0]):
        out_ref[other_block(i, k)] = got_ref[i]
    if not last:
        for i in range(got_ref.shape[0]):
            send_ref[0][i] = out_ref[other_block(i, k + 1)]


def spread_kernel(matrix_ref, blocks_ref):
    slabs, rows, _ = blocks_ref.shape
    prim = matrix_ref.shape[0] // slabs
    half = prim // 2
    sectors = matrix_ref.shape[1] // prim
    width = blocks_ref.shape[2] // 2
    depth = width // sectors
    source = lax.broadcasted_iota(jnp.int32, (sectors * prim, 2 * width), 0)
    place = lax.broadcasted_iota(jnp.int32, (sectors * prim, 2 * width), 1)
    later = place // width
    within = place % width
    sector, at = within // depth, within % depth
    chosen = jnp.logical_and(at < half, source == sector * prim + later * half + at)
    spread = jnp.dot(matrix_ref[...], jnp.where(chosen, 1.0, 0.0).astype(BF16), preferred_element_type=F32)
    empty = jnp.zeros((rows - prim, 2 * width), F32)
    for g in range(slabs):
        own = jnp.concatenate([spread[g * prim : (g + 1) * prim], empty], axis=0)
        blocks_ref[g] = own.astype(BF16)


def conduct_at(row, sector):
    lane = lax.broadcasted_iota(jnp.int32, row.shape, 1)
    return jnp.sum(jnp.where(lane == sector, row, 0.0), axis=1, keepdims=True)


def early_kernel(perm_ref, conduct_ref, dir_ref, image_ref, resid_ref, basis_ref,
                 weight_ref, rhs_ref, curv_ref, scaled_ref):
    slab, sector = lax.axis_index("gx"), lax.axis_index("col")
    slabs, sectors = lax.axis_size("gx"), lax.axis_size("col")
    row = conduct_ref[pl.ds(slab, 1), :]
    own = conduct_at(row, sector)
    below = conduct_at(conduct_ref[pl.ds(jnp.maximum(slab - 1, 0), 1), :], sector)
    above = conduct_at(conduct_ref[pl.ds(jnp.minimum(slab + 1, slabs - 1), 1), :], sector)
    below = jnp.where(slab > 0, below, 0.0)
    above = jnp.where(slab < slabs - 1, above, 0.0)
    left = conduct_at(row, (sector + sectors - 1) % sectors)
    right = conduct_at(row, (sector + 1) % sectors)
    across = [jnp.broadcast_to(own / (own + other), (1, BLK)) for other in (below, above, left, right)]
    places = [slot_place(perm_ref, slot) for slot in range(8)]
    for b in range(weight_ref.shape[1] // BLK):
        weight = across[0]
        for slot in range(2, 8):
            weight = jnp.where(places[slot] == b, across[slot // 2], weight)
        weight_ref[:, b * BLK : (b + 1) * BLK] = jnp.broadcast_to(weight, (8, BLK))
    scaled = (weight_ref[0:1, :] * resid_ref[...]).astype(BF16)
    scaled_ref[...] = scaled
    rhs_ref[...] = lax.dot_general(
        basis_ref[...], scaled, (((1,), (1,)), ((), ())), preferred_element_type=F32
    )
    curv = to_row(jnp.sum(dir_ref[...] * image_ref[...], axis=1, keepdims=True))
    high = curv.astype(BF16).astype(F32)
    n = curv.shape[1]
    curv_ref[...] = jnp.zeros_like(curv_ref)
    curv_ref[0:1, 0:n] = high
    curv_ref[0:1, n : 2 * n] = curv - high


def coarse_rhs_kernel(perm_ref, image_ref, r0, r1, r2, r3, weight_ref, basis_ref, rhs_ref, curv_ref,
                      assembled_ref, scaled_ref, out_ref):
    for at, part in received_blocks(perm_ref, (r0, r1, r2, r3), image_ref.shape[1] // BLK):
        assembled_ref[:, at] = image_ref[:, at] + part
    scaled = (weight_ref[0:1, :] * assembled_ref[...]).astype(BF16)
    scaled_ref[...] = scaled
    rhs_q = lax.dot_general(
        basis_ref[...], scaled, (((1,), (1,)), ((), ())), preferred_element_type=F32
    )
    rhs_r = rhs_ref[...]
    half = rhs_r.shape[0] // 2
    rows = out_ref.shape[1]
    packed = jnp.concatenate([rhs_r[:half], rhs_q[:half], rhs_r[half:], rhs_q[half:]], axis=1)
    packed = jnp.concatenate(
        [packed, curv_ref[0:1, :], jnp.zeros((rows - half - 1, BLK), F32)], axis=0
    ).astype(BF16)
    for i in range(out_ref.shape[0]):
        out_ref[i] = packed


def neumann_kernel(scaled_r_ref, scaled_q_ref, neumann_ref, sol_r_ref, sol_q_ref):
    sol_r_ref[...] = jnp.dot(scaled_r_ref[...], neumann_ref[...], preferred_element_type=F32)
    sol_q_ref[...] = jnp.dot(scaled_q_ref[...], neumann_ref[...], preferred_element_type=F32)


def solve_kernel(perm_ref, gathered_ref, blocks_ref, rz_ref, resid_ref, assembled_ref, weight_ref,
                 basis_ref, sol_r_ref, sol_q_ref, step_out, weighted_out, rz_out, *faces):
    n = rz_ref.shape[1]
    prim = basis_ref.shape[0]
    slabs, _, width = blocks_ref.shape
    width = width // 2
    sectors = gathered_ref.shape[0] // slabs
    depth = gathered_ref.shape[1]
    total = None
    for h in range(slabs):
        part = gathered_ref[h * sectors : (h + 1) * sectors].reshape(width, 4 * n)
        halves = jnp.concatenate([part[:, : 2 * n], part[:, 2 * n :]], axis=0)
        term = jnp.dot(blocks_ref[h], halves, preferred_element_type=F32)
        total = term if total is None else total + term
    everything = gathered_ref[...].reshape(slabs * width, 4 * n)
    at = lax.broadcasted_iota(jnp.int32, (16, slabs * width), 1) % depth
    picks = jnp.where(at == prim // 2, 1.0, 0.0).astype(BF16)
    sums = jnp.dot(picks, everything, preferred_element_type=F32)
    step = rz_ref[...] / (sums[0:1, 0:n] + sums[0:1, n : 2 * n])
    coarse_sol = (total[0:prim, 0:n] - step * total[0:prim, n : 2 * n]).astype(BF16)
    correction = lax.dot_general(
        coarse_sol, basis_ref[...], (((0,), (0,)), ((), ())), preferred_element_type=F32
    )
    step_col = to_column(step)
    step_out[...] = jnp.broadcast_to(step_col, step_out.shape)
    resid_new = resid_ref[...] - step_col * assembled_ref[...]
    local = sol_r_ref[...] - step_col * sol_q_ref[...] + correction
    weighted = weight_ref[0:1, :] * local
    weighted_out[...] = weighted
    put_faces(perm_ref, weighted, faces)
    partial = to_row(jnp.sum(resid_new * weighted, axis=1, keepdims=True))
    partial = jnp.concatenate([partial, jnp.zeros((1, BLK - n), F32)], axis=1)
    for i in range(rz_out.shape[0]):
        rz_out[i] = partial


def resid_kernel(step_ref, resid_ref, assembled_ref, out_ref):
    out_ref[...] = resid_ref[...] - step_ref[:, 0:1] * assembled_ref[...]


def direction_kernel(perm_ref, partials_ref, rz_ref, dir_ref, weighted_ref, r0, r1, r2, r3,
                     out_ref, rz_out):
    n = rz_ref.shape[1]
    rz_next = jnp.sum(partials_ref[...], axis=0)[:, 0:n]
    rz_out[...] = rz_next
    factor = to_column(rz_next / rz_ref[...])
    for at, part in received_blocks(perm_ref, (r0, r1, r2, r3), dir_ref.shape[1] // BLK):
        out_ref[:, at] = weighted_ref[:, at] + factor * dir_ref[:, at] + part


def body(resid, direction, rz_prev, schur, neumann, basis, coarse_inv, conduct, face_perm):
    resid, direction, schur, neumann = resid[0, 0], direction[0, 0], schur[0, 0], neumann[0, 0]
    basis_t = basis[0, 0].T
    perm = face_perm[0]
    rhs, width = resid.shape
    prim = basis_t.shape[0]
    slabs, sectors = lax.axis_size("gx"), lax.axis_size("col")
    rows = -(-(prim // 2 + 1) // 16) * 16
    block_rows = -(-prim // 16) * 16
    rounds = slabs.bit_length() - 1
    face = jax.ShapeDtypeStruct((rhs, 2 * BLK), BF16)
    full = jax.ShapeDtypeStruct((rhs, width), F32)
    rz_row = rz_prev[None, :]
    vmem = pl.BlockSpec(memory_space=VMEM)
    hbm = pl.BlockSpec(memory_space=pltpu.HBM)
    flops = 2 * rhs * width * width
    coarse = coarse_inv[0, :, :, 0]
    coarse_type = jax.ShapeDtypeStruct(coarse.shape, BF16)
    send_type = jax.ShapeDtypeStruct((slabs // 2,) + coarse.shape[1:], BF16)
    blocks_type = jax.ShapeDtypeStruct((slabs, block_rows, 2 * sectors * rows), BF16)

    fetched = [pltpu.with_memory_space_constraint(x, pltpu.HBM) for x in (perm, direction, schur, resid, basis_t, coarse)]
    image, f0, f1, f2, f3, send, direction, resid, basis_t, coarse = pl.pallas_call(
        image_kernel,
        out_shape=(full,) + (face,) * 4
        + (send_type, full, full, jax.ShapeDtypeStruct((prim, width), BF16), coarse_type),
        in_specs=[hbm] * 6, out_specs=(vmem,) * 10,
        scratch_shapes=[
            pltpu.VMEM(perm.shape, jnp.int32),
            pltpu.VMEM((width, width), BF16),
            pltpu.SemaphoreType.DMA((CHUNKS + 5 + slabs // 2,)),
        ],
        compiler_params=params(), cost_estimate=cost(flops, 2 * width * width),
    )(*fetched)
    received = swap_faces((f0, f1, f2, f3))
    weight, rhs_r, curv, scaled_r = pl.pallas_call(
        early_kernel,
        out_shape=(
            jax.ShapeDtypeStruct((8, width), F32),
            jax.ShapeDtypeStruct((prim, rhs), F32),
            jax.ShapeDtypeStruct((8, BLK), F32),
            jax.ShapeDtypeStruct((rhs, width), BF16),
        ),
        in_specs=[vmem] * 6, out_specs=(vmem,) * 4, compiler_params=params(),
        cost_estimate=cost(2 * rhs * width * prim, 8 * rhs * width),
    )(perm, conduct, direction, image, resid, basis_t)
    for k in range(rounds):
        got = swap_bit(send, k)
        last = k + 1 == rounds
        coarse, *send = pl.pallas_call(
            functools.partial(merge_kernel, k, last),
            out_shape=(coarse_type,) if last else (coarse_type, send_type),
            in_specs=[vmem] * 2, out_specs=(vmem,) if last else (vmem,) * 2,
            compiler_params=params(), cost_estimate=cost(1 << 10, 1 << 16),
        )(coarse, got)
        send = send[0] if send else None
    blocks = pl.pallas_call(
        spread_kernel, out_shape=blocks_type, in_specs=[vmem], out_specs=vmem,
        compiler_params=params(), cost_estimate=cost(1 << 20, 1 << 16),
    )(coarse.reshape(slabs * prim, sectors * prim))
    assembled, scaled_q, packed = pl.pallas_call(
        coarse_rhs_kernel,
        out_shape=(
            full,
            jax.ShapeDtypeStruct((rhs, width), BF16),
            jax.ShapeDtypeStruct((slabs * sectors, rows, BLK), BF16),
        ),
        in_specs=[vmem] + [vmem] * 9, out_specs=(vmem,) * 3, compiler_params=params(),
        cost_estimate=cost(2 * rhs * width * prim, 8 * rhs * width),
    )(perm, image, *received, weight, basis_t, rhs_r, curv)
    gathered = lax.all_to_all(packed, ("gx", "col"), 0, 0)
    sol_r, sol_q = pl.pallas_call(
        neumann_kernel, out_shape=(full, full), in_specs=[vmem] * 3, out_specs=(vmem,) * 2,
        compiler_params=params(), cost_estimate=cost(1000 * flops, 2 * width * width),
    )(scaled_r, scaled_q, neumann)
    step, weighted, partial, *faces = pl.pallas_call(
        solve_kernel,
        out_shape=(
            jax.ShapeDtypeStruct((rhs, BLK), F32),
            full,
            jax.ShapeDtypeStruct((slabs * sectors, 1, BLK), F32),
        )
        + (face,) * 4,
        in_specs=[vmem] + [vmem] * 9, out_specs=(vmem,) * 7, compiler_params=params(),
        cost_estimate=cost(2 * rhs * width * prim, 8 * rhs * width),
    )(perm, gathered, blocks, rz_row, resid, assembled, weight, basis_t, sol_r, sol_q)
    partials = lax.all_to_all(partial, ("gx", "col"), 0, 0)
    received = swap_faces(faces)
    resid_new = pl.pallas_call(
        resid_kernel, out_shape=full, in_specs=[vmem] * 3, out_specs=vmem,
        compiler_params=params(), cost_estimate=cost(2 * rhs * width, 12 * rhs * width),
    )(step, resid, assembled)
    direction_new, rz_next = pl.pallas_call(
        direction_kernel, out_shape=(full, jax.ShapeDtypeStruct((1, rhs), F32)),
        in_specs=[vmem] + [vmem] * 8, out_specs=(vmem,) * 2, compiler_params=params(),
        cost_estimate=cost(2 * rhs * width, 8 * rhs * width),
    )(perm, partials, rz_row, direction, weighted, *received)
    return (resid_new[None, None], direction_new[None, None], rz_next[0])


def solution(mesh):
    placed = (
        P("gx", "col", None, None),
        P("gx", "col", None, None),
        P(),
        P("gx", "col", None, None),
        P("gx", "col", None, None),
        P("gx", "col", None, None),
        P("col", None, None, "gx", None, None),
        P(),
        P("gx", "col", None),
    )
    return jax.shard_map(
        body,
        mesh=mesh,
        in_specs=placed,
        out_specs=(P("gx", "col", None, None), P("gx", "col", None, None), P()),
        check_vma=False,
    )
```

time: 55.4 us -> 38.4 us (0.69)
  local copies, waits for them, and re-layouts: 6.21 us -> 0.23 us
  waiting for transfers between devices: 12.7 us -> 7.17 us
  other arithmetic: 2.97 us -> 0 us
  starting transfers between devices: 24.4 us -> 22.4 us
  between operations: 1.45 us -> 0.74 us
    all_to_all x1, waiting for transfers between devices: 7.79 us -> 2.45 us  [body(): gathered = lax.all_to_all(packed, ('gx', 'col'), 0, 0)]
    all_to_all x1 -> x0, starting transfers between devices: 5.17 us -> none  [body(): coarse = lax.all_to_all(coarse_blocks(coarse_inv[0], rows), 'gx', 0, 0)]
    unnamed x20 -> x9, local copies, waits for them, and re-layouts: 3.87 us -> 0.1 us
    ppermute x0 -> x3, starting transfers between devices: none -> 3.29 us  [swap_bit(): return lax.ppermute(value, 'gx', [(i, i ^ 1 << k) for i in range(count)])]
    ppermute x8, waiting for transfers between devices: 4.92 us -> 1.95 us  [swap(): return lax.ppermute(value, axis, pairs)]
    another operation x2 -> x0, other arithmetic: 2.81 us -> none
    ppermute x0 -> x3, waiting for transfers between devices: none -> 2.76 us  [swap_bit(): return lax.ppermute(value, 'gx', [(i, i ^ 1 << k) for i in range(count)])]
    pallas_call x3 -> x8, Pallas kernels: 3.26 us -> 5.5 us  [the longest x1 2.19 us: body(): pl.pallas_call(image_kernel, out_shape=(full,) + (face,) * 4 + (send_type...]
  transfers between devices with their start and end apart: 11 -> 13, of which waited for: 3 -> 6; matrix products, arithmetic and copies ran while one was open for 0% -> 1% of each run, Pallas kernels for 7% -> 9%
where the time goes in v2:
time: 38.4 us; the launch traced here: 38.2 us
  starting transfers between devices  22.4 us (58%)
  Pallas kernels  7.59 us (20%)
  waiting for transfers between devices  7.17 us (19%)
  between operations  0.74 us (2%)
    ppermute x8, starting transfers between devices, swap(): return lax.ppermute(value, axis, pairs)  12.5 us
    all_to_all x1, starting transfers between devices, body(): gathered = lax.all_to_all(packed, ('gx', 'col'), 0, 0)  3.76 us
    ppermute x3, starting transfers between devices, swap_bit(): return lax.ppermute(value, 'gx', [(i, i ^ 1 << k) for i in range(count)])  3.29 us
    all_to_all x1, starting transfers between devices, body(): partials = lax.all_to_all(partial, ('gx', 'col'), 0, 0)  2.9 us
    ppermute x3, waiting for transfers between devices, swap_bit(): return lax.ppermute(value, 'gx', [(i, i ^ 1 << k) for i in range(count)])  2.76 us
    all_to_all x1, waiting for transfers between devices, body(): gathered = lax.all_to_all(packed, ('gx', 'col'), 0, 0)  2.45 us
    pallas_call x1, Pallas kernels, body(): pl.pallas_call(image_kernel, out_shape=(full,) + (face,) * 4 + (send_type...  2.19 us
    ppermute x8, waiting for transfers between devices, swap(): return lax.ppermute(value, axis, pairs)  1.95 us
  transfers between devices with their start and end apart: 13, of which 6 were waited for; matrix products, arithmetic and copies ran while one was open for 1% of the time, Pallas kernels for 9%

profile of v2, /device:TPU:0, one launch (start us, length us, event | category | flops | bytes accessed | tf_op | source)
XLA Modules:
  0.0 38.2 jit_solution(12228635180489665922)
XLA Ops:
  0.6 0.0 copy-start
  0.6 0.0 copy-start.3
  0.7 0.0 copy-start.2
  0.7 2.2 %shard_map.112 = (f32[32,1024]{1,0:T(8,128)S(1)}, bf16[32,256]{1,0:T(8,128)(2,1)S(1)}, bf16[32,256]{1,0:T(8,128)(2,1)S(1)}, bf16[32,256]{1,0:T(8,128)(2,1)S(1)},...) custom-call(s32[1,8]{1,0:T(1,128)} %bitcast.13, ...), custom_call_target="tpu_custom_call" | custom-call | flops 67108864 | bytes 2097152 | tf_op jit(solution)/shard_map/pallas_call | solution.py:302
  2.9 0.5 %collective-permute-start.4 = (bf16[4,20,4,20]{3,2,1,0:T(4,128)(2,1)S(1)}, bf16[4,20,4,20]{3,2,1,0:T(4,128)(2,1)S(1)}, u32[]{:S(2)}, u32[]{:S(2)}) collective-permute-start(bf16[4,20,4,20]{3,2,1,0:T(4,128)(2,1)S(1)} %get-tuple-element.48), channel_id=1, source_target_pairs={{0,4},{4,0},{8,12},{12,8},{16,20},{20,16},{24,28},{28,24},{1,5},{5... | collective-permute-start | bytes 38408 | tf_op jit(solution)/shard_map/ppermute | solution.py:111
  3.4 4.7 %collective-permute-start = (bf16[32,256]{1,0:T(8,128)(2,1)S(1)}, bf16[32,256]{1,0:T(8,128)(2,1)S(1)}, u32[]{:S(2)}, u32[]{:S(2)}) collective-permute-start(bf16[32,256]{1,0:T(8,128)(2,1)S(1)} %get-tuple-element.36), channel_id=1, source_target_pairs={{1,2},{2,1},{3,0},{0,3},{5,6},{6,5},{7,4},{4,7},{9,10},{10,9},{11,... | collective-permute-start | bytes 49160 | tf_op jit(solution)/shard_map/ppermute | solution.py:31
  8.1 0.0 collective-permute-start.1
  8.1 2.2 %collective-permute-start.2 = (bf16[32,256]{1,0:T(8,128)(2,1)S(1)}, bf16[32,256]{1,0:T(8,128)(2,1)S(1)}, u32[]{:S(2)}, u32[]{:S(2)}) collective-permute-start(bf16[32,256]{1,0:T(8,128)(2,1)S(1)} %get-tuple-element.38), channel_id=1, source_target_pairs={{4,8},{8,4},{12,16},{16,12},{20,24},{24,20},{28,0},{0,28},{5,9},{9... | collective-permute-start | bytes 49160 | tf_op jit(solution)/shard_map/ppermute | solution.py:31
  10.3 0.0 collective-permute-start.3
  10.3 0.0 collective-permute-done.4.got_ref
  10.3 0.1 shard_map.115
  10.4 0.9 %collective-permute-start.5 = (bf16[4,20,4,20]{3,2,1,0:T(4,128)(2,1)S(1)}, bf16[4,20,4,20]{3,2,1,0:T(4,128)(2,1)S(1)}, u32[]{:S(2)}, u32[]{:S(2)}) collective-permute-start(bf16[4,20,4,20]{3,2,1,0:T(4,128)(2,1)S(1)} %get-tuple-element.50), channel_id=1, source_target_pairs={{0,8},{4,12},{8,0},{12,4},{16,24},{20,28},{24,16},{28,20},{1,9},{5... | collective-permute-start | bytes 38408 | tf_op jit(solution)/shard_map/ppermute | solution.py:111
  11.4 0.0 copy-done.3
  11.4 0.1 copy.12.conduct_ref
  11.4 0.0 copy-done
  11.4 0.3 shard_map.113
  11.7 0.0 collective-permute-done.r0
  11.7 0.1 collective-permute-done.1.r1
  11.8 0.3 collective-permute-done.2.r2
  12.1 0.0 collective-permute-done.3.r3
  12.1 1.0 %shard_map.114 = (f32[32,1024]{1,0:T(8,128)S(1)}, bf16[32,1024]{1,0:T(8,128)(2,1)S(1)}, bf16[32,16,128]{2,1,0:T(8,128)(2,1)}) custom-call(s32[1,8]{1,0:T(1,128)S(1)} %bitcast.15, f32[32,1024]{1,0:T(8,128)S(1)} %get-tuple-element.35.image_ref, bf16[32,256]{1,0:T(8,128)(2,1)S(1)} %collective-permute-done.r0, bf16[32,256]{1,0:T(8,128)(2,1)S(1)} %collective-permute-done.1.r1, ...), custom_call_target="tpu_custom_call" | custom-call | flops 1310720 | bytes 262144 | tf_op jit(solution)/shard_map/pallas_call | solution.py:340
  13.1 3.8 %all-to-all-start = ((bf16[32,16,128]{2,1,0:T(8,128)(2,1)}), bf16[32,16,128]{2,1,0:T(8,128)(2,1)S(1)}, u32[]{:S(2)}, u32[]{:S(2)}) async-start(bf16[32,16,128]{2,1,0:T(8,128)(2,1)} %get-tuple-element.46), calls=%async_computation | async-start | bytes 262144 | tf_op jit(solution)/shard_map/all_to_all | solution.py:350
  16.9 0.0 collective-permute-done.5.got_ref
  16.9 0.1 shard_map.116
  17.0 1.8 %collective-permute-start.6 = (bf16[4,20,4,20]{3,2,1,0:T(4,128)(2,1)S(1)}, bf16[4,20,4,20]{3,2,1,0:T(4,128)(2,1)S(1)}, u32[]{:S(2)}, u32[]{:S(2)}) collective-permute-start(bf16[4,20,4,20]{3,2,1,0:T(4,128)(2,1)S(1)} %get-tuple-element.52), channel_id=1, source_target_pairs={{0,16},{4,20},{8,24},{12,28},{16,0},{20,4},{24,8},{28,12},{1,17},{... | collective-permute-start | bytes 38408 | tf_op jit(solution)/shard_map/ppermute | solution.py:111
  18.9 0.0 copy-done.2
  18.9 0.0 copy-start.1
  18.9 0.8 %shard_map.119 = (f32[32,1024]{1,0:T(8,128)S(1)}, f32[32,1024]{1,0:T(8,128)S(1)}) custom-call(bf16[32,1024]{1,0:T(8,128)(2,1)S(1)} %get-tuple-element.54.scaled_r_ref, bf16[32,1024]{1,0:T(8,128)(2,1)S(1)} %get-tuple-element.55.scaled_q_ref, bf16[1024,1024]{1,0:T(8,128)(2,1)S(1)} %bitcast.20), custom_call_target="tpu_custom_call" | custom-call | flops 67108864000 | bytes 2097152 | tf_op jit(solution)/shard_map/pallas_call | solution.py:351
  19.7 2.8 %collective-permute-done.6.got_ref = bf16[4,20,4,20]{3,2,1,0:T(4,128)(2,1)S(1)} collective-permute-done((bf16[4,20,4,20]{3,2,1,0:T(4,128)(2,1)S(1)}, bf16[4,20,4,20]{3,2,1,0:T(4,128)(2,1)S(1)}, u32[]{:S(2)}, u32[]{:S(2)}) %collective-permute-start.6) | collective-permute-done | bytes 12832 | tf_op jit(solution)/shard_map/ppermute | solution.py:111
  22.4 0.1 shard_map.117
  22.5 0.1 reshape.9.matrix_ref
  22.7 0.1 shard_map.118.blocks_ref
  22.8 2.5 %all-to-all-done.gathered_ref = bf16[32,16,128]{2,1,0:T(8,128)(2,1)S(1)} async-done(((bf16[32,16,128]{2,1,0:T(8,128)(2,1)}), bf16[32,16,128]{2,1,0:T(8,128)(2,1)S(1)}, u32[]{:S(2)}, u32[]{:S(2)}) %all-to-all-start) | async-done | bytes 131104 | tf_op jit(solution)/shard_map/all_to_all | solution.py:350
  25.3 0.0 copy-done.1
  25.3 1.3 %shard_map.120 = (f32[32,128]{1,0:T(8,128)S(1)}, f32[32,1024]{1,0:T(8,128)S(1)}, f32[32,1,128]{2,1,0:T(1,128)}, bf16[32,256]{1,0:T(8,128)(2,1)S(1)}, bf16[32,256...) custom-call(s32[1,8]{1,0:T(1,128)S(1)} %bitcast.16, ...), custom_call_target="tpu_custom_call" | custom-call | flops 1310720 | bytes 262144 | tf_op jit(solution)/shard_map/pallas_call | solution.py:355
  26.6 2.9 %all-to-all-start.1 = ((f32[32,1,128]{2,1,0:T(1,128)}), f32[32,1,128]{2,1,0:T(1,128)S(1)}, u32[]{:S(2)}, u32[]{:S(2)}) async-start(f32[32,1,128]{2,1,0:T(1,128)} %get-tuple-element.59), calls=%async_computation.1 | async-start | bytes 32768 | tf_op jit(solution)/shard_map/all_to_all | solution.py:366
  29.5 3.7 %collective-permute-start.7 = (bf16[32,256]{1,0:T(8,128)(2,1)S(1)}, bf16[32,256]{1,0:T(8,128)(2,1)S(1)}, u32[]{:S(2)}, u32[]{:S(2)}) collective-permute-start(bf16[32,256]{1,0:T(8,128)(2,1)S(1)} %get-tuple-element.61), channel_id=1, source_target_pairs={{1,2},{2,1},{3,0},{0,3},{5,6},{6,5},{7,4},{4,7},{9,10},{10,9},{11,... | collective-permute-start | bytes 49160 | tf_op jit(solution)/shard_map/ppermute | solution.py:31
  33.2 0.0 collective-permute-start.8
  33.2 1.9 %collective-permute-start.9 = (bf16[32,256]{1,0:T(8,128)(2,1)S(1)}, bf16[32,256]{1,0:T(8,128)(2,1)S(1)}, u32[]{:S(2)}, u32[]{:S(2)}) collective-permute-start(bf16[32,256]{1,0:T(8,128)(2,1)S(1)} %get-tuple-element.63), channel_id=1, source_target_pairs={{4,8},{8,4},{12,16},{16,12},{20,24},{24,20},{28,0},{0,28},{5,9},{9... | collective-permute-start | bytes 49160 | tf_op jit(solution)/shard_map/ppermute | solution.py:31
  35.0 0.0 collective-permute-start.10
  35.1 0.7 %shard_map.121 = f32[32,1024]{1,0:T(8,128)} custom-call(f32[32,128]{1,0:T(8,128)S(1)} %get-tuple-element.58.step_ref, f32[32,1024]{1,0:T(8,128)S(1)} %get-tuple-element.41.resid_ref, f32[32,1024]{1,0:T(8,128)S(1)} %get-tuple-element.53.assembled_ref), custom_call_target="tpu_custom_call" | custom-call | flops 65536 | bytes 393216 | tf_op jit(solution)/shard_map/pallas_call | solution.py:368
  35.8 0.0 collective-permute-done.7.r0
  35.8 1.1 %collective-permute-done.8.r1 = bf16[32,256]{1,0:T(8,128)(2,1)S(1)} collective-permute-done((bf16[32,256]{1,0:T(8,128)(2,1)S(1)}, bf16[32,256]{1,0:T(8,128)(2,1)S(1)}, u32[]{:S(2)}, u32[]{:S(2)}) %collective-permute-start.8) | collective-permute-done | bytes 16416 | tf_op jit(solution)/shard_map/ppermute | solution.py:31
  36.9 0.4 %collective-permute-done.9.r2 = bf16[32,256]{1,0:T(8,128)(2,1)S(1)} collective-permute-done((bf16[32,256]{1,0:T(8,128)(2,1)S(1)}, bf16[32,256]{1,0:T(8,128)(2,1)S(1)}, u32[]{:S(2)}, u32[]{:S(2)}) %collective-permute-start.9) | collective-permute-done | bytes 16416 | tf_op jit(solution)/shard_map/ppermute | solution.py:31
  37.3 0.0 collective-permute-done.10.r3
  37.3 0.0 all-to-all-done.1.partials_ref
  37.3 0.8 %shard_map.122 = (f32[32,1024]{1,0:T(8,128)}, f32[1,32]{1,0:T(1,128)}) custom-call(s32[1,8]{1,0:T(1,128)S(1)} %bitcast.17, f32[32,1,128]{2,1,0:T(1,128)S(1)} %all-to-all-done.1.partials_ref, f32[1,32]{1,0:T(1,128)S(1)} %bitcast.19, f32[32,1024]{1,0:T(8,128)S(1)} %get-tuple-element.40.dir_ref, f32[32,1024]{1,0:T(8,128)S(1)} %get-tuple-element.60.weighted_ref, ...), custom_call_target="tpu_custom_call" | custom-call | flops 65536 | bytes 262144 | tf_op jit(solution)/shard_map/pallas_call | solution.py:372
Async XLA Ops:
  0.6 10.8 %copy-start = (s32[1,1,8]{2,1,0:T(1,128)S(1)}, s32[1,1,8]{2,1,0:T(1,128)}, u32[]{:S(2)}) copy-start(s32[1,1,8]{2,1,0:T(1,128)} %param.17) | copy-start | bytes 100
  0.6 10.7 %copy-start.3 = (f32[8,4]{0,1:T(4,128)S(1)}, f32[8,4]{0,1:T(4,128)}, u32[]{:S(2)}) copy-start(f32[8,4]{0,1:T(4,128)} %param.16) | copy-start | bytes 388
  0.7 18.2 %copy-start.2 = (bf16[1,1,1024,1024]{3,2,1,0:T(8,128)(2,1)S(1)}, bf16[1,1,1024,1024]{3,2,1,0:T(8,128)(2,1)}, u32[]{:S(2)}) copy-start(bf16[1,1,1024,1024]{3,2,1,0:T(8,128)(2,1)} %param.13) | copy-start | bytes 6291460
  2.9 7.4 %collective-permute-start.4 = (bf16[4,20,4,20]{3,2,1,0:T(4,128)(2,1)S(1)}, bf16[4,20,4,20]{3,2,1,0:T(4,128)(2,1)S(1)}, u32[]{:S(2)}, u32[]{:S(2)}) collective-permute-start(bf16[4,20,4,20]{3,2,1,0:T(4,128)(2,1)S(1)} %get-tuple-element.48), channel_id=1, source_target_pairs={{0,4},{4,0},{8,12},{12,8},{16,20},{20,16},{24,28},{28,24},{1,5},{5... | collective-permute-start | bytes 38408 | tf_op jit(solution)/shard_map/ppermute | solution.py:111
  3.4 8.3 %collective-permute-start = (bf16[32,256]{1,0:T(8,128)(2,1)S(1)}, bf16[32,256]{1,0:T(8,128)(2,1)S(1)}, u32[]{:S(2)}, u32[]{:S(2)}) collective-permute-start(bf16[32,256]{1,0:T(8,128)(2,1)S(1)} %get-tuple-element.36), channel_id=1, source_target_pairs={{1,2},{2,1},{3,0},{0,3},{5,6},{6,5},{7,4},{4,7},{9,10},{10,9},{11,... | collective-permute-start | bytes 49160 | tf_op jit(solution)/shard_map/ppermute | solution.py:31
  8.1 3.7 %collective-permute-start.1 = (bf16[32,256]{1,0:T(8,128)(2,1)S(1)}, bf16[32,256]{1,0:T(8,128)(2,1)S(1)}, u32[]{:S(2)}, u32[]{:S(2)}) collective-permute-start(bf16[32,256]{1,0:T(8,128)(2,1)S(1)} %get-tuple-element.37), channel_id=1, source_target_pairs={{0,1},{1,0},{2,3},{3,2},{4,5},{5,4},{6,7},{7,6},{8,9},{9,8},{10,11... | collective-permute-start | bytes 49160 | tf_op jit(solution)/shard_map/ppermute | solution.py:31
  8.1 4.1 %collective-permute-start.2 = (bf16[32,256]{1,0:T(8,128)(2,1)S(1)}, bf16[32,256]{1,0:T(8,128)(2,1)S(1)}, u32[]{:S(2)}, u32[]{:S(2)}) collective-permute-start(bf16[32,256]{1,0:T(8,128)(2,1)S(1)} %get-tuple-element.38), channel_id=1, source_target_pairs={{4,8},{8,4},{12,16},{16,12},{20,24},{24,20},{28,0},{0,28},{5,9},{9... | collective-permute-start | bytes 49160 | tf_op jit(solution)/shard_map/ppermute | solution.py:31
  10.3 1.8 %collective-permute-start.3 = (bf16[32,256]{1,0:T(8,128)(2,1)S(1)}, bf16[32,256]{1,0:T(8,128)(2,1)S(1)}, u32[]{:S(2)}, u32[]{:S(2)}) collective-permute-start(bf16[32,256]{1,0:T(8,128)(2,1)S(1)} %get-tuple-element.39), channel_id=1, source_target_pairs={{0,4},{4,0},{8,12},{12,8},{16,20},{20,16},{24,28},{28,24},{1,5},{5... | collective-permute-start | bytes 49160 | tf_op jit(solution)/shard_map/ppermute | solution.py:31
  10.4 6.5 %collective-permute-start.5 = (bf16[4,20,4,20]{3,2,1,0:T(4,128)(2,1)S(1)}, bf16[4,20,4,20]{3,2,1,0:T(4,128)(2,1)S(1)}, u32[]{:S(2)}, u32[]{:S(2)}) collective-permute-start(bf16[4,20,4,20]{3,2,1,0:T(4,128)(2,1)S(1)} %get-tuple-element.50), channel_id=1, source_target_pairs={{0,8},{4,12},{8,0},{12,4},{16,24},{20,28},{24,16},{28,20},{1,9},{5... | collective-permute-start | bytes 38408 | tf_op jit(solution)/shard_map/ppermute | solution.py:111
  13.1 12.2 %all-to-all-start = ((bf16[32,16,128]{2,1,0:T(8,128)(2,1)}), bf16[32,16,128]{2,1,0:T(8,128)(2,1)S(1)}, u32[]{:S(2)}, u32[]{:S(2)}) async-start(bf16[32,16,128]{2,1,0:T(8,128)(2,1)} %get-tuple-element.46), calls=%async_computation | async-start | bytes 262144 | tf_op jit(solution)/shard_map/all_to_all | solution.py:350
  17.0 5.4 %collective-permute-start.6 = (bf16[4,20,4,20]{3,2,1,0:T(4,128)(2,1)S(1)}, bf16[4,20,4,20]{3,2,1,0:T(4,128)(2,1)S(1)}, u32[]{:S(2)}, u32[]{:S(2)}) collective-permute-start(bf16[4,20,4,20]{3,2,1,0:T(4,128)(2,1)S(1)} %get-tuple-element.52), channel_id=1, source_target_pairs={{0,16},{4,20},{8,24},{12,28},{16,0},{20,4},{24,8},{28,12},{1,17},{... | collective-permute-start | bytes 38408 | tf_op jit(solution)/shard_map/ppermute | solution.py:111
  18.9 6.4 %copy-start.1 = (f32[32]{0:T(128)S(1)}, f32[32]{0:T(128)}, u32[]{:S(2)}) copy-start(f32[32]{0:T(128)} %param.11) | copy-start | bytes 388
  26.6 10.8 %all-to-all-start.1 = ((f32[32,1,128]{2,1,0:T(1,128)}), f32[32,1,128]{2,1,0:T(1,128)S(1)}, u32[]{:S(2)}, u32[]{:S(2)}) async-start(f32[32,1,128]{2,1,0:T(1,128)} %get-tuple-element.59), calls=%async_computation.1 | async-start | bytes 32768 | tf_op jit(solution)/shard_map/all_to_all | solution.py:366
  29.5 6.3 %collective-permute-start.7 = (bf16[32,256]{1,0:T(8,128)(2,1)S(1)}, bf16[32,256]{1,0:T(8,128)(2,1)S(1)}, u32[]{:S(2)}, u32[]{:S(2)}) collective-permute-start(bf16[32,256]{1,0:T(8,128)(2,1)S(1)} %get-tuple-element.61), channel_id=1, source_target_pairs={{1,2},{2,1},{3,0},{0,3},{5,6},{6,5},{7,4},{4,7},{9,10},{10,9},{11,... | collective-permute-start | bytes 49160 | tf_op jit(solution)/shard_map/ppermute | solution.py:31
  33.2 3.7 %collective-permute-start.8 = (bf16[32,256]{1,0:T(8,128)(2,1)S(1)}, bf16[32,256]{1,0:T(8,128)(2,1)S(1)}, u32[]{:S(2)}, u32[]{:S(2)}) collective-permute-start(bf16[32,256]{1,0:T(8,128)(2,1)S(1)} %get-tuple-element.62), channel_id=1, source_target_pairs={{0,1},{1,0},{2,3},{3,2},{4,5},{5,4},{6,7},{7,6},{8,9},{9,8},{10,11... | collective-permute-start | bytes 49160 | tf_op jit(solution)/shard_map/ppermute | solution.py:31
  33.2 4.2 %collective-permute-start.9 = (bf16[32,256]{1,0:T(8,128)(2,1)S(1)}, bf16[32,256]{1,0:T(8,128)(2,1)S(1)}, u32[]{:S(2)}, u32[]{:S(2)}) collective-permute-start(bf16[32,256]{1,0:T(8,128)(2,1)S(1)} %get-tuple-element.63), channel_id=1, source_target_pairs={{4,8},{8,4},{12,16},{16,12},{20,24},{24,20},{28,0},{0,28},{5,9},{9... | collective-permute-start | bytes 49160 | tf_op jit(solution)/shard_map/ppermute | solution.py:31
  35.0 2.3 %collective-permute-start.10 = (bf16[32,256]{1,0:T(8,128)(2,1)S(1)}, bf16[32,256]{1,0:T(8,128)(2,1)S(1)}, u32[]{:S(2)}, u32[]{:S(2)}) collective-permute-start(bf16[32,256]{1,0:T(8,128)(2,1)S(1)} %get-tuple-element.64), channel_id=1, source_target_pairs={{0,4},{4,0},{8,12},{12,8},{16,20},{20,16},{24,28},{28,24},{1,5},{5... | collective-permute-start | bytes 49160 | tf_op jit(solution)/shard_map/ppermute | solution.py:31

commit v3 on v2

--- a/solution.py
+++ b/solution.py
@@ -145,7 +145,7 @@
             send_ref[0][i] = out_ref[other_block(i, k + 1)]
 
 
-def spread_kernel(matrix_ref, blocks_ref):
+def spread_kernel(k, matrix_ref, blocks_ref, send_ref):
     slabs, rows, _ = blocks_ref.shape
     prim = matrix_ref.shape[0] // slabs
     half = prim // 2
@@ -163,6 +163,8 @@
     for g in range(slabs):
         own = jnp.concatenate([spread[g * prim : (g + 1) * prim], empty], axis=0)
         blocks_ref[g] = own.astype(BF16)
+    for i in range(send_ref.shape[0]):
+        send_ref[i] = blocks_ref[other_block(i, k)]
 
 
 def conduct_at(row, sector):
@@ -202,7 +204,7 @@
     curv_ref[0:1, n : 2 * n] = curv - high
 
 
-def coarse_rhs_kernel(perm_ref, image_ref, r0, r1, r2, r3, weight_ref, basis_ref, rhs_ref, curv_ref,
+def coarse_rhs_kernel(rows, sectors, perm_ref, image_ref, r0, r1, r2, r3, weight_ref, basis_ref, rhs_ref, curv_ref,
                       assembled_ref, scaled_ref, out_ref):
     for at, part in received_blocks(perm_ref, (r0, r1, r2, r3), image_ref.shape[1] // BLK):
         assembled_ref[:, at] = image_ref[:, at] + part
@@ -213,36 +215,50 @@
     )
     rhs_r = rhs_ref[...]
     half = rhs_r.shape[0] // 2
-    rows = out_ref.shape[1]
     packed = jnp.concatenate([rhs_r[:half], rhs_q[:half], rhs_r[half:], rhs_q[half:]], axis=1)
     packed = jnp.concatenate(
         [packed, curv_ref[0:1, :], jnp.zeros((rows - half - 1, BLK), F32)], axis=0
-    ).astype(BF16)
-    for i in range(out_ref.shape[0]):
-        out_ref[i] = packed
-
-
-def neumann_kernel(scaled_r_ref, scaled_q_ref, neumann_ref, sol_r_ref, sol_q_ref):
-    sol_r_ref[...] = jnp.dot(scaled_r_ref[...], neumann_ref[...], preferred_element_type=F32)
-    sol_q_ref[...] = jnp.dot(scaled_q_ref[...], neumann_ref[...], preferred_element_type=F32)
-
-
-def solve_kernel(perm_ref, gathered_ref, blocks_ref, rz_ref, resid_ref, assembled_ref, weight_ref,
+    )
+    several = jnp.concatenate([packed] * sectors, axis=0).astype(BF16)
+    step = several.shape[0]
+    for i in range(out_ref.shape[0] // step):
+        out_ref[i * step : (i + 1) * step] = several
+
+
+def neumann_kernel(scaled_r_ref, scaled_q_ref, neumann_hbm, sol_r_ref, sol_q_ref, neumann_ref, sems):
+    rows = neumann_ref.shape[0] // CHUNKS
+    parts = [pl.ds(i * rows, rows) for i in range(CHUNKS)]
+    copies = [
+        pltpu.make_async_copy(neumann_hbm.at[part], neumann_ref.at[part], sems.at[i])
+        for i, part in enumerate(parts)
+    ]
+    for copy in copies:
+        copy.start()
+    total_r = total_q = None
+    for copy, part in zip(copies, parts):
+        copy.wait()
+        term_r = jnp.dot(scaled_r_ref[:, part], neumann_ref[part], preferred_element_type=F32)
+        term_q = jnp.dot(scaled_q_ref[:, part], neumann_ref[part], preferred_element_type=F32)
+        total_r = term_r if total_r is None else total_r + term_r
+        total_q = term_q if total_q is None else total_q + term_q
+    sol_r_ref[...] = total_r
+    sol_q_ref[...] = total_q
+
+
+def solve_kernel(rows, perm_ref, gathered_ref, blocks_ref, rz_ref, resid_ref, assembled_ref, weight_ref,
                  basis_ref, sol_r_ref, sol_q_ref, step_out, weighted_out, rz_out, *faces):
     n = rz_ref.shape[1]
     prim = basis_ref.shape[0]
     slabs, _, width = blocks_ref.shape
     width = width // 2
-    sectors = gathered_ref.shape[0] // slabs
-    depth = gathered_ref.shape[1]
     total = None
     for h in range(slabs):
-        part = gathered_ref[h * sectors : (h + 1) * sectors].reshape(width, 4 * n)
+        part = gathered_ref[h * width : (h + 1) * width]
         halves = jnp.concatenate([part[:, : 2 * n], part[:, 2 * n :]], axis=0)
         term = jnp.dot(blocks_ref[h], halves, preferred_element_type=F32)
         total = term if total is None else total + term
-    everything = gathered_ref[...].reshape(slabs * width, 4 * n)
-    at = lax.broadcasted_iota(jnp.int32, (16, slabs * width), 1) % depth
+    everything = gathered_ref[...]
+    at = lax.broadcasted_iota(jnp.int32, (16, slabs * width), 1) % rows
     picks = jnp.where(at == prim // 2, 1.0, 0.0).astype(BF16)
     sums = jnp.dot(picks, everything, preferred_element_type=F32)
     step = rz_ref[...] / (sums[0:1, 0:n] + sums[0:1, n : 2 * n])
@@ -284,7 +300,7 @@
     rhs, width = resid.shape
     prim = basis_t.shape[0]
     slabs, sectors = lax.axis_size("gx"), lax.axis_size("col")
-    rows = -(-(prim // 2 + 1) // 16) * 16
+    rows = -(-(prim // 2 + 1) // 4) * 4
     block_rows = -(-prim // 16) * 16
     rounds = slabs.bit_length() - 1
     face = jax.ShapeDtypeStruct((rhs, 2 * BLK), BF16)
@@ -323,9 +339,9 @@
         in_specs=[vmem] * 6, out_specs=(vmem,) * 4, compiler_params=params(),
         cost_estimate=cost(2 * rhs * width * prim, 8 * rhs * width),
     )(perm, conduct, direction, image, resid, basis_t)
-    for k in range(rounds):
+    for k in range(rounds - 1):
         got = swap_bit(send, k)
-        last = k + 1 == rounds
+        last = k + 2 == rounds
         coarse, *send = pl.pallas_call(
             functools.partial(merge_kernel, k, last),
             out_shape=(coarse_type,) if last else (coarse_type, send_type),
@@ -333,27 +349,36 @@
             compiler_params=params(), cost_estimate=cost(1 << 10, 1 << 16),
         )(coarse, got)
         send = send[0] if send else None
-    blocks = pl.pallas_call(
-        spread_kernel, out_shape=blocks_type, in_specs=[vmem], out_specs=vmem,
+    blocks, send = pl.pallas_call(
+        functools.partial(spread_kernel, rounds - 1),
+        out_shape=(blocks_type, jax.ShapeDtypeStruct((slabs // 2,) + blocks_type.shape[1:], BF16)),
+        in_specs=[vmem], out_specs=(vmem,) * 2,
         compiler_params=params(), cost_estimate=cost(1 << 20, 1 << 16),
     )(coarse.reshape(slabs * prim, sectors * prim))
+    (blocks,) = pl.pallas_call(
+        functools.partial(merge_kernel, rounds - 1, True),
+        out_shape=(blocks_type,), in_specs=[vmem] * 2, out_specs=(vmem,),
+        compiler_params=params(), cost_estimate=cost(1 << 10, 1 << 16),
+    )(blocks, swap_bit(send, rounds - 1))
     assembled, scaled_q, packed = pl.pallas_call(
-        coarse_rhs_kernel,
+        functools.partial(coarse_rhs_kernel, rows, sectors),
         out_shape=(
             full,
             jax.ShapeDtypeStruct((rhs, width), BF16),
-            jax.ShapeDtypeStruct((slabs * sectors, rows, BLK), BF16),
+            jax.ShapeDtypeStruct((slabs * sectors * rows, BLK), BF16),
         ),
         in_specs=[vmem] + [vmem] * 9, out_specs=(vmem,) * 3, compiler_params=params(),
         cost_estimate=cost(2 * rhs * width * prim, 8 * rhs * width),
     )(perm, image, *received, weight, basis_t, rhs_r, curv)
-    gathered = lax.all_to_all(packed, ("gx", "col"), 0, 0)
+    packed = packed.reshape(slabs * sectors, rows // 2, 2, BLK)
+    gathered = lax.all_to_all(packed, ("gx", "col"), 0, 0).reshape(slabs * sectors * rows, BLK)
     sol_r, sol_q = pl.pallas_call(
-        neumann_kernel, out_shape=(full, full), in_specs=[vmem] * 3, out_specs=(vmem,) * 2,
+        neumann_kernel, out_shape=(full, full), in_specs=[vmem, vmem, hbm], out_specs=(vmem,) * 2,
+        scratch_shapes=[pltpu.VMEM((width, width), BF16), pltpu.SemaphoreType.DMA((CHUNKS,))],
         compiler_params=params(), cost_estimate=cost(1000 * flops, 2 * width * width),
-    )(scaled_r, scaled_q, neumann)
+    )(scaled_r, scaled_q, pltpu.with_memory_space_constraint(neumann, pltpu.HBM))
     step, weighted, partial, *faces = pl.pallas_call(
-        solve_kernel,
+        functools.partial(solve_kernel, rows),
         out_shape=(
             jax.ShapeDtypeStruct((rhs, BLK), F32),
             full,

time: 38.4 us -> 37.4 us (0.974)
  waiting for transfers between devices: 7.17 us -> 5.51 us
  Pallas kernels: 7.59 us -> 8.64 us
    ppermute x3, waiting for transfers between devices: 2.76 us -> 0.06 us  [swap_bit(): return lax.ppermute(value, 'gx', [(i, i ^ 1 << k) for i in range(count)])]
    pallas_call x4 -> x5, Pallas kernels: 3.22 us -> 4.54 us  [the longest x1 2.1 us: body(): pl.pallas_call(neumann_kernel, out_shape=(full, full), in_specs=[vmem, vm...]
    all_to_all x1, waiting for transfers between devices: 2.45 us -> 3.49 us  [body(): lax.all_to_all(packed, ('gx', 'col'), 0, 0)]
  transfers between devices with their start and end apart: 13 -> 13, of which waited for: 6 -> 6; matrix products, arithmetic and copies ran while one was open for 1% -> 1% of each run, Pallas kernels for 9% -> 12%
where the time goes in v3:
time: 37.4 us; the launch traced here: 37.2 us
  starting transfers between devices  22.1 us (59%)
  Pallas kernels  8.64 us (23%)
  waiting for transfers between devices  5.51 us (15%)
  between operations  0.74 us (2%)
    ppermute x8, starting transfers between devices, swap(): return lax.ppermute(value, axis, pairs)  12.5 us
    all_to_all x1, starting transfers between devices, body(): lax.all_to_all(packed, ('gx', 'col'), 0, 0)  3.76 us
    all_to_all x1, waiting for transfers between devices, body(): lax.all_to_all(packed, ('gx', 'col'), 0, 0)  3.49 us
    ppermute x3, starting transfers between devices, swap_bit(): return lax.ppermute(value, 'gx', [(i, i ^ 1 << k) for i in range(count)])  3.29 us
    all_to_all x1, starting transfers between devices, body(): partials = lax.all_to_all(partial, ('gx', 'col'), 0, 0)  2.54 us
    pallas_call x1, Pallas kernels, body(): pl.pallas_call(neumann_kernel, out_shape=(full, full), in_specs=[vmem, vm...  2.1 us
    pallas_call x1, Pallas kernels, body(): pl.pallas_call(image_kernel, out_shape=(full,) + (face,) * 4 + (send_type...  2.06 us
    ppermute x8, waiting for transfers between devices, swap(): return lax.ppermute(value, axis, pairs)  1.95 us
  transfers between devices with their start and end apart: 13, of which 6 were waited for; matrix products, arithmetic and copies ran while one was open for 1% of the time, Pallas kernels for 12%

profile of v3, /device:TPU:0, one launch (start us, length us, event | category | flops | bytes accessed | tf_op | source)
XLA Modules:
  0.0 37.2 jit_solution(5155707087585875401)
XLA Ops:
  0.6 0.0 copy-start
  0.6 0.0 copy-start.2
  0.7 2.1 %shard_map.112 = (f32[32,1024]{1,0:T(8,128)S(1)}, bf16[32,256]{1,0:T(8,128)(2,1)S(1)}, bf16[32,256]{1,0:T(8,128)(2,1)S(1)}, bf16[32,256]{1,0:T(8,128)(2,1)S(1)},...) custom-call(s32[1,8]{1,0:T(1,128)} %bitcast.16, ...), custom_call_target="tpu_custom_call" | custom-call | flops 67108864 | bytes 2097152 | tf_op jit(solution)/shard_map/pallas_call | solution.py:318
  2.7 0.5 %collective-permute-start.4 = (bf16[4,20,4,20]{3,2,1,0:T(4,128)(2,1)S(1)}, bf16[4,20,4,20]{3,2,1,0:T(4,128)(2,1)S(1)}, u32[]{:S(2)}, u32[]{:S(2)}) collective-permute-start(bf16[4,20,4,20]{3,2,1,0:T(4,128)(2,1)S(1)} %get-tuple-element.48), channel_id=1, source_target_pairs={{0,4},{4,0},{8,12},{12,8},{16,20},{20,16},{24,28},{28,24},{1,5},{5... | collective-permute-start | bytes 38408 | tf_op jit(solution)/shard_map/ppermute | solution.py:111
  3.2 4.7 %collective-permute-start = (bf16[32,256]{1,0:T(8,128)(2,1)S(1)}, bf16[32,256]{1,0:T(8,128)(2,1)S(1)}, u32[]{:S(2)}, u32[]{:S(2)}) collective-permute-start(bf16[32,256]{1,0:T(8,128)(2,1)S(1)} %get-tuple-element.36), channel_id=1, source_target_pairs={{1,2},{2,1},{3,0},{0,3},{5,6},{6,5},{7,4},{4,7},{9,10},{10,9},{11,... | collective-permute-start | bytes 49160 | tf_op jit(solution)/shard_map/ppermute | solution.py:31
  7.9 0.0 collective-permute-start.1
  7.9 2.2 %collective-permute-start.2 = (bf16[32,256]{1,0:T(8,128)(2,1)S(1)}, bf16[32,256]{1,0:T(8,128)(2,1)S(1)}, u32[]{:S(2)}, u32[]{:S(2)}) collective-permute-start(bf16[32,256]{1,0:T(8,128)(2,1)S(1)} %get-tuple-element.38), channel_id=1, source_target_pairs={{4,8},{8,4},{12,16},{16,12},{20,24},{24,20},{28,0},{0,28},{5,9},{9... | collective-permute-start | bytes 49160 | tf_op jit(solution)/shard_map/ppermute | solution.py:31
  10.1 0.0 collective-permute-start.3
  10.1 0.0 collective-permute-done.4.got_ref
  10.1 0.1 shard_map.115
  10.3 0.9 %collective-permute-start.5 = (bf16[4,20,4,20]{3,2,1,0:T(4,128)(2,1)S(1)}, bf16[4,20,4,20]{3,2,1,0:T(4,128)(2,1)S(1)}, u32[]{:S(2)}, u32[]{:S(2)}) collective-permute-start(bf16[4,20,4,20]{3,2,1,0:T(4,128)(2,1)S(1)} %get-tuple-element.50), channel_id=1, source_target_pairs={{0,8},{4,12},{8,0},{12,4},{16,24},{20,28},{24,16},{28,20},{1,9},{5... | collective-permute-start | bytes 38408 | tf_op jit(solution)/shard_map/ppermute | solution.py:111
  11.2 0.0 copy-done.2
  11.2 0.1 copy.12.conduct_ref
  11.3 0.0 copy-done
  11.3 0.3 shard_map.113
  11.6 0.0 collective-permute-done.r0
  11.6 0.1 collective-permute-done.1.r1
  11.7 0.3 collective-permute-done.2.r2
  12.0 0.0 collective-permute-done.3.r3
  12.0 1.0 %shard_map.114 = (f32[32,1024]{1,0:T(8,128)S(1)}, bf16[32,1024]{1,0:T(8,128)(2,1)S(1)}, bf16[384,128]{1,0:T(8,128)(2,1)}) custom-call(s32[1,8]{1,0:T(1,128)S(1)} %bitcast.18, f32[32,1024]{1,0:T(8,128)S(1)} %get-tuple-element.35.image_ref, bf16[32,256]{1,0:T(8,128)(2,1)S(1)} %collective-permute-done.r0, bf16[32,256]{1,0:T(8,128)(2,1)S(1)} %collective-permute-done.1.r1, ...), custom_call_target="tpu_custom_call" | custom-call | flops 1310720 | bytes 262144 | tf_op jit(solution)/shard_map/pallas_call | solution.py:363
  13.0 3.8 %all-to-all-start = ((bf16[32,6,2,128]{3,2,1,0:T(2,128)(2,1)}), bf16[32,6,2,128]{3,2,1,0:T(2,128)(2,1)S(1)}, u32[]{:S(2)}, u32[]{:S(2)}) async-start(bf16[32,6,2,128]{3,2,1,0:T(2,128)(2,1)} %bitcast.7), calls=%async_computation | async-start | bytes 196608 | tf_op jit(solution)/shard_map/all_to_all | solution.py:374
  16.7 0.0 collective-permute-done.5.got_ref
  16.7 0.1 shard_map.116
  16.8 0.1 reshape.17.matrix_ref
  17.0 0.2 shard_map.117
  17.2 1.8 %collective-permute-start.6 = (bf16[4,32,96]{2,1,0:T(8,128)(2,1)S(1)}, bf16[4,32,96]{2,1,0:T(8,128)(2,1)S(1)}, u32[]{:S(2)}, u32[]{:S(2)}) collective-permute-start(bf16[4,32,96]{2,1,0:T(8,128)(2,1)S(1)} %get-tuple-element.52), channel_id=1, source_target_pairs={{0,16},{4,20},{8,24},{12,28},{16,0},{20,4},{24,8},{28,12},{1,17},{... | collective-permute-start | bytes 73736 | tf_op jit(solution)/shard_map/ppermute | solution.py:111
  19.0 0.0 copy-start.1
  19.0 2.1 %shard_map.119 = (f32[32,1024]{1,0:T(8,128)S(1)}, f32[32,1024]{1,0:T(8,128)S(1)}) custom-call(bf16[32,1024]{1,0:T(8,128)(2,1)S(1)} %get-tuple-element.54.scaled_r_ref, bf16[32,1024]{1,0:T(8,128)(2,1)S(1)} %get-tuple-element.55.scaled_q_ref, bf16[1024,1024]{1,0:T(8,128)(2,1)} %bitcast.29), custom_call_target="tpu_custom_call" | custom-call | flops 67108864000 | bytes 2097152 | tf_op jit(solution)/shard_map/pallas_call | solution.py:375
  21.1 0.1 collective-permute-done.6.got_ref
  21.2 3.5 %all-to-all-done = bf16[32,6,2,128]{3,2,1,0:T(2,128)(2,1)S(1)} async-done(((bf16[32,6,2,128]{3,2,1,0:T(2,128)(2,1)}), bf16[32,6,2,128]{3,2,1,0:T(2,128)(2,1)S(1)}, u32[]{:S(2)}, u32[]{:S(2)}) %all-to-all-start) | async-done | bytes 98336 | tf_op jit(solution)/shard_map/all_to_all | solution.py:374
  24.7 0.0 copy-done.1
  24.7 1.3 %shard_map.120 = (f32[32,128]{1,0:T(8,128)S(1)}, f32[32,1024]{1,0:T(8,128)S(1)}, f32[32,1,128]{2,1,0:T(1,128)}, bf16[32,256]{1,0:T(8,128)(2,1)S(1)}, bf16[32,256...) custom-call(s32[1,8]{1,0:T(1,128)S(1)} %bitcast.19, bf16[384,128]{1,0:T(8,128)(2,1)S(1)} %bitcast.15, ...), custom_call_target="tpu_custom_call" | custom-call | flops 1310720 | bytes 262144 | tf_op jit(solution)/shard_map/pallas_call | solution.py:380
  25.9 2.5 %all-to-all-start.1 = ((f32[32,1,128]{2,1,0:T(1,128)}), f32[32,1,128]{2,1,0:T(1,128)S(1)}, u32[]{:S(2)}, u32[]{:S(2)}) async-start(f32[32,1,128]{2,1,0:T(1,128)} %get-tuple-element.59), calls=%async_computation.1 | async-start | bytes 32768 | tf_op jit(solution)/shard_map/all_to_all | solution.py:391
  28.5 3.7 %collective-permute-start.7 = (bf16[32,256]{1,0:T(8,128)(2,1)S(1)}, bf16[32,256]{1,0:T(8,128)(2,1)S(1)}, u32[]{:S(2)}, u32[]{:S(2)}) collective-permute-start(bf16[32,256]{1,0:T(8,128)(2,1)S(1)} %get-tuple-element.61), channel_id=1, source_target_pairs={{1,2},{2,1},{3,0},{0,3},{5,6},{6,5},{7,4},{4,7},{9,10},{10,9},{11,... | collective-permute-start | bytes 49160 | tf_op jit(solution)/shard_map/ppermute | solution.py:31
  32.2 0.0 collective-permute-start.8
  32.2 1.9 %collective-permute-start.9 = (bf16[32,256]{1,0:T(8,128)(2,1)S(1)}, bf16[32,256]{1,0:T(8,128)(2,1)S(1)}, u32[]{:S(2)}, u32[]{:S(2)}) collective-permute-start(bf16[32,256]{1,0:T(8,128)(2,1)S(1)} %get-tuple-element.63), channel_id=1, source_target_pairs={{4,8},{8,4},{12,16},{16,12},{20,24},{24,20},{28,0},{0,28},{5,9},{9... | collective-permute-start | bytes 49160 | tf_op jit(solution)/shard_map/ppermute | solution.py:31
  34.1 0.0 collective-permute-start.10
  34.1 0.7 %shard_map.121 = f32[32,1024]{1,0:T(8,128)} custom-call(f32[32,128]{1,0:T(8,128)S(1)} %get-tuple-element.58.step_ref, f32[32,1024]{1,0:T(8,128)S(1)} %get-tuple-element.41.resid_ref, f32[32,1024]{1,0:T(8,128)S(1)} %get-tuple-element.53.assembled_ref), custom_call_target="tpu_custom_call" | custom-call | flops 65536 | bytes 393216 | tf_op jit(solution)/shard_map/pallas_call | solution.py:393
  34.8 0.0 collective-permute-done.7.r0
  34.8 1.1 %collective-permute-done.8.r1 = bf16[32,256]{1,0:T(8,128)(2,1)S(1)} collective-permute-done((bf16[32,256]{1,0:T(8,128)(2,1)S(1)}, bf16[32,256]{1,0:T(8,128)(2,1)S(1)}, u32[]{:S(2)}, u32[]{:S(2)}) %collective-permute-start.8) | collective-permute-done | bytes 16416 | tf_op jit(solution)/shard_map/ppermute | solution.py:31
  35.9 0.4 %collective-permute-done.9.r2 = bf16[32,256]{1,0:T(8,128)(2,1)S(1)} collective-permute-done((bf16[32,256]{1,0:T(8,128)(2,1)S(1)}, bf16[32,256]{1,0:T(8,128)(2,1)S(1)}, u32[]{:S(2)}, u32[]{:S(2)}) %collective-permute-start.9) | collective-permute-done | bytes 16416 | tf_op jit(solution)/shard_map/ppermute | solution.py:31
  36.3 0.0 collective-permute-done.10.r3
  36.3 0.0 all-to-all-done.1.partials_ref
  36.3 0.8 %shard_map.122 = (f32[32,1024]{1,0:T(8,128)}, f32[1,32]{1,0:T(1,128)}) custom-call(s32[1,8]{1,0:T(1,128)S(1)} %bitcast.20, f32[32,1,128]{2,1,0:T(1,128)S(1)} %all-to-all-done.1.partials_ref, f32[1,32]{1,0:T(1,128)S(1)} %bitcast.22, f32[32,1024]{1,0:T(8,128)S(1)} %get-tuple-element.40.dir_ref, f32[32,1024]{1,0:T(8,128)S(1)} %get-tuple-element.60.weighted_ref, ...), custom_call_target="tpu_custom_call" | custom-call | flops 65536 | bytes 262144 | tf_op jit(solution)/shard_map/pallas_call | solution.py:397
  (1 shorter events, 0.0 us)
Async XLA Ops:
  0.6 10.7 %copy-start = (s32[1,1,8]{2,1,0:T(1,128)S(1)}, s32[1,1,8]{2,1,0:T(1,128)}, u32[]{:S(2)}) copy-start(s32[1,1,8]{2,1,0:T(1,128)} %param.17) | copy-start | bytes 100
  0.6 10.6 %copy-start.2 = (f32[8,4]{0,1:T(4,128)S(1)}, f32[8,4]{0,1:T(4,128)}, u32[]{:S(2)}) copy-start(f32[8,4]{0,1:T(4,128)} %param.16) | copy-start | bytes 388
  2.7 7.4 %collective-permute-start.4 = (bf16[4,20,4,20]{3,2,1,0:T(4,128)(2,1)S(1)}, bf16[4,20,4,20]{3,2,1,0:T(4,128)(2,1)S(1)}, u32[]{:S(2)}, u32[]{:S(2)}) collective-permute-start(bf16[4,20,4,20]{3,2,1,0:T(4,128)(2,1)S(1)} %get-tuple-element.48), channel_id=1, source_target_pairs={{0,4},{4,0},{8,12},{12,8},{16,20},{20,16},{24,28},{28,24},{1,5},{5... | collective-permute-start | bytes 38408 | tf_op jit(solution)/shard_map/ppermute | solution.py:111
  3.2 8.3 %collective-permute-start = (bf16[32,256]{1,0:T(8,128)(2,1)S(1)}, bf16[32,256]{1,0:T(8,128)(2,1)S(1)}, u32[]{:S(2)}, u32[]{:S(2)}) collective-permute-start(bf16[32,256]{1,0:T(8,128)(2,1)S(1)} %get-tuple-element.36), channel_id=1, source_target_pairs={{1,2},{2,1},{3,0},{0,3},{5,6},{6,5},{7,4},{4,7},{9,10},{10,9},{11,... | collective-permute-start | bytes 49160 | tf_op jit(solution)/shard_map/ppermute | solution.py:31
  7.9 3.7 %collective-permute-start.1 = (bf16[32,256]{1,0:T(8,128)(2,1)S(1)}, bf16[32,256]{1,0:T(8,128)(2,1)S(1)}, u32[]{:S(2)}, u32[]{:S(2)}) collective-permute-start(bf16[32,256]{1,0:T(8,128)(2,1)S(1)} %get-tuple-element.37), channel_id=1, source_target_pairs={{0,1},{1,0},{2,3},{3,2},{4,5},{5,4},{6,7},{7,6},{8,9},{9,8},{10,11... | collective-permute-start | bytes 49160 | tf_op jit(solution)/shard_map/ppermute | solution.py:31
  7.9 4.1 %collective-permute-start.2 = (bf16[32,256]{1,0:T(8,128)(2,1)S(1)}, bf16[32,256]{1,0:T(8,128)(2,1)S(1)}, u32[]{:S(2)}, u32[]{:S(2)}) collective-permute-start(bf16[32,256]{1,0:T(8,128)(2,1)S(1)} %get-tuple-element.38), channel_id=1, source_target_pairs={{4,8},{8,4},{12,16},{16,12},{20,24},{24,20},{28,0},{0,28},{5,9},{9... | collective-permute-start | bytes 49160 | tf_op jit(solution)/shard_map/ppermute | solution.py:31
  10.1 1.8 %collective-permute-start.3 = (bf16[32,256]{1,0:T(8,128)(2,1)S(1)}, bf16[32,256]{1,0:T(8,128)(2,1)S(1)}, u32[]{:S(2)}, u32[]{:S(2)}) collective-permute-start(bf16[32,256]{1,0:T(8,128)(2,1)S(1)} %get-tuple-element.39), channel_id=1, source_target_pairs={{0,4},{4,0},{8,12},{12,8},{16,20},{20,16},{24,28},{28,24},{1,5},{5... | collective-permute-start | bytes 49160 | tf_op jit(solution)/shard_map/ppermute | solution.py:31
  10.3 6.5 %collective-permute-start.5 = (bf16[4,20,4,20]{3,2,1,0:T(4,128)(2,1)S(1)}, bf16[4,20,4,20]{3,2,1,0:T(4,128)(2,1)S(1)}, u32[]{:S(2)}, u32[]{:S(2)}) collective-permute-start(bf16[4,20,4,20]{3,2,1,0:T(4,128)(2,1)S(1)} %get-tuple-element.50), channel_id=1, source_target_pairs={{0,8},{4,12},{8,0},{12,4},{16,24},{20,28},{24,16},{28,20},{1,9},{5... | collective-permute-start | bytes 38408 | tf_op jit(solution)/shard_map/ppermute | solution.py:111
  13.0 11.7 %all-to-all-start = ((bf16[32,6,2,128]{3,2,1,0:T(2,128)(2,1)}), bf16[32,6,2,128]{3,2,1,0:T(2,128)(2,1)S(1)}, u32[]{:S(2)}, u32[]{:S(2)}) async-start(bf16[32,6,2,128]{3,2,1,0:T(2,128)(2,1)} %bitcast.7), calls=%async_computation | async-start | bytes 196608 | tf_op jit(solution)/shard_map/all_to_all | solution.py:374
  17.2 4.0 %collective-permute-start.6 = (bf16[4,32,96]{2,1,0:T(8,128)(2,1)S(1)}, bf16[4,32,96]{2,1,0:T(8,128)(2,1)S(1)}, u32[]{:S(2)}, u32[]{:S(2)}) collective-permute-start(bf16[4,32,96]{2,1,0:T(8,128)(2,1)S(1)} %get-tuple-element.52), channel_id=1, source_target_pairs={{0,16},{4,20},{8,24},{12,28},{16,0},{20,4},{24,8},{28,12},{1,17},{... | collective-permute-start | bytes 73736 | tf_op jit(solution)/shard_map/ppermute | solution.py:111
  19.0 5.7 %copy-start.1 = (f32[32]{0:T(128)S(1)}, f32[32]{0:T(128)}, u32[]{:S(2)}) copy-start(f32[32]{0:T(128)} %param.11) | copy-start | bytes 388
  25.9 10.4 %all-to-all-start.1 = ((f32[32,1,128]{2,1,0:T(1,128)}), f32[32,1,128]{2,1,0:T(1,128)S(1)}, u32[]{:S(2)}, u32[]{:S(2)}) async-start(f32[32,1,128]{2,1,0:T(1,128)} %get-tuple-element.59), calls=%async_computation.1 | async-start | bytes 32768 | tf_op jit(solution)/shard_map/all_to_all | solution.py:391
  28.5 6.3 %collective-permute-start.7 = (bf16[32,256]{1,0:T(8,128)(2,1)S(1)}, bf16[32,256]{1,0:T(8,128)(2,1)S(1)}, u32[]{:S(2)}, u32[]{:S(2)}) collective-permute-start(bf16[32,256]{1,0:T(8,128)(2,1)S(1)} %get-tuple-element.61), channel_id=1, source_target_pairs={{1,2},{2,1},{3,0},{0,3},{5,6},{6,5},{7,4},{4,7},{9,10},{10,9},{11,... | collective-permute-start | bytes 49160 | tf_op jit(solution)/shard_map/ppermute | solution.py:31
  32.2 3.7 %collective-permute-start.8 = (bf16[32,256]{1,0:T(8,128)(2,1)S(1)}, bf16[32,256]{1,0:T(8,128)(2,1)S(1)}, u32[]{:S(2)}, u32[]{:S(2)}) collective-permute-start(bf16[32,256]{1,0:T(8,128)(2,1)S(1)} %get-tuple-element.62), channel_id=1, source_target_pairs={{0,1},{1,0},{2,3},{3,2},{4,5},{5,4},{6,7},{7,6},{8,9},{9,8},{10,11... | collective-permute-start | bytes 49160 | tf_op jit(solution)/shard_map/ppermute | solution.py:31
  32.2 4.2 %collective-permute-start.9 = (bf16[32,256]{1,0:T(8,128)(2,1)S(1)}, bf16[32,256]{1,0:T(8,128)(2,1)S(1)}, u32[]{:S(2)}, u32[]{:S(2)}) collective-permute-start(bf16[32,256]{1,0:T(8,128)(2,1)S(1)} %get-tuple-element.63), channel_id=1, source_target_pairs={{4,8},{8,4},{12,16},{16,12},{20,24},{24,20},{28,0},{0,28},{5,9},{9... | collective-permute-start | bytes 49160 | tf_op jit(solution)/shard_map/ppermute | solution.py:31
  34.1 2.3 %collective-permute-start.10 = (bf16[32,256]{1,0:T(8,128)(2,1)S(1)}, bf16[32,256]{1,0:T(8,128)(2,1)S(1)}, u32[]{:S(2)}, u32[]{:S(2)}) collective-permute-start(bf16[32,256]{1,0:T(8,128)(2,1)S(1)} %get-tuple-element.64), channel_id=1, source_target_pairs={{0,4},{4,0},{8,12},{12,8},{16,20},{20,16},{24,28},{28,24},{1,5},{5... | collective-permute-start | bytes 49160 | tf_op jit(solution)/shard_map/ppermute | solution.py:31

commit v4 on v3

--- a/solution.py
+++ b/solution.py
@@ -31,11 +31,23 @@
     return lax.ppermute(value, axis, pairs)
 
 
+def swap_second(value):
+    slabs, sectors = lax.axis_size("gx"), lax.axis_size("col")
+    pairs = []
+    for slab in range(slabs):
+        for sector in range(sectors):
+            other = (slab + 1 if slab % 2 else slab - 1, sector)
+            if not 0 <= other[0] < slabs:
+                other = (slab, sector ^ 1)
+            pairs.append((slab * sectors + sector, other[0] * sectors + other[1]))
+    return lax.ppermute(value, ("gx", "col"), pairs)
+
+
 def swap_faces(faces):
     return (
         swap(faces[0], "col", 1),
         swap(faces[1], "col", 0),
-        swap(faces[2], "gx", 1),
+        swap_second(faces[2]),
         swap(faces[3], "gx", 0),
     )
 
@@ -145,6 +157,23 @@
             send_ref[0][i] = out_ref[other_block(i, k + 1)]
 
 
+def join_kernel(k, depth, prim, blocks_ref, got_ref, wide_ref, all_ref):
+    all_ref[...] = blocks_ref[...]
+    for i in range(got_ref.shape[0]):
+        all_ref[other_block(i, k)] = got_ref[i]
+    slabs, rows, width = blocks_ref.shape
+    width = width // 2
+    for half in range(2):
+        for h in range(slabs):
+            at = (half * slabs + h) * width
+            wide_ref[:, at : at + width] = all_ref[h, :, half * width : (half + 1) * width]
+    row = lax.broadcasted_iota(jnp.int32, wide_ref.shape, 0)
+    lane = lax.broadcasted_iota(jnp.int32, wide_ref.shape, 1)
+    picked = jnp.logical_and(lane < slabs * width, lane % depth == prim // 2)
+    wide = jnp.where(row == prim, jnp.where(picked, 1.0, 0.0), wide_ref[...].astype(F32))
+    wide_ref[...] = wide.astype(BF16)
+
+
 def spread_kernel(k, matrix_ref, blocks_ref, send_ref):
     slabs, rows, _ = blocks_ref.shape
     prim = matrix_ref.shape[0] // slabs
@@ -205,7 +234,7 @@
 
 
 def coarse_rhs_kernel(rows, sectors, perm_ref, image_ref, r0, r1, r2, r3, weight_ref, basis_ref, rhs_ref, curv_ref,
-                      assembled_ref, scaled_ref, out_ref):
+                      assembled_ref, scaled_ref, rhs_q_ref, out_ref):
     for at, part in received_blocks(perm_ref, (r0, r1, r2, r3), image_ref.shape[1] // BLK):
         assembled_ref[:, at] = image_ref[:, at] + part
     scaled = (weight_ref[0:1, :] * assembled_ref[...]).astype(BF16)
@@ -213,6 +242,7 @@
     rhs_q = lax.dot_general(
         basis_ref[...], scaled, (((1,), (1,)), ((), ())), preferred_element_type=F32
     )
+    rhs_q_ref[...] = rhs_q
     rhs_r = rhs_ref[...]
     half = rhs_r.shape[0] // 2
     packed = jnp.concatenate([rhs_r[:half], rhs_q[:half], rhs_r[half:], rhs_q[half:]], axis=1)
@@ -225,7 +255,8 @@
         out_ref[i * step : (i + 1) * step] = several
 
 
-def neumann_kernel(scaled_r_ref, scaled_q_ref, neumann_hbm, sol_r_ref, sol_q_ref, neumann_ref, sems):
+def neumann_kernel(scaled_r_ref, scaled_q_ref, resid_ref, assembled_ref, weight_ref, neumann_hbm,
+                   sol_r_ref, sol_q_ref, sums_ref, neumann_ref, sems):
     rows = neumann_ref.shape[0] // CHUNKS
     parts = [pl.ds(i * rows, rows) for i in range(CHUNKS)]
     copies = [
@@ -243,40 +274,44 @@
         total_q = term_q if total_q is None else total_q + term_q
     sol_r_ref[...] = total_r
     sol_q_ref[...] = total_q
-
-
-def solve_kernel(rows, perm_ref, gathered_ref, blocks_ref, rz_ref, resid_ref, assembled_ref, weight_ref,
-                 basis_ref, sol_r_ref, sol_q_ref, step_out, weighted_out, rz_out, *faces):
+    weighted_r = weight_ref[0:1, :] * resid_ref[...]
+    weighted_q = weight_ref[0:1, :] * assembled_ref[...]
+    n = total_r.shape[0]
+    sums_ref[...] = jnp.zeros_like(sums_ref)
+    for i, product in enumerate(
+        (weighted_r * total_r, weighted_r * total_q + weighted_q * total_r, weighted_q * total_q)
+    ):
+        sums_ref[0:1, i * n : (i + 1) * n] = to_row(jnp.sum(product, axis=1, keepdims=True))
+
+
+def solve_kernel(perm_ref, gathered_ref, wide_ref, rz_ref, weight_ref, basis_ref, sol_r_ref, sol_q_ref,
+                 sums_ref, rhs_r_ref, rhs_q_ref, step_out, weighted_out, rz_hbm, f0, f1, f2, f3, rz_ref_out, sem):
     n = rz_ref.shape[1]
     prim = basis_ref.shape[0]
-    slabs, _, width = blocks_ref.shape
-    width = width // 2
-    total = None
-    for h in range(slabs):
-        part = gathered_ref[h * width : (h + 1) * width]
-        halves = jnp.concatenate([part[:, : 2 * n], part[:, 2 * n :]], axis=0)
-        term = jnp.dot(blocks_ref[h], halves, preferred_element_type=F32)
-        total = term if total is None else total + term
-    everything = gathered_ref[...]
-    at = lax.broadcasted_iota(jnp.int32, (16, slabs * width), 1) % rows
-    picks = jnp.where(at == prim // 2, 1.0, 0.0).astype(BF16)
-    sums = jnp.dot(picks, everything, preferred_element_type=F32)
-    step = rz_ref[...] / (sums[0:1, 0:n] + sums[0:1, n : 2 * n])
+    halves = jnp.concatenate([gathered_ref[:, : 2 * n], gathered_ref[:, 2 * n :]], axis=0)
+    total = jnp.dot(wide_ref[...], halves, preferred_element_type=F32)
+    step = rz_ref[...] / (total[prim : prim + 1, 0:n] + total[prim : prim + 1, n : 2 * n])
     coarse_sol = (total[0:prim, 0:n] - step * total[0:prim, n : 2 * n]).astype(BF16)
+    coarse_part = coarse_sol.astype(F32) * (rhs_r_ref[...] - step * rhs_q_ref[...])
+    partial = (
+        sums_ref[0:1, 0:n]
+        - step * (sums_ref[0:1, n : 2 * n] - step * sums_ref[0:1, 2 * n : 3 * n])
+        + jnp.sum(coarse_part, axis=0, keepdims=True)
+    )
+    partial = jnp.concatenate([partial, jnp.zeros((1, BLK - n), F32)], axis=1)
+    for i in range(rz_ref_out.shape[0]):
+        rz_ref_out[i] = partial
+    copy = pltpu.make_async_copy(rz_ref_out, rz_hbm, sem)
+    copy.start()
     correction = lax.dot_general(
         coarse_sol, basis_ref[...], (((0,), (0,)), ((), ())), preferred_element_type=F32
     )
     step_col = to_column(step)
     step_out[...] = jnp.broadcast_to(step_col, step_out.shape)
-    resid_new = resid_ref[...] - step_col * assembled_ref[...]
-    local = sol_r_ref[...] - step_col * sol_q_ref[...] + correction
-    weighted = weight_ref[0:1, :] * local
+    weighted = weight_ref[0:1, :] * (sol_r_ref[...] - step_col * sol_q_ref[...] + correction)
     weighted_out[...] = weighted
-    put_faces(perm_ref, weighted, faces)
-    partial = to_row(jnp.sum(resid_new * weighted, axis=1, keepdims=True))
-    partial = jnp.concatenate([partial, jnp.zeros((1, BLK - n), F32)], axis=1)
-    for i in range(rz_out.shape[0]):
-        rz_out[i] = partial
+    put_faces(perm_ref, weighted, (f0, f1, f2, f3))
+    copy.wait()
 
 
 def resid_kernel(step_ref, resid_ref, assembled_ref, out_ref):
@@ -301,7 +336,7 @@
     prim = basis_t.shape[0]
     slabs, sectors = lax.axis_size("gx"), lax.axis_size("col")
     rows = -(-(prim // 2 + 1) // 4) * 4
-    block_rows = -(-prim // 16) * 16
+    block_rows = -(-(prim + 1) // 16) * 16
     rounds = slabs.bit_length() - 1
     face = jax.ShapeDtypeStruct((rhs, 2 * BLK), BF16)
     full = jax.ShapeDtypeStruct((rhs, width), F32)
@@ -355,39 +390,45 @@
         in_specs=[vmem], out_specs=(vmem,) * 2,
         compiler_params=params(), cost_estimate=cost(1 << 20, 1 << 16),
     )(coarse.reshape(slabs * prim, sectors * prim))
-    (blocks,) = pl.pallas_call(
-        functools.partial(merge_kernel, rounds - 1, True),
-        out_shape=(blocks_type,), in_specs=[vmem] * 2, out_specs=(vmem,),
+    wide = pl.pallas_call(
+        functools.partial(join_kernel, rounds - 1, rows, prim),
+        out_shape=jax.ShapeDtypeStruct((block_rows, slabs * blocks_type.shape[2]), BF16),
+        in_specs=[vmem] * 2, out_specs=vmem,
+        scratch_shapes=[pltpu.VMEM(blocks_type.shape, BF16)],
         compiler_params=params(), cost_estimate=cost(1 << 10, 1 << 16),
     )(blocks, swap_bit(send, rounds - 1))
-    assembled, scaled_q, packed = pl.pallas_call(
+    assembled, scaled_q, rhs_q, packed = pl.pallas_call(
         functools.partial(coarse_rhs_kernel, rows, sectors),
         out_shape=(
             full,
             jax.ShapeDtypeStruct((rhs, width), BF16),
+            jax.ShapeDtypeStruct((prim, rhs), F32),
             jax.ShapeDtypeStruct((slabs * sectors * rows, BLK), BF16),
         ),
-        in_specs=[vmem] + [vmem] * 9, out_specs=(vmem,) * 3, compiler_params=params(),
+        in_specs=[vmem] + [vmem] * 9, out_specs=(vmem,) * 4, compiler_params=params(),
         cost_estimate=cost(2 * rhs * width * prim, 8 * rhs * width),
     )(perm, image, *received, weight, basis_t, rhs_r, curv)
     packed = packed.reshape(slabs * sectors, rows // 2, 2, BLK)
     gathered = lax.all_to_all(packed, ("gx", "col"), 0, 0).reshape(slabs * sectors * rows, BLK)
-    sol_r, sol_q = pl.pallas_call(
-        neumann_kernel, out_shape=(full, full), in_specs=[vmem, vmem, hbm], out_specs=(vmem,) * 2,
+    sol_r, sol_q, sums = pl.pallas_call(
+        neumann_kernel,
+        out_shape=(full, full, jax.ShapeDtypeStruct((8, BLK), F32)),
+        in_specs=[vmem] * 5 + [hbm], out_specs=(vmem,) * 3,
         scratch_shapes=[pltpu.VMEM((width, width), BF16), pltpu.SemaphoreType.DMA((CHUNKS,))],
         compiler_params=params(), cost_estimate=cost(1000 * flops, 2 * width * width),
-    )(scaled_r, scaled_q, pltpu.with_memory_space_constraint(neumann, pltpu.HBM))
+    )(scaled_r, scaled_q, resid, assembled, weight, pltpu.with_memory_space_constraint(neumann, pltpu.HBM))
     step, weighted, partial, *faces = pl.pallas_call(
-        functools.partial(solve_kernel, rows),
+        solve_kernel,
         out_shape=(
             jax.ShapeDtypeStruct((rhs, BLK), F32),
             full,
             jax.ShapeDtypeStruct((slabs * sectors, 1, BLK), F32),
         )
         + (face,) * 4,
-        in_specs=[vmem] + [vmem] * 9, out_specs=(vmem,) * 7, compiler_params=params(),
-        cost_estimate=cost(2 * rhs * width * prim, 8 * rhs * width),
-    )(perm, gathered, blocks, rz_row, resid, assembled, weight, basis_t, sol_r, sol_q)
+        in_specs=[vmem] * 11, out_specs=(vmem, vmem, hbm) + (vmem,) * 4,
+        scratch_shapes=[pltpu.VMEM((slabs * sectors, 1, BLK), F32), pltpu.SemaphoreType.DMA],
+        compiler_params=params(), cost_estimate=cost(2 * rhs * width * prim, 8 * rhs * width),
+    )(perm, gathered, wide, rz_row, weight, basis_t, sol_r, sol_q, sums, rhs_r, rhs_q)
     partials = lax.all_to_all(partial, ("gx", "col"), 0, 0)
     received = swap_faces(faces)
     resid_new = pl.pallas_call(

time: 37.4 us -> 37 us (0.989)
  waiting for transfers between devices: 5.51 us -> 4.68 us
    ppermute x8 -> x6, starting transfers between devices: 12.5 us -> 8.37 us  [swap(): return lax.ppermute(value, axis, pairs)]
    ppermute x0 -> x2, starting transfers between devices: none -> 4.05 us  [swap_second(): return lax.ppermute(value, ('gx', 'col'), pairs)]
    ppermute x8 -> x6, waiting for transfers between devices: 1.95 us -> 1.07 us  [swap(): return lax.ppermute(value, axis, pairs)]
  transfers between devices with their start and end apart: 13 -> 13, of which waited for: 6 -> 5; matrix products, arithmetic and copies ran while one was open for 1% -> 1% of each run, Pallas kernels for 12% -> 13%
where the time goes in v4:
time: 37 us; the launch traced here: 36.7 us
  starting transfers between devices  22.4 us (61%)
  Pallas kernels  8.72 us (24%)
  waiting for transfers between devices  4.68 us (13%)
  between operations  0.75 us (2%)
    ppermute x6, starting transfers between devices, swap(): return lax.ppermute(value, axis, pairs)  8.37 us
    ppermute x2, starting transfers between devices, swap_second(): return lax.ppermute(value, ('gx', 'col'), pairs)  4.05 us
    all_to_all x1, starting transfers between devices, body(): lax.all_to_all(packed, ('gx', 'col'), 0, 0)  3.89 us
    ppermute x3, starting transfers between devices, swap_bit(): return lax.ppermute(value, 'gx', [(i, i ^ 1 << k) for i in range(count)])  3.49 us
    all_to_all x1, waiting for transfers between devices, body(): lax.all_to_all(packed, ('gx', 'col'), 0, 0)  3.25 us
    all_to_all x1, starting transfers between devices, body(): partials = lax.all_to_all(partial, ('gx', 'col'), 0, 0)  2.56 us
    pallas_call x1, Pallas kernels, body(): pl.pallas_call(neumann_kernel, out_shape=(full, full, jax.ShapeDtypeStruc...  2.26 us
    pallas_call x1, Pallas kernels, body(): pl.pallas_call(image_kernel, out_shape=(full,) + (face,) * 4 + (send_type...  2.06 us
  transfers between devices with their start and end apart: 13, of which 5 were waited for; matrix products, arithmetic and copies ran while one was open for 1% of the time, Pallas kernels for 13%

profile of v4, /device:TPU:0, one launch (start us, length us, event | category | flops | bytes accessed | tf_op | source)
XLA Modules:
  0.0 36.7 jit_solution(6176352579577677713)
XLA Ops:
  0.6 0.0 copy-start
  0.6 0.0 copy-start.2
  0.7 2.1 %shard_map.112 = (f32[32,1024]{1,0:T(8,128)S(1)}, bf16[32,256]{1,0:T(8,128)(2,1)S(1)}, bf16[32,256]{1,0:T(8,128)(2,1)S(1)}, bf16[32,256]{1,0:T(8,128)(2,1)S(1)},...) custom-call(s32[1,8]{1,0:T(1,128)} %bitcast.16, ...), custom_call_target="tpu_custom_call" | custom-call | flops 67108864 | bytes 2097152 | tf_op jit(solution)/shard_map/pallas_call | solution.py:353
  2.7 0.5 %collective-permute-start.4 = (bf16[4,20,4,20]{3,2,1,0:T(4,128)(2,1)S(1)}, bf16[4,20,4,20]{3,2,1,0:T(4,128)(2,1)S(1)}, u32[]{:S(2)}, u32[]{:S(2)}) collective-permute-start(bf16[4,20,4,20]{3,2,1,0:T(4,128)(2,1)S(1)} %get-tuple-element.50), channel_id=1, source_target_pairs={{0,4},{4,0},{8,12},{12,8},{16,20},{20,16},{24,28},{28,24},{1,5},{5... | collective-permute-start | bytes 38408 | tf_op jit(solution)/shard_map/ppermute | solution.py:123
  3.2 4.7 %collective-permute-start = (bf16[32,256]{1,0:T(8,128)(2,1)S(1)}, bf16[32,256]{1,0:T(8,128)(2,1)S(1)}, u32[]{:S(2)}, u32[]{:S(2)}) collective-permute-start(bf16[32,256]{1,0:T(8,128)(2,1)S(1)} %get-tuple-element.38), channel_id=1, source_target_pairs={{1,2},{2,1},{3,0},{0,3},{5,6},{6,5},{7,4},{4,7},{9,10},{10,9},{11,... | collective-permute-start | bytes 49160 | tf_op jit(solution)/shard_map/ppermute | solution.py:31
  7.9 0.0 collective-permute-start.1
  7.9 2.0 %collective-permute-start.2 = (bf16[32,256]{1,0:T(8,128)(2,1)S(1)}, bf16[32,256]{1,0:T(8,128)(2,1)S(1)}, u32[]{:S(2)}, u32[]{:S(2)}) collective-permute-start(bf16[32,256]{1,0:T(8,128)(2,1)S(1)} %get-tuple-element.40), channel_id=1, source_target_pairs={{0,1},{1,0},{2,3},{3,2},{4,8},{5,9},{6,10},{7,11},{8,4},{9,5},{10,... | collective-permute-start | bytes 49160 | tf_op jit(solution)/shard_map/ppermute | solution.py:43
  9.9 0.0 collective-permute-start.3
  9.9 0.0 collective-permute-done.4.got_ref
  9.9 0.1 shard_map.115
  10.1 1.1 %collective-permute-start.5 = (bf16[4,20,4,20]{3,2,1,0:T(4,128)(2,1)S(1)}, bf16[4,20,4,20]{3,2,1,0:T(4,128)(2,1)S(1)}, u32[]{:S(2)}, u32[]{:S(2)}) collective-permute-start(bf16[4,20,4,20]{3,2,1,0:T(4,128)(2,1)S(1)} %get-tuple-element.52), channel_id=1, source_target_pairs={{0,8},{4,12},{8,0},{12,4},{16,24},{20,28},{24,16},{28,20},{1,9},{5... | collective-permute-start | bytes 38408 | tf_op jit(solution)/shard_map/ppermute | solution.py:123
  11.2 0.0 copy-done.2
  11.2 0.1 copy.12.conduct_ref
  11.3 0.0 copy-done
  11.3 0.3 shard_map.113
  11.6 0.0 collective-permute-done.r0
  11.6 0.1 collective-permute-done.1.r1
  11.7 0.2 collective-permute-done.2.r2
  11.8 0.0 collective-permute-done.3.r3
  11.8 1.0 %shard_map.114 = (f32[32,1024]{1,0:T(8,128)S(1)}, bf16[32,1024]{1,0:T(8,128)(2,1)S(1)}, f32[20,32]{1,0:T(8,128)S(1)}, bf16[384,128]{1,0:T(8,128)(2,1)}) custom-call(s32[1,8]{1,0:T(1,128)S(1)} %bitcast.18, f32[32,1024]{1,0:T(8,128)S(1)} %get-tuple-element.37.image_ref, bf16[32,256]{1,0:T(8,128)(2,1)S(1)} %collective-permute-done.r0, ...), custom_call_target="tpu_custom_call" | custom-call | flops 1310720 | bytes 262144 | tf_op jit(solution)/shard_map/pallas_call | solution.py:400
  12.8 3.9 %all-to-all-start = ((bf16[32,6,2,128]{3,2,1,0:T(2,128)(2,1)}), bf16[32,6,2,128]{3,2,1,0:T(2,128)(2,1)S(1)}, u32[]{:S(2)}, u32[]{:S(2)}) async-start(bf16[32,6,2,128]{3,2,1,0:T(2,128)(2,1)} %bitcast.7), calls=%async_computation | async-start | bytes 196608 | tf_op jit(solution)/shard_map/all_to_all | solution.py:412
  16.7 0.0 collective-permute-done.5.got_ref
  16.7 0.1 shard_map.116
  16.8 0.1 reshape.17.matrix_ref
  17.0 0.2 shard_map.117
  17.1 1.8 %collective-permute-start.6 = (bf16[4,32,96]{2,1,0:T(8,128)(2,1)S(1)}, bf16[4,32,96]{2,1,0:T(8,128)(2,1)S(1)}, u32[]{:S(2)}, u32[]{:S(2)}) collective-permute-start(bf16[4,32,96]{2,1,0:T(8,128)(2,1)S(1)} %get-tuple-element.54), channel_id=1, source_target_pairs={{0,16},{4,20},{8,24},{12,28},{16,0},{20,4},{24,8},{28,12},{1,17},{... | collective-permute-start | bytes 73736 | tf_op jit(solution)/shard_map/ppermute | solution.py:123
  19.0 0.0 copy-start.1
  19.0 2.3 %shard_map.119 = (f32[32,1024]{1,0:T(8,128)S(1)}, f32[32,1024]{1,0:T(8,128)S(1)}, f32[8,128]{1,0:T(8,128)S(1)}) custom-call(bf16[32,1024]{1,0:T(8,128)(2,1)S(1)} %get-tuple-element.55.scaled_r_ref, bf16[32,1024]{1,0:T(8,128)(2,1)S(1)} %get-tuple-element.56.scaled_q_ref, f32[32,1024]{1,0:T(8,128)S(1)} %get-tuple-element.43.resid_ref, ...), custom_call_target="tpu_custom_call" | custom-call | flops 67108864000 | bytes 2097152 | tf_op jit(solution)/shard_map/pallas_call | solution.py:413
  21.2 0.0 collective-permute-done.6.got_ref
  21.2 0.1 shard_map.118.wide_ref
  21.4 3.3 %all-to-all-done = bf16[32,6,2,128]{3,2,1,0:T(2,128)(2,1)S(1)} async-done(((bf16[32,6,2,128]{3,2,1,0:T(2,128)(2,1)}), bf16[32,6,2,128]{3,2,1,0:T(2,128)(2,1)S(1)}, u32[]{:S(2)}, u32[]{:S(2)}) %all-to-all-start) | async-done | bytes 98336 | tf_op jit(solution)/shard_map/all_to_all | solution.py:412
  24.6 0.0 copy-done.1
  24.7 1.1 %shard_map.120 = (f32[32,128]{1,0:T(8,128)S(1)}, f32[32,1024]{1,0:T(8,128)S(1)}, f32[32,1,128]{2,1,0:T(1,128)}, bf16[32,256]{1,0:T(8,128)(2,1)S(1)}, bf16[32,256...) custom-call(s32[1,8]{1,0:T(1,128)S(1)} %bitcast.19, bf16[384,128]{1,0:T(8,128)(2,1)S(1)} %bitcast.15, ...), custom_call_target="tpu_custom_call" | custom-call | flops 1310720 | bytes 262144 | tf_op jit(solution)/shard_map/pallas_call | solution.py:420
  25.7 2.6 %all-to-all-start.1 = ((f32[32,1,128]{2,1,0:T(1,128)}), f32[32,1,128]{2,1,0:T(1,128)S(1)}, u32[]{:S(2)}, u32[]{:S(2)}) async-start(f32[32,1,128]{2,1,0:T(1,128)} %get-tuple-element.63), calls=%async_computation.1 | async-start | bytes 32768 | tf_op jit(solution)/shard_map/all_to_all | solution.py:432
  28.3 3.7 %collective-permute-start.7 = (bf16[32,256]{1,0:T(8,128)(2,1)S(1)}, bf16[32,256]{1,0:T(8,128)(2,1)S(1)}, u32[]{:S(2)}, u32[]{:S(2)}) collective-permute-start(bf16[32,256]{1,0:T(8,128)(2,1)S(1)} %get-tuple-element.65), channel_id=1, source_target_pairs={{1,2},{2,1},{3,0},{0,3},{5,6},{6,5},{7,4},{4,7},{9,10},{10,9},{11,... | collective-permute-start | bytes 49160 | tf_op jit(solution)/shard_map/ppermute | solution.py:31
  32.0 0.0 collective-permute-start.8
  32.0 2.0 %collective-permute-start.9 = (bf16[32,256]{1,0:T(8,128)(2,1)S(1)}, bf16[32,256]{1,0:T(8,128)(2,1)S(1)}, u32[]{:S(2)}, u32[]{:S(2)}) collective-permute-start(bf16[32,256]{1,0:T(8,128)(2,1)S(1)} %get-tuple-element.67), channel_id=1, source_target_pairs={{0,1},{1,0},{2,3},{3,2},{4,8},{5,9},{6,10},{7,11},{8,4},{9,5},{10,... | collective-permute-start | bytes 49160 | tf_op jit(solution)/shard_map/ppermute | solution.py:43
  34.0 0.0 collective-permute-start.10
  34.0 0.7 %shard_map.121 = f32[32,1024]{1,0:T(8,128)} custom-call(f32[32,128]{1,0:T(8,128)S(1)} %get-tuple-element.62.step_ref, f32[32,1024]{1,0:T(8,128)S(1)} %get-tuple-element.43.resid_ref, f32[32,1024]{1,0:T(8,128)S(1)} %get-tuple-element.57.assembled_ref), custom_call_target="tpu_custom_call" | custom-call | flops 65536 | bytes 393216 | tf_op jit(solution)/shard_map/pallas_call | solution.py:434
  34.7 0.0 collective-permute-done.7.r0
  34.8 1.0 %collective-permute-done.8.r1 = bf16[32,256]{1,0:T(8,128)(2,1)S(1)} collective-permute-done((bf16[32,256]{1,0:T(8,128)(2,1)S(1)}, bf16[32,256]{1,0:T(8,128)(2,1)S(1)}, u32[]{:S(2)}, u32[]{:S(2)}) %collective-permute-start.8) | collective-permute-done | bytes 16416 | tf_op jit(solution)/shard_map/ppermute | solution.py:31
  35.7 0.2 collective-permute-done.9.r2
  35.9 0.0 collective-permute-done.10.r3
  35.9 0.0 all-to-all-done.1.partials_ref
  35.9 0.8 %shard_map.122 = (f32[32,1024]{1,0:T(8,128)}, f32[1,32]{1,0:T(1,128)}) custom-call(s32[1,8]{1,0:T(1,128)S(1)} %bitcast.20, f32[32,1,128]{2,1,0:T(1,128)S(1)} %all-to-all-done.1.partials_ref, f32[1,32]{1,0:T(1,128)S(1)} %bitcast.22, f32[32,1024]{1,0:T(8,128)S(1)} %get-tuple-element.42.dir_ref, f32[32,1024]{1,0:T(8,128)S(1)} %get-tuple-element.64.weighted_ref, ...), custom_call_target="tpu_custom_call" | custom-call | flops 65536 | bytes 262144 | tf_op jit(solution)/shard_map/pallas_call | solution.py:438
Async XLA Ops:
  0.6 10.7 %copy-start = (s32[1,1,8]{2,1,0:T(1,128)S(1)}, s32[1,1,8]{2,1,0:T(1,128)}, u32[]{:S(2)}) copy-start(s32[1,1,8]{2,1,0:T(1,128)} %param.17) | copy-start | bytes 100
  0.6 10.6 %copy-start.2 = (f32[8,4]{0,1:T(4,128)S(1)}, f32[8,4]{0,1:T(4,128)}, u32[]{:S(2)}) copy-start(f32[8,4]{0,1:T(4,128)} %param.16) | copy-start | bytes 388
  2.7 7.2 %collective-permute-start.4 = (bf16[4,20,4,20]{3,2,1,0:T(4,128)(2,1)S(1)}, bf16[4,20,4,20]{3,2,1,0:T(4,128)(2,1)S(1)}, u32[]{:S(2)}, u32[]{:S(2)}) collective-permute-start(bf16[4,20,4,20]{3,2,1,0:T(4,128)(2,1)S(1)} %get-tuple-element.50), channel_id=1, source_target_pairs={{0,4},{4,0},{8,12},{12,8},{16,20},{20,16},{24,28},{28,24},{1,5},{5... | collective-permute-start | bytes 38408 | tf_op jit(solution)/shard_map/ppermute | solution.py:123
  3.2 8.3 %collective-permute-start = (bf16[32,256]{1,0:T(8,128)(2,1)S(1)}, bf16[32,256]{1,0:T(8,128)(2,1)S(1)}, u32[]{:S(2)}, u32[]{:S(2)}) collective-permute-start(bf16[32,256]{1,0:T(8,128)(2,1)S(1)} %get-tuple-element.38), channel_id=1, source_target_pairs={{1,2},{2,1},{3,0},{0,3},{5,6},{6,5},{7,4},{4,7},{9,10},{10,9},{11,... | collective-permute-start | bytes 49160 | tf_op jit(solution)/shard_map/ppermute | solution.py:31
  7.9 3.7 %collective-permute-start.1 = (bf16[32,256]{1,0:T(8,128)(2,1)S(1)}, bf16[32,256]{1,0:T(8,128)(2,1)S(1)}, u32[]{:S(2)}, u32[]{:S(2)}) collective-permute-start(bf16[32,256]{1,0:T(8,128)(2,1)S(1)} %get-tuple-element.39), channel_id=1, source_target_pairs={{0,1},{1,0},{2,3},{3,2},{4,5},{5,4},{6,7},{7,6},{8,9},{9,8},{10,11... | collective-permute-start | bytes 49160 | tf_op jit(solution)/shard_map/ppermute | solution.py:31
  7.9 3.9 %collective-permute-start.2 = (bf16[32,256]{1,0:T(8,128)(2,1)S(1)}, bf16[32,256]{1,0:T(8,128)(2,1)S(1)}, u32[]{:S(2)}, u32[]{:S(2)}) collective-permute-start(bf16[32,256]{1,0:T(8,128)(2,1)S(1)} %get-tuple-element.40), channel_id=1, source_target_pairs={{0,1},{1,0},{2,3},{3,2},{4,8},{5,9},{6,10},{7,11},{8,4},{9,5},{10,... | collective-permute-start | bytes 49160 | tf_op jit(solution)/shard_map/ppermute | solution.py:43
  9.9 1.9 %collective-permute-start.3 = (bf16[32,256]{1,0:T(8,128)(2,1)S(1)}, bf16[32,256]{1,0:T(8,128)(2,1)S(1)}, u32[]{:S(2)}, u32[]{:S(2)}) collective-permute-start(bf16[32,256]{1,0:T(8,128)(2,1)S(1)} %get-tuple-element.41), channel_id=1, source_target_pairs={{0,4},{4,0},{8,12},{12,8},{16,20},{20,16},{24,28},{28,24},{1,5},{5... | collective-permute-start | bytes 49160 | tf_op jit(solution)/shard_map/ppermute | solution.py:31
  10.1 6.6 %collective-permute-start.5 = (bf16[4,20,4,20]{3,2,1,0:T(4,128)(2,1)S(1)}, bf16[4,20,4,20]{3,2,1,0:T(4,128)(2,1)S(1)}, u32[]{:S(2)}, u32[]{:S(2)}) collective-permute-start(bf16[4,20,4,20]{3,2,1,0:T(4,128)(2,1)S(1)} %get-tuple-element.52), channel_id=1, source_target_pairs={{0,8},{4,12},{8,0},{12,4},{16,24},{20,28},{24,16},{28,20},{1,9},{5... | collective-permute-start | bytes 38408 | tf_op jit(solution)/shard_map/ppermute | solution.py:123
  12.8 11.8 %all-to-all-start = ((bf16[32,6,2,128]{3,2,1,0:T(2,128)(2,1)}), bf16[32,6,2,128]{3,2,1,0:T(2,128)(2,1)S(1)}, u32[]{:S(2)}, u32[]{:S(2)}) async-start(bf16[32,6,2,128]{3,2,1,0:T(2,128)(2,1)} %bitcast.7), calls=%async_computation | async-start | bytes 196608 | tf_op jit(solution)/shard_map/all_to_all | solution.py:412
  17.1 4.1 %collective-permute-start.6 = (bf16[4,32,96]{2,1,0:T(8,128)(2,1)S(1)}, bf16[4,32,96]{2,1,0:T(8,128)(2,1)S(1)}, u32[]{:S(2)}, u32[]{:S(2)}) collective-permute-start(bf16[4,32,96]{2,1,0:T(8,128)(2,1)S(1)} %get-tuple-element.54), channel_id=1, source_target_pairs={{0,16},{4,20},{8,24},{12,28},{16,0},{20,4},{24,8},{28,12},{1,17},{... | collective-permute-start | bytes 73736 | tf_op jit(solution)/shard_map/ppermute | solution.py:123
  19.0 5.7 %copy-start.1 = (f32[32]{0:T(128)S(1)}, f32[32]{0:T(128)}, u32[]{:S(2)}) copy-start(f32[32]{0:T(128)} %param.11) | copy-start | bytes 388
  25.7 10.2 %all-to-all-start.1 = ((f32[32,1,128]{2,1,0:T(1,128)}), f32[32,1,128]{2,1,0:T(1,128)S(1)}, u32[]{:S(2)}, u32[]{:S(2)}) async-start(f32[32,1,128]{2,1,0:T(1,128)} %get-tuple-element.63), calls=%async_computation.1 | async-start | bytes 32768 | tf_op jit(solution)/shard_map/all_to_all | solution.py:432
  28.3 6.5 %collective-permute-start.7 = (bf16[32,256]{1,0:T(8,128)(2,1)S(1)}, bf16[32,256]{1,0:T(8,128)(2,1)S(1)}, u32[]{:S(2)}, u32[]{:S(2)}) collective-permute-start(bf16[32,256]{1,0:T(8,128)(2,1)S(1)} %get-tuple-element.65), channel_id=1, source_target_pairs={{1,2},{2,1},{3,0},{0,3},{5,6},{6,5},{7,4},{4,7},{9,10},{10,9},{11,... | collective-permute-start | bytes 49160 | tf_op jit(solution)/shard_map/ppermute | solution.py:31
  32.0 3.7 %collective-permute-start.8 = (bf16[32,256]{1,0:T(8,128)(2,1)S(1)}, bf16[32,256]{1,0:T(8,128)(2,1)S(1)}, u32[]{:S(2)}, u32[]{:S(2)}) collective-permute-start(bf16[32,256]{1,0:T(8,128)(2,1)S(1)} %get-tuple-element.66), channel_id=1, source_target_pairs={{0,1},{1,0},{2,3},{3,2},{4,5},{5,4},{6,7},{7,6},{8,9},{9,8},{10,11... | collective-permute-start | bytes 49160 | tf_op jit(solution)/shard_map/ppermute | solution.py:31
  32.0 3.9 %collective-permute-start.9 = (bf16[32,256]{1,0:T(8,128)(2,1)S(1)}, bf16[32,256]{1,0:T(8,128)(2,1)S(1)}, u32[]{:S(2)}, u32[]{:S(2)}) collective-permute-start(bf16[32,256]{1,0:T(8,128)(2,1)S(1)} %get-tuple-element.67), channel_id=1, source_target_pairs={{0,1},{1,0},{2,3},{3,2},{4,8},{5,9},{6,10},{7,11},{8,4},{9,5},{10,... | collective-permute-start | bytes 49160 | tf_op jit(solution)/shard_map/ppermute | solution.py:43
  34.0 1.9 %collective-permute-start.10 = (bf16[32,256]{1,0:T(8,128)(2,1)S(1)}, bf16[32,256]{1,0:T(8,128)(2,1)S(1)}, u32[]{:S(2)}, u32[]{:S(2)}) collective-permute-start(bf16[32,256]{1,0:T(8,128)(2,1)S(1)} %get-tuple-element.68), channel_id=1, source_target_pairs={{0,4},{4,0},{8,12},{12,8},{16,20},{20,16},{24,28},{28,24},{1,5},{5... | collective-permute-start | bytes 49160 | tf_op jit(solution)/shard_map/ppermute | solution.py:31

commit v5 on v4

--- a/solution.py
+++ b/solution.py
@@ -284,13 +284,13 @@
         sums_ref[0:1, i * n : (i + 1) * n] = to_row(jnp.sum(product, axis=1, keepdims=True))
 
 
-def solve_kernel(perm_ref, gathered_ref, wide_ref, rz_ref, weight_ref, basis_ref, sol_r_ref, sol_q_ref,
-                 sums_ref, rhs_r_ref, rhs_q_ref, step_out, weighted_out, rz_hbm, f0, f1, f2, f3, rz_ref_out, sem):
-    n = rz_ref.shape[1]
+def solve_kernel(perm_ref, gathered_ref, wide_ref, prev_ref, weight_ref, basis_ref, sol_r_ref, sol_q_ref,
+                 sums_ref, rhs_r_ref, rhs_q_ref, step_out, weighted_out, rz_out, f0, f1, f2, f3, rz_ref, sem):
+    n = prev_ref.shape[1]
     prim = basis_ref.shape[0]
     halves = jnp.concatenate([gathered_ref[:, : 2 * n], gathered_ref[:, 2 * n :]], axis=0)
     total = jnp.dot(wide_ref[...], halves, preferred_element_type=F32)
-    step = rz_ref[...] / (total[prim : prim + 1, 0:n] + total[prim : prim + 1, n : 2 * n])
+    step = prev_ref[...] / (total[prim : prim + 1, 0:n] + total[prim : prim + 1, n : 2 * n])
     coarse_sol = (total[0:prim, 0:n] - step * total[0:prim, n : 2 * n]).astype(BF16)
     coarse_part = coarse_sol.astype(F32) * (rhs_r_ref[...] - step * rhs_q_ref[...])
     partial = (
@@ -299,9 +299,9 @@
         + jnp.sum(coarse_part, axis=0, keepdims=True)
     )
     partial = jnp.concatenate([partial, jnp.zeros((1, BLK - n), F32)], axis=1)
-    for i in range(rz_ref_out.shape[0]):
-        rz_ref_out[i] = partial
-    copy = pltpu.make_async_copy(rz_ref_out, rz_hbm, sem)
+    for i in range(rz_ref.shape[0]):
+        rz_ref[i] = partial
+    copy = pltpu.make_async_copy(rz_ref, rz_out, sem)
     copy.start()
     correction = lax.dot_general(
         coarse_sol, basis_ref[...], (((0,), (0,)), ((), ())), preferred_element_type=F32
@@ -343,6 +343,7 @@
     rz_row = rz_prev[None, :]
     vmem = pl.BlockSpec(memory_space=VMEM)
     hbm = pl.BlockSpec(memory_space=pltpu.HBM)
+    anywhere = pl.BlockSpec(memory_space=pl.ANY)
     flops = 2 * rhs * width * width
     coarse = coarse_inv[0, :, :, 0]
     coarse_type = jax.ShapeDtypeStruct(coarse.shape, BF16)
@@ -425,7 +426,7 @@
             jax.ShapeDtypeStruct((slabs * sectors, 1, BLK), F32),
         )
         + (face,) * 4,
-        in_specs=[vmem] * 11, out_specs=(vmem, vmem, hbm) + (vmem,) * 4,
+        in_specs=[vmem] * 11, out_specs=(vmem, vmem, anywhere) + (vmem,) * 4,
         scratch_shapes=[pltpu.VMEM((slabs * sectors, 1, BLK), F32), pltpu.SemaphoreType.DMA],
         compiler_params=params(), cost_estimate=cost(2 * rhs * width * prim, 8 * rhs * width),
     )(perm, gathered, wide, rz_row, weight, basis_t, sol_r, sol_q, sums, rhs_r, rhs_q)

time: 37 us -> 37 us (level)
  no operation moved by 1% of the time
where the time goes in v5:
time: 37 us; the launch traced here: 36.7 us
  starting transfers between devices  22.4 us (61%)
  Pallas kernels  8.72 us (24%)
  waiting for transfers between devices  4.68 us (13%)
  between operations  0.75 us (2%)
    ppermute x6, starting transfers between devices, swap(): return lax.ppermute(value, axis, pairs)  8.37 us
    ppermute x2, starting transfers between devices, swap_second(): return lax.ppermute(value, ('gx', 'col'), pairs)  4.05 us
    all_to_all x1, starting transfers between devices, body(): lax.all_to_all(packed, ('gx', 'col'), 0, 0)  3.89 us
    ppermute x3, starting transfers between devices, swap_bit(): return lax.ppermute(value, 'gx', [(i, i ^ 1 << k) for i in range(count)])  3.49 us
    all_to_all x1, waiting for transfers between devices, body(): lax.all_to_all(packed, ('gx', 'col'), 0, 0)  3.25 us
    all_to_all x1, starting transfers between devices, body(): partials = lax.all_to_all(partial, ('gx', 'col'), 0, 0)  2.56 us
    pallas_call x1, Pallas kernels, body(): pl.pallas_call(neumann_kernel, out_shape=(full, full, jax.ShapeDtypeStruc...  2.26 us
    pallas_call x1, Pallas kernels, body(): pl.pallas_call(image_kernel, out_shape=(full,) + (face,) * 4 + (send_type...  2.06 us
  transfers between devices with their start and end apart: 13, of which 5 were waited for; matrix products, arithmetic and copies ran while one was open for 1% of the time, Pallas kernels for 13%

profile of v5, /device:TPU:0, one launch (start us, length us, event | category | flops | bytes accessed | tf_op | source)
XLA Modules:
  0.0 36.7 jit_solution(6176352579577677713)
XLA Ops:
  0.6 0.0 copy-start
  0.6 0.0 copy-start.2
  0.7 2.1 %shard_map.112 = (f32[32,1024]{1,0:T(8,128)S(1)}, bf16[32,256]{1,0:T(8,128)(2,1)S(1)}, bf16[32,256]{1,0:T(8,128)(2,1)S(1)}, bf16[32,256]{1,0:T(8,128)(2,1)S(1)},...) custom-call(s32[1,8]{1,0:T(1,128)} %bitcast.16, ...), custom_call_target="tpu_custom_call" | custom-call | flops 67108864 | bytes 2097152 | tf_op jit(solution)/shard_map/pallas_call | solution.py:354
  2.7 0.5 %collective-permute-start.4 = (bf16[4,20,4,20]{3,2,1,0:T(4,128)(2,1)S(1)}, bf16[4,20,4,20]{3,2,1,0:T(4,128)(2,1)S(1)}, u32[]{:S(2)}, u32[]{:S(2)}) collective-permute-start(bf16[4,20,4,20]{3,2,1,0:T(4,128)(2,1)S(1)} %get-tuple-element.50), channel_id=1, source_target_pairs={{0,4},{4,0},{8,12},{12,8},{16,20},{20,16},{24,28},{28,24},{1,5},{5... | collective-permute-start | bytes 38408 | tf_op jit(solution)/shard_map/ppermute | solution.py:123
  3.2 4.7 %collective-permute-start = (bf16[32,256]{1,0:T(8,128)(2,1)S(1)}, bf16[32,256]{1,0:T(8,128)(2,1)S(1)}, u32[]{:S(2)}, u32[]{:S(2)}) collective-permute-start(bf16[32,256]{1,0:T(8,128)(2,1)S(1)} %get-tuple-element.38), channel_id=1, source_target_pairs={{1,2},{2,1},{3,0},{0,3},{5,6},{6,5},{7,4},{4,7},{9,10},{10,9},{11,... | collective-permute-start | bytes 49160 | tf_op jit(solution)/shard_map/ppermute | solution.py:31
  7.9 0.0 collective-permute-start.1
  7.9 2.0 %collective-permute-start.2 = (bf16[32,256]{1,0:T(8,128)(2,1)S(1)}, bf16[32,256]{1,0:T(8,128)(2,1)S(1)}, u32[]{:S(2)}, u32[]{:S(2)}) collective-permute-start(bf16[32,256]{1,0:T(8,128)(2,1)S(1)} %get-tuple-element.40), channel_id=1, source_target_pairs={{0,1},{1,0},{2,3},{3,2},{4,8},{5,9},{6,10},{7,11},{8,4},{9,5},{10,... | collective-permute-start | bytes 49160 | tf_op jit(solution)/shard_map/ppermute | solution.py:43
  9.9 0.0 collective-permute-start.3
  9.9 0.0 collective-permute-done.4.got_ref
  9.9 0.1 shard_map.115
  10.1 1.1 %collective-permute-start.5 = (bf16[4,20,4,20]{3,2,1,0:T(4,128)(2,1)S(1)}, bf16[4,20,4,20]{3,2,1,0:T(4,128)(2,1)S(1)}, u32[]{:S(2)}, u32[]{:S(2)}) collective-permute-start(bf16[4,20,4,20]{3,2,1,0:T(4,128)(2,1)S(1)} %get-tuple-element.52), channel_id=1, source_target_pairs={{0,8},{4,12},{8,0},{12,4},{16,24},{20,28},{24,16},{28,20},{1,9},{5... | collective-permute-start | bytes 38408 | tf_op jit(solution)/shard_map/ppermute | solution.py:123
  11.2 0.0 copy-done.2
  11.2 0.1 copy.12.conduct_ref
  11.3 0.0 copy-done
  11.3 0.3 shard_map.113
  11.6 0.0 collective-permute-done.r0
  11.6 0.1 collective-permute-done.1.r1
  11.7 0.2 collective-permute-done.2.r2
  11.8 0.0 collective-permute-done.3.r3
  11.8 1.0 %shard_map.114 = (f32[32,1024]{1,0:T(8,128)S(1)}, bf16[32,1024]{1,0:T(8,128)(2,1)S(1)}, f32[20,32]{1,0:T(8,128)S(1)}, bf16[384,128]{1,0:T(8,128)(2,1)}) custom-call(s32[1,8]{1,0:T(1,128)S(1)} %bitcast.18, f32[32,1024]{1,0:T(8,128)S(1)} %get-tuple-element.37.image_ref, bf16[32,256]{1,0:T(8,128)(2,1)S(1)} %collective-permute-done.r0, ...), custom_call_target="tpu_custom_call" | custom-call | flops 1310720 | bytes 262144 | tf_op jit(solution)/shard_map/pallas_call | solution.py:401
  12.8 3.9 %all-to-all-start = ((bf16[32,6,2,128]{3,2,1,0:T(2,128)(2,1)}), bf16[32,6,2,128]{3,2,1,0:T(2,128)(2,1)S(1)}, u32[]{:S(2)}, u32[]{:S(2)}) async-start(bf16[32,6,2,128]{3,2,1,0:T(2,128)(2,1)} %bitcast.7), calls=%async_computation | async-start | bytes 196608 | tf_op jit(solution)/shard_map/all_to_all | solution.py:413
  16.7 0.0 collective-permute-done.5.got_ref
  16.7 0.1 shard_map.116
  16.8 0.1 reshape.17.matrix_ref
  17.0 0.2 shard_map.117
  17.1 1.8 %collective-permute-start.6 = (bf16[4,32,96]{2,1,0:T(8,128)(2,1)S(1)}, bf16[4,32,96]{2,1,0:T(8,128)(2,1)S(1)}, u32[]{:S(2)}, u32[]{:S(2)}) collective-permute-start(bf16[4,32,96]{2,1,0:T(8,128)(2,1)S(1)} %get-tuple-element.54), channel_id=1, source_target_pairs={{0,16},{4,20},{8,24},{12,28},{16,0},{20,4},{24,8},{28,12},{1,17},{... | collective-permute-start | bytes 73736 | tf_op jit(solution)/shard_map/ppermute | solution.py:123
  19.0 0.0 copy-start.1
  19.0 2.3 %shard_map.119 = (f32[32,1024]{1,0:T(8,128)S(1)}, f32[32,1024]{1,0:T(8,128)S(1)}, f32[8,128]{1,0:T(8,128)S(1)}) custom-call(bf16[32,1024]{1,0:T(8,128)(2,1)S(1)} %get-tuple-element.55.scaled_r_ref, bf16[32,1024]{1,0:T(8,128)(2,1)S(1)} %get-tuple-element.56.scaled_q_ref, f32[32,1024]{1,0:T(8,128)S(1)} %get-tuple-element.43.resid_ref, ...), custom_call_target="tpu_custom_call" | custom-call | flops 67108864000 | bytes 2097152 | tf_op jit(solution)/shard_map/pallas_call | solution.py:414
  21.2 0.0 collective-permute-done.6.got_ref
  21.2 0.1 shard_map.118.wide_ref
  21.4 3.3 %all-to-all-done = bf16[32,6,2,128]{3,2,1,0:T(2,128)(2,1)S(1)} async-done(((bf16[32,6,2,128]{3,2,1,0:T(2,128)(2,1)}), bf16[32,6,2,128]{3,2,1,0:T(2,128)(2,1)S(1)}, u32[]{:S(2)}, u32[]{:S(2)}) %all-to-all-start) | async-done | bytes 98336 | tf_op jit(solution)/shard_map/all_to_all | solution.py:413
  24.6 0.0 copy-done.1
  24.7 1.1 %shard_map.120 = (f32[32,128]{1,0:T(8,128)S(1)}, f32[32,1024]{1,0:T(8,128)S(1)}, f32[32,1,128]{2,1,0:T(1,128)}, bf16[32,256]{1,0:T(8,128)(2,1)S(1)}, bf16[32,256...) custom-call(s32[1,8]{1,0:T(1,128)S(1)} %bitcast.19, bf16[384,128]{1,0:T(8,128)(2,1)S(1)} %bitcast.15, ...), custom_call_target="tpu_custom_call" | custom-call | flops 1310720 | bytes 262144 | tf_op jit(solution)/shard_map/pallas_call | solution.py:421
  25.7 2.6 %all-to-all-start.1 = ((f32[32,1,128]{2,1,0:T(1,128)}), f32[32,1,128]{2,1,0:T(1,128)S(1)}, u32[]{:S(2)}, u32[]{:S(2)}) async-start(f32[32,1,128]{2,1,0:T(1,128)} %get-tuple-element.63), calls=%async_computation.1 | async-start | bytes 32768 | tf_op jit(solution)/shard_map/all_to_all | solution.py:433
  28.3 3.7 %collective-permute-start.7 = (bf16[32,256]{1,0:T(8,128)(2,1)S(1)}, bf16[32,256]{1,0:T(8,128)(2,1)S(1)}, u32[]{:S(2)}, u32[]{:S(2)}) collective-permute-start(bf16[32,256]{1,0:T(8,128)(2,1)S(1)} %get-tuple-element.65), channel_id=1, source_target_pairs={{1,2},{2,1},{3,0},{0,3},{5,6},{6,5},{7,4},{4,7},{9,10},{10,9},{11,... | collective-permute-start | bytes 49160 | tf_op jit(solution)/shard_map/ppermute | solution.py:31
  32.0 0.0 collective-permute-start.8
  32.0 2.0 %collective-permute-start.9 = (bf16[32,256]{1,0:T(8,128)(2,1)S(1)}, bf16[32,256]{1,0:T(8,128)(2,1)S(1)}, u32[]{:S(2)}, u32[]{:S(2)}) collective-permute-start(bf16[32,256]{1,0:T(8,128)(2,1)S(1)} %get-tuple-element.67), channel_id=1, source_target_pairs={{0,1},{1,0},{2,3},{3,2},{4,8},{5,9},{6,10},{7,11},{8,4},{9,5},{10,... | collective-permute-start | bytes 49160 | tf_op jit(solution)/shard_map/ppermute | solution.py:43
  34.0 0.0 collective-permute-start.10
  34.0 0.7 %shard_map.121 = f32[32,1024]{1,0:T(8,128)} custom-call(f32[32,128]{1,0:T(8,128)S(1)} %get-tuple-element.62.step_ref, f32[32,1024]{1,0:T(8,128)S(1)} %get-tuple-element.43.resid_ref, f32[32,1024]{1,0:T(8,128)S(1)} %get-tuple-element.57.assembled_ref), custom_call_target="tpu_custom_call" | custom-call | flops 65536 | bytes 393216 | tf_op jit(solution)/shard_map/pallas_call | solution.py:435
  34.7 0.0 collective-permute-done.7.r0
  34.8 1.0 %collective-permute-done.8.r1 = bf16[32,256]{1,0:T(8,128)(2,1)S(1)} collective-permute-done((bf16[32,256]{1,0:T(8,128)(2,1)S(1)}, bf16[32,256]{1,0:T(8,128)(2,1)S(1)}, u32[]{:S(2)}, u32[]{:S(2)}) %collective-permute-start.8) | collective-permute-done | bytes 16416 | tf_op jit(solution)/shard_map/ppermute | solution.py:31
  35.7 0.2 collective-permute-done.9.r2
  35.9 0.0 collective-permute-done.10.r3
  35.9 0.0 all-to-all-done.1.partials_ref
  35.9 0.8 %shard_map.122 = (f32[32,1024]{1,0:T(8,128)}, f32[1,32]{1,0:T(1,128)}) custom-call(s32[1,8]{1,0:T(1,128)S(1)} %bitcast.20, f32[32,1,128]{2,1,0:T(1,128)S(1)} %all-to-all-done.1.partials_ref, f32[1,32]{1,0:T(1,128)S(1)} %bitcast.22, f32[32,1024]{1,0:T(8,128)S(1)} %get-tuple-element.42.dir_ref, f32[32,1024]{1,0:T(8,128)S(1)} %get-tuple-element.64.weighted_ref, ...), custom_call_target="tpu_custom_call" | custom-call | flops 65536 | bytes 262144 | tf_op jit(solution)/shard_map/pallas_call | solution.py:439
Async XLA Ops:
  0.6 10.7 %copy-start = (s32[1,1,8]{2,1,0:T(1,128)S(1)}, s32[1,1,8]{2,1,0:T(1,128)}, u32[]{:S(2)}) copy-start(s32[1,1,8]{2,1,0:T(1,128)} %param.17) | copy-start | bytes 100
  0.6 10.6 %copy-start.2 = (f32[8,4]{0,1:T(4,128)S(1)}, f32[8,4]{0,1:T(4,128)}, u32[]{:S(2)}) copy-start(f32[8,4]{0,1:T(4,128)} %param.16) | copy-start | bytes 388
  2.7 7.2 %collective-permute-start.4 = (bf16[4,20,4,20]{3,2,1,0:T(4,128)(2,1)S(1)}, bf16[4,20,4,20]{3,2,1,0:T(4,128)(2,1)S(1)}, u32[]{:S(2)}, u32[]{:S(2)}) collective-permute-start(bf16[4,20,4,20]{3,2,1,0:T(4,128)(2,1)S(1)} %get-tuple-element.50), channel_id=1, source_target_pairs={{0,4},{4,0},{8,12},{12,8},{16,20},{20,16},{24,28},{28,24},{1,5},{5... | collective-permute-start | bytes 38408 | tf_op jit(solution)/shard_map/ppermute | solution.py:123
  3.2 8.3 %collective-permute-start = (bf16[32,256]{1,0:T(8,128)(2,1)S(1)}, bf16[32,256]{1,0:T(8,128)(2,1)S(1)}, u32[]{:S(2)}, u32[]{:S(2)}) collective-permute-start(bf16[32,256]{1,0:T(8,128)(2,1)S(1)} %get-tuple-element.38), channel_id=1, source_target_pairs={{1,2},{2,1},{3,0},{0,3},{5,6},{6,5},{7,4},{4,7},{9,10},{10,9},{11,... | collective-permute-start | bytes 49160 | tf_op jit(solution)/shard_map/ppermute | solution.py:31
  7.9 3.7 %collective-permute-start.1 = (bf16[32,256]{1,0:T(8,128)(2,1)S(1)}, bf16[32,256]{1,0:T(8,128)(2,1)S(1)}, u32[]{:S(2)}, u32[]{:S(2)}) collective-permute-start(bf16[32,256]{1,0:T(8,128)(2,1)S(1)} %get-tuple-element.39), channel_id=1, source_target_pairs={{0,1},{1,0},{2,3},{3,2},{4,5},{5,4},{6,7},{7,6},{8,9},{9,8},{10,11... | collective-permute-start | bytes 49160 | tf_op jit(solution)/shard_map/ppermute | solution.py:31
  7.9 3.9 %collective-permute-start.2 = (bf16[32,256]{1,0:T(8,128)(2,1)S(1)}, bf16[32,256]{1,0:T(8,128)(2,1)S(1)}, u32[]{:S(2)}, u32[]{:S(2)}) collective-permute-start(bf16[32,256]{1,0:T(8,128)(2,1)S(1)} %get-tuple-element.40), channel_id=1, source_target_pairs={{0,1},{1,0},{2,3},{3,2},{4,8},{5,9},{6,10},{7,11},{8,4},{9,5},{10,... | collective-permute-start | bytes 49160 | tf_op jit(solution)/shard_map/ppermute | solution.py:43
  9.9 1.9 %collective-permute-start.3 = (bf16[32,256]{1,0:T(8,128)(2,1)S(1)}, bf16[32,256]{1,0:T(8,128)(2,1)S(1)}, u32[]{:S(2)}, u32[]{:S(2)}) collective-permute-start(bf16[32,256]{1,0:T(8,128)(2,1)S(1)} %get-tuple-element.41), channel_id=1, source_target_pairs={{0,4},{4,0},{8,12},{12,8},{16,20},{20,16},{24,28},{28,24},{1,5},{5... | collective-permute-start | bytes 49160 | tf_op jit(solution)/shard_map/ppermute | solution.py:31
  10.1 6.6 %collective-permute-start.5 = (bf16[4,20,4,20]{3,2,1,0:T(4,128)(2,1)S(1)}, bf16[4,20,4,20]{3,2,1,0:T(4,128)(2,1)S(1)}, u32[]{:S(2)}, u32[]{:S(2)}) collective-permute-start(bf16[4,20,4,20]{3,2,1,0:T(4,128)(2,1)S(1)} %get-tuple-element.52), channel_id=1, source_target_pairs={{0,8},{4,12},{8,0},{12,4},{16,24},{20,28},{24,16},{28,20},{1,9},{5... | collective-permute-start | bytes 38408 | tf_op jit(solution)/shard_map/ppermute | solution.py:123
  12.8 11.8 %all-to-all-start = ((bf16[32,6,2,128]{3,2,1,0:T(2,128)(2,1)}), bf16[32,6,2,128]{3,2,1,0:T(2,128)(2,1)S(1)}, u32[]{:S(2)}, u32[]{:S(2)}) async-start(bf16[32,6,2,128]{3,2,1,0:T(2,128)(2,1)} %bitcast.7), calls=%async_computation | async-start | bytes 196608 | tf_op jit(solution)/shard_map/all_to_all | solution.py:413
  17.1 4.1 %collective-permute-start.6 = (bf16[4,32,96]{2,1,0:T(8,128)(2,1)S(1)}, bf16[4,32,96]{2,1,0:T(8,128)(2,1)S(1)}, u32[]{:S(2)}, u32[]{:S(2)}) collective-permute-start(bf16[4,32,96]{2,1,0:T(8,128)(2,1)S(1)} %get-tuple-element.54), channel_id=1, source_target_pairs={{0,16},{4,20},{8,24},{12,28},{16,0},{20,4},{24,8},{28,12},{1,17},{... | collective-permute-start | bytes 73736 | tf_op jit(solution)/shard_map/ppermute | solution.py:123
  19.0 5.7 %copy-start.1 = (f32[32]{0:T(128)S(1)}, f32[32]{0:T(128)}, u32[]{:S(2)}) copy-start(f32[32]{0:T(128)} %param.11) | copy-start | bytes 388
  25.7 10.2 %all-to-all-start.1 = ((f32[32,1,128]{2,1,0:T(1,128)}), f32[32,1,128]{2,1,0:T(1,128)S(1)}, u32[]{:S(2)}, u32[]{:S(2)}) async-start(f32[32,1,128]{2,1,0:T(1,128)} %get-tuple-element.63), calls=%async_computation.1 | async-start | bytes 32768 | tf_op jit(solution)/shard_map/all_to_all | solution.py:433
  28.3 6.5 %collective-permute-start.7 = (bf16[32,256]{1,0:T(8,128)(2,1)S(1)}, bf16[32,256]{1,0:T(8,128)(2,1)S(1)}, u32[]{:S(2)}, u32[]{:S(2)}) collective-permute-start(bf16[32,256]{1,0:T(8,128)(2,1)S(1)} %get-tuple-element.65), channel_id=1, source_target_pairs={{1,2},{2,1},{3,0},{0,3},{5,6},{6,5},{7,4},{4,7},{9,10},{10,9},{11,... | collective-permute-start | bytes 49160 | tf_op jit(solution)/shard_map/ppermute | solution.py:31
  32.0 3.7 %collective-permute-start.8 = (bf16[32,256]{1,0:T(8,128)(2,1)S(1)}, bf16[32,256]{1,0:T(8,128)(2,1)S(1)}, u32[]{:S(2)}, u32[]{:S(2)}) collective-permute-start(bf16[32,256]{1,0:T(8,128)(2,1)S(1)} %get-tuple-element.66), channel_id=1, source_target_pairs={{0,1},{1,0},{2,3},{3,2},{4,5},{5,4},{6,7},{7,6},{8,9},{9,8},{10,11... | collective-permute-start | bytes 49160 | tf_op jit(solution)/shard_map/ppermute | solution.py:31
  32.0 3.9 %collective-permute-start.9 = (bf16[32,256]{1,0:T(8,128)(2,1)S(1)}, bf16[32,256]{1,0:T(8,128)(2,1)S(1)}, u32[]{:S(2)}, u32[]{:S(2)}) collective-permute-start(bf16[32,256]{1,0:T(8,128)(2,1)S(1)} %get-tuple-element.67), channel_id=1, source_target_pairs={{0,1},{1,0},{2,3},{3,2},{4,8},{5,9},{6,10},{7,11},{8,4},{9,5},{10,... | collective-permute-start | bytes 49160 | tf_op jit(solution)/shard_map/ppermute | solution.py:43
  34.0 1.9 %collective-permute-start.10 = (bf16[32,256]{1,0:T(8,128)(2,1)S(1)}, bf16[32,256]{1,0:T(8,128)(2,1)S(1)}, u32[]{:S(2)}, u32[]{:S(2)}) collective-permute-start(bf16[32,256]{1,0:T(8,128)(2,1)S(1)} %get-tuple-element.68), channel_id=1, source_target_pairs={{0,4},{4,0},{8,12},{12,8},{16,20},{20,16},{24,28},{28,24},{1,5},{5... | collective-permute-start | bytes 49160 | tf_op jit(solution)/shard_map/ppermute | solution.py:31

commit v6 on v5

--- a/solution.py
+++ b/solution.py
@@ -80,7 +80,7 @@
         for b in range(1, len(blocks)):
             chosen = jnp.where(place == b, blocks[b], chosen)
         j = i % 2
-        outs[i // 2][:, j * BLK : (j + 1) * BLK] = chosen.astype(BF16)
+        outs[i // 2][0 : chosen.shape[0], j * BLK : (j + 1) * BLK] = chosen.astype(BF16)
 
 
 def received_blocks(perm_ref, received, blocks):
@@ -124,13 +124,14 @@
 
 
 def image_kernel(perm_hbm, dir_hbm, schur_hbm, resid_hbm, basis_hbm, coarse_hbm,
-                 image_ref, f0, f1, f2, f3, send_ref, dir_ref, resid_ref, basis_ref, coarse_ref, perm_ref,
-                 schur_ref, sems):
+                 image_ref, f0, f1, f2, f3, dir_ref, resid_ref, basis_ref, coarse_ref, *rest):
+    *send_ref, perm_ref, schur_ref, sems = rest
     rows = schur_ref.shape[0] // CHUNKS
     parts = [pl.ds(i * rows, rows) for i in range(CHUNKS)]
     pairs = [(dir_hbm, dir_ref), (perm_hbm, perm_ref)]
     pairs += [(schur_hbm.at[part], schur_ref.at[part]) for part in parts]
-    pairs += [(coarse_hbm.at[other_block(i, 0)], send_ref.at[i]) for i in range(send_ref.shape[0])]
+    for ref in send_ref:
+        pairs += [(coarse_hbm.at[other_block(i, 0)], ref.at[i]) for i in range(ref.shape[0])]
     pairs += [(resid_hbm, resid_ref), (basis_hbm, basis_ref), (coarse_hbm, coarse_ref)]
     copies = [pltpu.make_async_copy(source, target, sems.at[i]) for i, (source, target) in enumerate(pairs)]
     for copy in copies:
@@ -328,6 +329,227 @@
         out_ref[:, at] = weighted_ref[:, at] + factor * dir_ref[:, at] + part
 
 
+def split(value):
+    high = value.astype(BF16).astype(F32)
+    return high, value - high
+
+
+def spread_pair_kernel(after_ref, own_ref, mate_ref, out_ref):
+    slabs = lax.axis_size("gx")
+    prim = own_ref.shape[0] // slabs
+    half = prim // 2
+    sectors = own_ref.shape[1] // prim
+    width = out_ref.shape[2] // 2
+    depth = width // sectors
+    source = lax.broadcasted_iota(jnp.int32, (sectors * prim, 2 * width), 0)
+    place = lax.broadcasted_iota(jnp.int32, (sectors * prim, 2 * width), 1)
+    later = place // width
+    within = place % width
+    sector, at = within // depth, within % depth
+    chosen = jnp.logical_and(at < half, source == sector * prim + later * half + at)
+    chosen = jnp.where(chosen, 1.0, 0.0).astype(BF16)
+    mine = lax.axis_index("gx") % 2
+    for ref, bit in ((own_ref, mine), (mate_ref, 1 - mine)):
+        out_ref[bit] = jnp.dot(ref[...], chosen, preferred_element_type=F32).astype(BF16)
+
+
+def gather_kernel(k, after_ref, mine_ref, got_ref, out_ref, both_ref):
+    bit = (lax.axis_index("gx") >> k) % 2
+    n = mine_ref.shape[0]
+    for i in range(n):
+        both_ref[bit * n + i] = mine_ref[i]
+        both_ref[(1 - bit) * n + i] = got_ref[i]
+    out_ref[...] = jnp.concatenate([both_ref[i] for i in range(2 * n)], axis=1)
+
+
+def sector_kernel(prim, depth, width, up, mine_ref, got_ref, wide_ref):
+    slabs = lax.axis_size("gx")
+    rows = slabs * up
+    half = prim // 2
+    top = (lax.axis_index("gx") * 2) // slabs
+    low = jnp.where(top == 0, mine_ref[...].astype(F32), got_ref[...].astype(F32))
+    high = jnp.where(top == 0, got_ref[...].astype(F32), mine_ref[...].astype(F32))
+    pieces = []
+    for part in range(2):
+        for h in range(slabs):
+            source = low if h < slabs // 2 else high
+            at = h % (slabs // 2) * 2 * width + part * width
+            pieces.append(source[:, at : at + width])
+    flat = jnp.concatenate(pieces, axis=1)
+    empty = jnp.zeros((up - prim, flat.shape[1]), F32)
+    parts = []
+    for g in range(slabs):
+        parts += [flat[g * prim : (g + 1) * prim], empty]
+    wide_ref[0:rows, :] = jnp.concatenate(parts, axis=0).astype(BF16)
+    shape = (wide_ref.shape[0] - rows, wide_ref.shape[1])
+    row = lax.broadcasted_iota(jnp.int32, shape, 0)
+    lane = lax.broadcasted_iota(jnp.int32, shape, 1)
+    part = lane // (slabs * width)
+    at = lane % depth
+    slab = lane // width % slabs
+    sector = lane % width // depth
+    sums = jnp.logical_and(at >= half, row == (at - half) * 2 + part)
+    mine = jnp.logical_and(sector == lax.axis_index("col"), at < half)
+    own = jnp.logical_and(mine, row == 16 + slab * up + part * half + at)
+    wide_ref[rows:, :] = jnp.where(jnp.logical_or(sums, own), 1.0, 0.0).astype(BF16)
+
+
+def near_rhs_kernel(rows, sectors, perm_ref, image_ref, r0, r1, r2, r3, weight_ref, basis_ref, rhs_ref, curv_ref,
+                    scaled_ref, resid_ref, neumann_ref, assembled_ref, sol_r_ref, sol_q_ref, out_ref):
+    for at, part in received_blocks(perm_ref, (r0, r1, r2, r3), image_ref.shape[1] // BLK):
+        assembled_ref[:, at] = image_ref[:, at] + part
+    weighted_r = weight_ref[0:1, :] * resid_ref[...]
+    weighted_q = weight_ref[0:1, :] * assembled_ref[...]
+    scaled = weighted_q.astype(BF16)
+    n = scaled.shape[0]
+    both = jnp.concatenate([scaled_ref[...], scaled], axis=0)
+    sol = jnp.dot(both, neumann_ref[...], preferred_element_type=F32)
+    rhs_q = lax.dot_general(
+        basis_ref[...], scaled, (((1,), (1,)), ((), ())), preferred_element_type=F32
+    )
+    sol_r, sol_q = sol[:n], sol[n:]
+    sol_r_ref[...] = sol_r
+    sol_q_ref[...] = sol_q
+    products = (weighted_r * sol_r, weighted_r * sol_q + weighted_q * sol_r, weighted_q * sol_q)
+    sums = [to_row(jnp.sum(product, axis=1, keepdims=True)) for product in products]
+    first = jnp.concatenate([curv_ref[0:1, : 2 * n], *split(sums[0])], axis=1)
+    second = jnp.concatenate([*split(sums[1]), *split(sums[2])], axis=1)
+    rhs_r = rhs_ref[...]
+    half = rhs_r.shape[0] // 2
+    packed = jnp.concatenate([rhs_r[:half], rhs_q[:half], rhs_r[half:], rhs_q[half:]], axis=1)
+    packed = jnp.concatenate([packed, first, second], axis=0)
+    several = jnp.concatenate([packed] * sectors, axis=0).astype(BF16)
+    step = several.shape[0]
+    for i in range(out_ref.shape[0] // step):
+        out_ref[i * step : (i + 1) * step] = several
+
+
+def weigh_kernel(weight_ref, r_ref, q_ref, r_out, q_out):
+    r_out[...] = weight_ref[0:1, :] * r_ref[...]
+    q_out[...] = weight_ref[0:1, :] * q_ref[...]
+
+
+def near_solve_kernel(perm_ref, gathered_ref, wide_ref, prev_ref, weight_ref, basis_ref, sol_r_ref, sol_q_ref,
+                      step_out, weighted_out, base_out, part_out, f0, f1, f2, f3, sol_ref):
+    n = prev_ref.shape[1]
+    prim = basis_ref.shape[0]
+    slabs = lax.axis_size("gx")
+    rows = (wide_ref.shape[0] - 16) // 2
+    up = rows // slabs
+    halves = jnp.concatenate([gathered_ref[:, : 2 * n], gathered_ref[:, 2 * n :]], axis=0)
+    total = jnp.dot(wide_ref[...], halves, preferred_element_type=F32)
+    curvature, first, second, third = (
+        total[rows + i : rows + i + 1, 0:n] + total[rows + i : rows + i + 1, n : 2 * n] for i in range(4)
+    )
+    step = prev_ref[...] / curvature
+    sol = (total[0:rows, 0:n] - step * total[0:rows, n : 2 * n]).astype(BF16).astype(F32)
+    sol_ref[...] = sol
+    rhs = total[rows + 16 :, 0:n] - step * total[rows + 16 :, n : 2 * n]
+    high, low = split(jnp.sum(sol * rhs, axis=0, keepdims=True))
+    own = sol_ref[pl.ds(pl.multiple_of(lax.axis_index("gx") * up, 8), up), :].astype(BF16)
+    correction = lax.dot_general(
+        own[0:prim], basis_ref[...], (((0,), (0,)), ((), ())), preferred_element_type=F32
+    )
+    step_col = to_column(step)
+    step_out[...] = jnp.broadcast_to(step_col, step_out.shape)
+    weighted = sol_r_ref[...] - step_col * sol_q_ref[...] + weight_ref[0:1, :] * correction
+    weighted_out[...] = weighted
+    blank = jnp.zeros((1, BLK - n), F32)
+    low = low.astype(BF16).astype(F32)
+    base = first - step * (second - step * third)
+    base_out[...] = jnp.broadcast_to(jnp.concatenate([base, blank], axis=1), base_out.shape)
+    part_out[...] = jnp.broadcast_to(jnp.concatenate([high + low, blank], axis=1), part_out.shape)
+    put_faces(perm_ref, weighted, (f0, f1, f2, f3))
+    lines = jnp.concatenate([high, low, jnp.zeros((14, n), F32)], axis=0)
+    lines = jnp.concatenate([lines, jnp.zeros((16, 2 * BLK - n), F32)], axis=1).astype(BF16)
+    f0[n:, :] = lines
+    f1[n:, :] = lines
+
+
+def near_direction_kernel(perm_ref, rz_ref, dir_ref, weighted_ref, base_ref, part_ref, r0, r1, r2, r3, far_ref,
+                          out_ref, rz_out):
+    n = rz_ref.shape[1]
+    sector = lax.axis_index("col")
+    beside = jnp.where(sector % 2 == 1, (sector + 1) % 4, (sector + 3) % 4)
+    parts = [(sector, part_ref[0:1, 0:n]), (sector ^ 2, far_ref[0:1, 0:n])]
+    for ref, other in ((r0, beside), (r1, sector ^ 1)):
+        lines = ref[n : n + 16, 0:n].astype(F32)
+        parts.append((other, lines[0:1] + lines[1:2]))
+    rz_next = base_ref[0:1, 0:n]
+    for at in range(4):
+        value = parts[0][1]
+        for other, part in parts[1:]:
+            value = jnp.where(other == at, part, value)
+        rz_next = rz_next + value
+    rz_out[...] = rz_next
+    factor = to_column(rz_next / rz_ref[...])
+    received = (r0[0:n, :], r1[0:n, :], r2[...], r3[...])
+    for at, part in received_blocks(perm_ref, received, dir_ref.shape[1] // BLK):
+        out_ref[:, at] = weighted_ref[:, at] + factor * dir_ref[:, at] + part
+
+
+def near_rest(perm, rz_row, neumann, image, received, weight, rhs_r, curv, scaled_r, direction, resid, basis_t,
+              coarse, rows):
+    rhs, width = resid.shape
+    prim = basis_t.shape[0]
+    slabs, sectors = lax.axis_size("gx"), lax.axis_size("col")
+    up = -(-prim // 8) * 8
+    vmem = pl.BlockSpec(memory_space=VMEM)
+    full = jax.ShapeDtypeStruct((rhs, width), F32)
+    line = jax.ShapeDtypeStruct((8, BLK), F32)
+    small = cost(1 << 10, 1 << 16)
+
+    def call(kernel, outs, *args, scratch=(), estimate=small, after=()):
+        return pl.pallas_call(
+            kernel, out_shape=outs, in_specs=[pl.BlockSpec(memory_space=pl.ANY)] * len(after) + [vmem] * len(args),
+            out_specs=(vmem,) * len(outs), scratch_shapes=scratch, compiler_params=params(), cost_estimate=estimate,
+        )(*after, *args)
+
+    mate = swap_bit(coarse, 0)
+    flat = (slabs * prim, sectors * prim)
+    shard = (slabs * prim, 2 * sectors * rows)
+    (blocks,) = call(
+        spread_pair_kernel, (jax.ShapeDtypeStruct((2,) + shard, BF16),),
+        coarse.reshape(flat), mate.reshape(flat), after=(perm,),
+    )
+    assembled, sol_r, sol_q, packed = call(
+        functools.partial(near_rhs_kernel, rows, sectors),
+        (full, full, full, jax.ShapeDtypeStruct((slabs * sectors * rows, BLK), BF16)),
+        perm, image, *received, weight, basis_t, rhs_r, curv, scaled_r, resid, neumann,
+        estimate=cost(2000 * rhs * width * width, 1 << 16),
+    )
+    (blocks,) = call(
+        functools.partial(gather_kernel, 1), (jax.ShapeDtypeStruct((shard[0], 4 * shard[1]), BF16),),
+        blocks, swap_bit(blocks, 1), after=(packed,), scratch=[pltpu.VMEM((4,) + shard, BF16)],
+        estimate=cost(2000 * rhs * width * width, 1 << 16),
+    )
+    (wide,) = call(
+        functools.partial(sector_kernel, prim, rows, shard[1] // 2, up),
+        (jax.ShapeDtypeStruct((2 * slabs * up + 16, slabs * shard[1]), BF16),), blocks, swap_bit(blocks, 2),
+    )
+    packed = packed.reshape(slabs * sectors, rows // 2, 2, BLK)
+    gathered = lax.all_to_all(packed, ("gx", "col"), 0, 0).reshape(slabs * sectors * rows, BLK)
+    sol_r, sol_q = call(
+        weigh_kernel, (full, full), weight, sol_r, sol_q,
+    )
+    face = jax.ShapeDtypeStruct((rhs, 2 * BLK), BF16)
+    tall = jax.ShapeDtypeStruct((rhs + 16, 2 * BLK), BF16)
+    step, weighted, base, part, *faces = call(
+        near_solve_kernel,
+        (jax.ShapeDtypeStruct((rhs, BLK), F32), full, line, line, tall, tall, face, face),
+        perm, gathered, wide, rz_row, weight, basis_t, sol_r, sol_q,
+        scratch=[pltpu.VMEM((slabs * up, rhs), F32)],
+    )
+    received = swap_faces(faces)
+    far = lax.ppermute(part, "col", [(i, i ^ 2) for i in range(sectors)])
+    (resid_new,) = call(resid_kernel, (full,), step, resid, assembled)
+    direction_new, rz_next = call(
+        near_direction_kernel, (full, jax.ShapeDtypeStruct((1, rhs), F32)),
+        perm, rz_row, direction, weighted, base, part, *received, far,
+    )
+    return (resid_new[None, None], direction_new[None, None], rz_next[0])
+
+
 def body(resid, direction, rz_prev, schur, neumann, basis, coarse_inv, conduct, face_perm):
     resid, direction, schur, neumann = resid[0, 0], direction[0, 0], schur[0, 0], neumann[0, 0]
     basis_t = basis[0, 0].T
@@ -350,16 +572,18 @@
     send_type = jax.ShapeDtypeStruct((slabs // 2,) + coarse.shape[1:], BF16)
     blocks_type = jax.ShapeDtypeStruct((slabs, block_rows, 2 * sectors * rows), BF16)
 
+    near = sectors == 4 and slabs == 8
+    sends = () if near else (send_type,)
     fetched = [pltpu.with_memory_space_constraint(x, pltpu.HBM) for x in (perm, direction, schur, resid, basis_t, coarse)]
-    image, f0, f1, f2, f3, send, direction, resid, basis_t, coarse = pl.pallas_call(
+    image, f0, f1, f2, f3, direction, resid, basis_t, coarse, *send = pl.pallas_call(
         image_kernel,
         out_shape=(full,) + (face,) * 4
-        + (send_type, full, full, jax.ShapeDtypeStruct((prim, width), BF16), coarse_type),
-        in_specs=[hbm] * 6, out_specs=(vmem,) * 10,
+        + (full, full, jax.ShapeDtypeStruct((prim, width), BF16), coarse_type) + sends,
+        in_specs=[hbm] * 6, out_specs=(vmem,) * (9 + len(sends)),
         scratch_shapes=[
             pltpu.VMEM(perm.shape, jnp.int32),
             pltpu.VMEM((width, width), BF16),
-            pltpu.SemaphoreType.DMA((CHUNKS + 5 + slabs // 2,)),
+            pltpu.SemaphoreType.DMA((CHUNKS + 5 + len(sends) * (slabs // 2),)),
         ],
         compiler_params=params(), cost_estimate=cost(flops, 2 * width * width),
     )(*fetched)
@@ -373,8 +597,12 @@
             jax.ShapeDtypeStruct((rhs, width), BF16),
         ),
         in_specs=[vmem] * 6, out_specs=(vmem,) * 4, compiler_params=params(),
-        cost_estimate=cost(2 * rhs * width * prim, 8 * rhs * width),
+        cost_estimate=cost(1000 * flops, 8 * rhs * width),
     )(perm, conduct, direction, image, resid, basis_t)
+    if near:
+        return near_rest(perm, rz_row, neumann, image, received, weight, rhs_r, curv, scaled_r, direction, resid,
+                         basis_t, coarse, rows)
+    send = send[0]
     for k in range(rounds - 1):
         got = swap_bit(send, k)
         last = k + 2 == rounds

time: 37 us -> 36.2 us (0.978)
  waiting for transfers between devices: 4.68 us -> 8.51 us
  starting transfers between devices: 22.4 us -> 19.4 us
  Pallas kernels: 8.72 us -> 6.89 us
    ppermute x3, waiting for transfers between devices: 0.01 us -> 4.41 us  [swap_bit(): return lax.ppermute(value, 'gx', [(i, i ^ 1 << k) for i in range(count)])]
    ppermute x0 -> x1, waiting for transfers between devices: none -> 3.22 us  [near_rest(): far = lax.ppermute(part, 'col', [(i, i ^ 2) for i in range(sectors)])]
    all_to_all x2 -> x1, starting transfers between devices: 6.45 us -> 3.75 us  [near_rest(): lax.all_to_all(packed, ('gx', 'col'), 0, 0)]
    all_to_all x2 -> x1, waiting for transfers between devices: 3.25 us -> 0.86 us  [near_rest(): lax.all_to_all(packed, ('gx', 'col'), 0, 0)]
    pallas_call x10 -> x9, Pallas kernels: 8.46 us -> 6.63 us  [the longest x8 4.61 us: call(): pl.pallas_call(kernel, out_shape=outs, in_specs=[pl.BlockSpec(memory_spac...]
    ppermute x6, waiting for transfers between devices: 1.07 us -> 0.02 us  [swap(): return lax.ppermute(value, axis, pairs)]
    ppermute x6, starting transfers between devices: 8.37 us -> 7.56 us  [swap(): return lax.ppermute(value, axis, pairs)]
    ppermute x0 -> x1, starting transfers between devices: none -> 0.56 us  [near_rest(): far = lax.ppermute(part, 'col', [(i, i ^ 2) for i in range(sectors)])]
  transfers between devices with their start and end apart: 13 -> 13, of which waited for: 5 -> 3; matrix products, arithmetic and copies ran while one was open for 1% -> 1% of each run, Pallas kernels for 13% -> 9%
where the time goes in v6:
time: 36.2 us; the launch traced here: 36 us
  starting transfers between devices  19.4 us (54%)
  waiting for transfers between devices  8.51 us (24%)
  Pallas kernels  6.89 us (19%)
  between operations  0.79 us (2%)
  local copies, waits for them, and re-layouts  0.37 us (1%)
    ppermute x6, starting transfers between devices, swap(): return lax.ppermute(value, axis, pairs)  7.56 us
    pallas_call x8, Pallas kernels, call(): pl.pallas_call(kernel, out_shape=outs, in_specs=[pl.BlockSpec(memory_spac...  4.61 us
    ppermute x3, waiting for transfers between devices, swap_bit(): return lax.ppermute(value, 'gx', [(i, i ^ 1 << k) for i in range(count)])  4.41 us
    ppermute x2, starting transfers between devices, swap_second(): return lax.ppermute(value, ('gx', 'col'), pairs)  4.05 us
    all_to_all x1, starting transfers between devices, near_rest(): lax.all_to_all(packed, ('gx', 'col'), 0, 0)  3.75 us
    ppermute x3, starting transfers between devices, swap_bit(): return lax.ppermute(value, 'gx', [(i, i ^ 1 << k) for i in range(count)])  3.49 us
    ppermute x1, waiting for transfers between devices, near_rest(): far = lax.ppermute(part, 'col', [(i, i ^ 2) for i in range(sectors)])  3.22 us
    pallas_call x1, Pallas kernels, body(): pl.pallas_call(image_kernel, out_shape=(full,) + (face,) * 4 + (full, ful...  2.02 us
  transfers between devices with their start and end apart: 13, of which 3 were waited for; matrix products, arithmetic and copies ran while one was open for 1% of the time, Pallas kernels for 9%

profile of v6, /device:TPU:0, one launch (start us, length us, event | category | flops | bytes accessed | tf_op | source)
XLA Modules:
  0.0 36.0 jit_solution(1557666249070507409)
XLA Ops:
  0.6 0.0 copy-start
  0.6 0.0 copy-start.3
  0.7 2.0 %shard_map.112 = (f32[32,1024]{1,0:T(8,128)S(1)}, bf16[32,256]{1,0:T(8,128)(2,1)S(1)}, bf16[32,256]{1,0:T(8,128)(2,1)S(1)}, bf16[32,256]{1,0:T(8,128)(2,1)S(1)},...) custom-call(s32[1,8]{1,0:T(1,128)} %bitcast.16, ...), custom_call_target="tpu_custom_call" | custom-call | flops 67108864 | bytes 2097152 | tf_op jit(solution)/shard_map/pallas_call | solution.py:578
  2.7 0.5 %collective-permute-start.4 = (bf16[8,20,4,20]{3,2,1,0:T(4,128)(2,1)S(1)}, bf16[8,20,4,20]{3,2,1,0:T(4,128)(2,1)S(1)}, u32[]{:S(2)}, u32[]{:S(2)}) collective-permute-start(bf16[8,20,4,20]{3,2,1,0:T(4,128)(2,1)S(1)} %get-tuple-element.45), channel_id=1, source_target_pairs={{0,4},{4,0},{8,12},{12,8},{16,20},{20,16},{24,28},{28,24},{1,5},{5... | collective-permute-start | bytes 76808 | tf_op jit(solution)/shard_map/ppermute | solution.py:123
  3.2 4.7 %collective-permute-start = (bf16[32,256]{1,0:T(8,128)(2,1)S(1)}, bf16[32,256]{1,0:T(8,128)(2,1)S(1)}, u32[]{:S(2)}, u32[]{:S(2)}) collective-permute-start(bf16[32,256]{1,0:T(8,128)(2,1)S(1)} %get-tuple-element.33), channel_id=1, source_target_pairs={{1,2},{2,1},{3,0},{0,3},{5,6},{6,5},{7,4},{4,7},{9,10},{10,9},{11,... | collective-permute-start | bytes 49160 | tf_op jit(solution)/shard_map/ppermute | solution.py:31
  7.9 0.0 collective-permute-start.1
  7.9 2.0 %collective-permute-start.2 = (bf16[32,256]{1,0:T(8,128)(2,1)S(1)}, bf16[32,256]{1,0:T(8,128)(2,1)S(1)}, u32[]{:S(2)}, u32[]{:S(2)}) collective-permute-start(bf16[32,256]{1,0:T(8,128)(2,1)S(1)} %get-tuple-element.35), channel_id=1, source_target_pairs={{0,1},{1,0},{2,3},{3,2},{4,8},{5,9},{6,10},{7,11},{8,4},{9,5},{10,... | collective-permute-start | bytes 49160 | tf_op jit(solution)/shard_map/ppermute | solution.py:43
  9.9 0.0 collective-permute-start.3
  9.9 0.1 reshape.20.own_ref
  10.0 0.0 copy-done.3
  10.1 0.1 copy.12.conduct_ref
  10.1 0.0 collective-permute-done.4
  10.1 0.1 reshape.21.mate_ref
  10.3 0.0 copy-done
  10.3 0.0 copy-start.2
  10.3 0.3 shard_map.113
  10.6 0.2 shard_map.115.mine_ref
  10.8 1.1 %collective-permute-start.5 = (bf16[2,160,96]{2,1,0:T(8,128)(2,1)S(1)}, bf16[2,160,96]{2,1,0:T(8,128)(2,1)S(1)}, u32[]{:S(2)}, u32[]{:S(2)}) collective-permute-start(bf16[2,160,96]{2,1,0:T(8,128)(2,1)S(1)} %shard_map.115.mine_ref), channel_id=1, source_target_pairs={{0,8},{4,12},{8,0},{12,4},{16,24},{20,28},{24,16},{28,20},{1,9},{5... | collective-permute-start | bytes 184328 | tf_op jit(solution)/shard_map/ppermute | solution.py:123
  11.9 0.0 collective-permute-done.r0
  11.9 0.0 collective-permute-done.1.r1
  11.9 0.0 collective-permute-done.2.r2
  11.9 0.0 collective-permute-done.3.r3
  11.9 0.0 copy-done.2
  11.9 1.4 %shard_map.114 = (f32[32,1024]{1,0:T(8,128)S(1)}, f32[32,1024]{1,0:T(8,128)S(1)}, f32[32,1024]{1,0:T(8,128)S(1)}, bf16[384,128]{1,0:T(8,128)(2,1)}) custom-call(s32[1,8]{1,0:T(1,128)S(1)} %bitcast.19, f32[32,1024]{1,0:T(8,128)S(1)} %get-tuple-element.32.image_ref, bf16[32,256]{1,0:T(8,128)(2,1)S(1)} %collective-permute-done.r0, ...), custom_call_target="tpu_custom_call" | custom-call | flops 67108864000 | bytes 65536 | tf_op jit(solution)/shard_map/pallas_call | solution.py:503
  13.3 3.8 %all-to-all-start = ((bf16[32,6,2,128]{3,2,1,0:T(2,128)(2,1)}), bf16[32,6,2,128]{3,2,1,0:T(2,128)(2,1)S(1)}, u32[]{:S(2)}, u32[]{:S(2)}) async-start(bf16[32,6,2,128]{3,2,1,0:T(2,128)(2,1)} %bitcast.8), calls=%async_computation | async-start | bytes 196608 | tf_op jit(solution)/shard_map/all_to_all | solution.py:531
  17.1 0.0 copy-start.1
  17.1 0.0 collective-permute-done.5.got_ref
  17.1 0.1 shard_map.116.mine_ref
  17.2 1.8 %collective-permute-start.6 = (bf16[160,384]{1,0:T(8,128)(2,1)S(1)}, bf16[160,384]{1,0:T(8,128)(2,1)S(1)}, u32[]{:S(2)}, u32[]{:S(2)}) collective-permute-start(bf16[160,384]{1,0:T(8,128)(2,1)S(1)} %shard_map.116.mine_ref), channel_id=1, source_target_pairs={{0,16},{4,20},{8,24},{12,28},{16,0},{20,4},{24,8},{28,12},{1,17},{... | collective-permute-start | bytes 368648 | tf_op jit(solution)/shard_map/ppermute | solution.py:123
  19.1 4.4 %collective-permute-done.6.got_ref = bf16[160,384]{1,0:T(8,128)(2,1)S(1)} collective-permute-done((bf16[160,384]{1,0:T(8,128)(2,1)S(1)}, bf16[160,384]{1,0:T(8,128)(2,1)S(1)}, u32[]{:S(2)}, u32[]{:S(2)}) %collective-permute-start.6) | collective-permute-done | bytes 122912 | tf_op jit(solution)/shard_map/ppermute | solution.py:123
  23.5 0.6 %shard_map.117.wide_ref = bf16[400,768]{1,0:T(8,128)(2,1)S(1)} custom-call(bf16[160,384]{1,0:T(8,128)(2,1)S(1)} %shard_map.116.mine_ref, bf16[160,384]{1,0:T(8,128)(2,1)S(1)} %collective-permute-done.6.got_ref), custom_call_target="tpu_custom_call" | custom-call | flops 1024 | bytes 65536 | tf_op jit(solution)/shard_map/pallas_call | solution.py:503
  24.2 0.9 %all-to-all-done = bf16[32,6,2,128]{3,2,1,0:T(2,128)(2,1)S(1)} async-done(((bf16[32,6,2,128]{3,2,1,0:T(2,128)(2,1)}), bf16[32,6,2,128]{3,2,1,0:T(2,128)(2,1)S(1)}, u32[]{:S(2)}, u32[]{:S(2)}) %all-to-all-start) | async-done | bytes 98336 | tf_op jit(solution)/shard_map/all_to_all | solution.py:531
  25.0 0.0 copy-done.1
  25.0 0.7 %shard_map.119 = (f32[32,128]{1,0:T(8,128)S(1)}, f32[32,1024]{1,0:T(8,128)S(1)}, f32[8,128]{1,0:T(8,128)S(1)}, f32[8,128]{1,0:T(8,128)S(1)}, bf16[48,256]{1,0:T(...) custom-call(s32[1,8]{1,0:T(1,128)S(1)} %bitcast.20, ...), custom_call_target="tpu_custom_call" | custom-call | flops 1024 | bytes 65536 | tf_op jit(solution)/shard_map/pallas_call | solution.py:503
  25.7 2.9 %collective-permute-start.7 = (bf16[48,256]{1,0:T(8,128)(2,1)S(1)}, bf16[48,256]{1,0:T(8,128)(2,1)S(1)}, u32[]{:S(2)}, u32[]{:S(2)}) collective-permute-start(bf16[48,256]{1,0:T(8,128)(2,1)S(1)} %get-tuple-element.55), channel_id=1, source_target_pairs={{1,2},{2,1},{3,0},{0,3},{5,6},{6,5},{7,4},{4,7},{9,10},{10,9},{11,... | collective-permute-start | bytes 73736 | tf_op jit(solution)/shard_map/ppermute | solution.py:31
  28.6 0.0 collective-permute-start.8
  28.6 2.0 %collective-permute-start.9 = (bf16[32,256]{1,0:T(8,128)(2,1)S(1)}, bf16[32,256]{1,0:T(8,128)(2,1)S(1)}, u32[]{:S(2)}, u32[]{:S(2)}) collective-permute-start(bf16[32,256]{1,0:T(8,128)(2,1)S(1)} %get-tuple-element.57), channel_id=1, source_target_pairs={{0,1},{1,0},{2,3},{3,2},{4,8},{5,9},{6,10},{7,11},{8,4},{9,5},{10,... | collective-permute-start | bytes 49160 | tf_op jit(solution)/shard_map/ppermute | solution.py:43
  30.6 0.0 collective-permute-start.10
  30.6 0.6 %collective-permute-start.11 = (f32[8,128]{1,0:T(8,128)S(1)}, f32[8,128]{1,0:T(8,128)S(1)}, u32[]{:S(2)}, u32[]{:S(2)}) collective-permute-start(f32[8,128]{1,0:T(8,128)S(1)} %get-tuple-element.54.part_ref), channel_id=1, source_target_pairs={{0,2},{1,3},{2,0},{3,1},{4,6},{5,7},{6,4},{7,5},{8,10},{9,11},{10,... | collective-permute-start | bytes 12296 | tf_op jit(solution)/shard_map/ppermute | solution.py:544
  31.2 0.7 %shard_map.120 = f32[32,1024]{1,0:T(8,128)} custom-call(f32[32,128]{1,0:T(8,128)S(1)} %get-tuple-element.50.step_ref, f32[32,1024]{1,0:T(8,128)S(1)} %get-tuple-element.38.resid_ref, f32[32,1024]{1,0:T(8,128)S(1)} %get-tuple-element.51.assembled_ref), custom_call_target="tpu_custom_call" | custom-call | flops 1024 | bytes 65536 | tf_op jit(solution)/shard_map/pallas_call | solution.py:503
  31.9 3.2 %collective-permute-done.11.far_ref = f32[8,128]{1,0:T(8,128)S(1)} collective-permute-done((f32[8,128]{1,0:T(8,128)S(1)}, f32[8,128]{1,0:T(8,128)S(1)}, u32[]{:S(2)}, u32[]{:S(2)}) %collective-permute-start.11) | collective-permute-done | bytes 4128 | tf_op jit(solution)/shard_map/ppermute | solution.py:544
  35.1 0.0 collective-permute-done.9.r2
  35.1 0.0 collective-permute-done.10.r3
  35.1 0.0 collective-permute-done.7.r0
  35.1 0.0 collective-permute-done.8.r1
  35.1 0.8 %shard_map.121 = (f32[32,1024]{1,0:T(8,128)}, f32[1,32]{1,0:T(1,128)}) custom-call(s32[1,8]{1,0:T(1,128)S(1)} %bitcast.21, f32[1,32]{1,0:T(1,128)S(1)} %bitcast.23, f32[32,1024]{1,0:T(8,128)S(1)} %get-tuple-element.37.dir_ref, f32[32,1024]{1,0:T(8,128)S(1)} %get-tuple-element.52.weighted_ref, f32[8,128]{1,0:T(8,128)S(1)} %get-tuple-element.53.base_ref, ...), custom_call_target="tpu_custom_call" | custom-call | flops 1024 | bytes 65536 | tf_op jit(solution)/shard_map/pallas_call | solution.py:503
  (1 shorter events, 0.0 us)
Async XLA Ops:
  0.6 9.6 %copy-start = (s32[1,1,8]{2,1,0:T(1,128)S(1)}, s32[1,1,8]{2,1,0:T(1,128)}, u32[]{:S(2)}) copy-start(s32[1,1,8]{2,1,0:T(1,128)} %param.17) | copy-start | bytes 100
  0.6 9.4 %copy-start.3 = (f32[8,4]{0,1:T(4,128)S(1)}, f32[8,4]{0,1:T(4,128)}, u32[]{:S(2)}) copy-start(f32[8,4]{0,1:T(4,128)} %param.16) | copy-start | bytes 388
  2.7 7.5 %collective-permute-start.4 = (bf16[8,20,4,20]{3,2,1,0:T(4,128)(2,1)S(1)}, bf16[8,20,4,20]{3,2,1,0:T(4,128)(2,1)S(1)}, u32[]{:S(2)}, u32[]{:S(2)}) collective-permute-start(bf16[8,20,4,20]{3,2,1,0:T(4,128)(2,1)S(1)} %get-tuple-element.45), channel_id=1, source_target_pairs={{0,4},{4,0},{8,12},{12,8},{16,20},{20,16},{24,28},{28,24},{1,5},{5... | collective-permute-start | bytes 76808 | tf_op jit(solution)/shard_map/ppermute | solution.py:123
  3.2 8.7 %collective-permute-start = (bf16[32,256]{1,0:T(8,128)(2,1)S(1)}, bf16[32,256]{1,0:T(8,128)(2,1)S(1)}, u32[]{:S(2)}, u32[]{:S(2)}) collective-permute-start(bf16[32,256]{1,0:T(8,128)(2,1)S(1)} %get-tuple-element.33), channel_id=1, source_target_pairs={{1,2},{2,1},{3,0},{0,3},{5,6},{6,5},{7,4},{4,7},{9,10},{10,9},{11,... | collective-permute-start | bytes 49160 | tf_op jit(solution)/shard_map/ppermute | solution.py:31
  7.9 4.0 %collective-permute-start.1 = (bf16[32,256]{1,0:T(8,128)(2,1)S(1)}, bf16[32,256]{1,0:T(8,128)(2,1)S(1)}, u32[]{:S(2)}, u32[]{:S(2)}) collective-permute-start(bf16[32,256]{1,0:T(8,128)(2,1)S(1)} %get-tuple-element.34), channel_id=1, source_target_pairs={{0,1},{1,0},{2,3},{3,2},{4,5},{5,4},{6,7},{7,6},{8,9},{9,8},{10,11... | collective-permute-start | bytes 49160 | tf_op jit(solution)/shard_map/ppermute | solution.py:31
  7.9 4.0 %collective-permute-start.2 = (bf16[32,256]{1,0:T(8,128)(2,1)S(1)}, bf16[32,256]{1,0:T(8,128)(2,1)S(1)}, u32[]{:S(2)}, u32[]{:S(2)}) collective-permute-start(bf16[32,256]{1,0:T(8,128)(2,1)S(1)} %get-tuple-element.35), channel_id=1, source_target_pairs={{0,1},{1,0},{2,3},{3,2},{4,8},{5,9},{6,10},{7,11},{8,4},{9,5},{10,... | collective-permute-start | bytes 49160 | tf_op jit(solution)/shard_map/ppermute | solution.py:43
  9.9 2.0 %collective-permute-start.3 = (bf16[32,256]{1,0:T(8,128)(2,1)S(1)}, bf16[32,256]{1,0:T(8,128)(2,1)S(1)}, u32[]{:S(2)}, u32[]{:S(2)}) collective-permute-start(bf16[32,256]{1,0:T(8,128)(2,1)S(1)} %get-tuple-element.36), channel_id=1, source_target_pairs={{0,4},{4,0},{8,12},{12,8},{16,20},{20,16},{24,28},{28,24},{1,5},{5... | collective-permute-start | bytes 49160 | tf_op jit(solution)/shard_map/ppermute | solution.py:31
  10.3 1.6 %copy-start.2 = (bf16[1,1,1024,1024]{3,2,1,0:T(8,128)(2,1)S(1)}, bf16[1,1,1024,1024]{3,2,1,0:T(8,128)(2,1)}, u32[]{:S(2)}) copy-start(bf16[1,1,1024,1024]{3,2,1,0:T(8,128)(2,1)} %param.13) | copy-start | bytes 6291460
  10.8 6.3 %collective-permute-start.5 = (bf16[2,160,96]{2,1,0:T(8,128)(2,1)S(1)}, bf16[2,160,96]{2,1,0:T(8,128)(2,1)S(1)}, u32[]{:S(2)}, u32[]{:S(2)}) collective-permute-start(bf16[2,160,96]{2,1,0:T(8,128)(2,1)S(1)} %shard_map.115.mine_ref), channel_id=1, source_target_pairs={{0,8},{4,12},{8,0},{12,4},{16,24},{20,28},{24,16},{28,20},{1,9},{5... | collective-permute-start | bytes 184328 | tf_op jit(solution)/shard_map/ppermute | solution.py:123
  13.3 11.7 %all-to-all-start = ((bf16[32,6,2,128]{3,2,1,0:T(2,128)(2,1)}), bf16[32,6,2,128]{3,2,1,0:T(2,128)(2,1)S(1)}, u32[]{:S(2)}, u32[]{:S(2)}) async-start(bf16[32,6,2,128]{3,2,1,0:T(2,128)(2,1)} %bitcast.8), calls=%async_computation | async-start | bytes 196608 | tf_op jit(solution)/shard_map/all_to_all | solution.py:531
  17.1 7.9 %copy-start.1 = (f32[32]{0:T(128)S(1)}, f32[32]{0:T(128)}, u32[]{:S(2)}) copy-start(f32[32]{0:T(128)} %param.11) | copy-start | bytes 388
  17.2 6.3 %collective-permute-start.6 = (bf16[160,384]{1,0:T(8,128)(2,1)S(1)}, bf16[160,384]{1,0:T(8,128)(2,1)S(1)}, u32[]{:S(2)}, u32[]{:S(2)}) collective-permute-start(bf16[160,384]{1,0:T(8,128)(2,1)S(1)} %shard_map.116.mine_ref), channel_id=1, source_target_pairs={{0,16},{4,20},{8,24},{12,28},{16,0},{20,4},{24,8},{28,12},{1,17},{... | collective-permute-start | bytes 368648 | tf_op jit(solution)/shard_map/ppermute | solution.py:123
  25.7 9.4 %collective-permute-start.7 = (bf16[48,256]{1,0:T(8,128)(2,1)S(1)}, bf16[48,256]{1,0:T(8,128)(2,1)S(1)}, u32[]{:S(2)}, u32[]{:S(2)}) collective-permute-start(bf16[48,256]{1,0:T(8,128)(2,1)S(1)} %get-tuple-element.55), channel_id=1, source_target_pairs={{1,2},{2,1},{3,0},{0,3},{5,6},{6,5},{7,4},{4,7},{9,10},{10,9},{11,... | collective-permute-start | bytes 73736 | tf_op jit(solution)/shard_map/ppermute | solution.py:31
  28.6 6.6 %collective-permute-start.8 = (bf16[48,256]{1,0:T(8,128)(2,1)S(1)}, bf16[48,256]{1,0:T(8,128)(2,1)S(1)}, u32[]{:S(2)}, u32[]{:S(2)}) collective-permute-start(bf16[48,256]{1,0:T(8,128)(2,1)S(1)} %get-tuple-element.56), channel_id=1, source_target_pairs={{0,1},{1,0},{2,3},{3,2},{4,5},{5,4},{6,7},{7,6},{8,9},{9,8},{10,11... | collective-permute-start | bytes 73736 | tf_op jit(solution)/shard_map/ppermute | solution.py:31
  28.6 6.5 %collective-permute-start.9 = (bf16[32,256]{1,0:T(8,128)(2,1)S(1)}, bf16[32,256]{1,0:T(8,128)(2,1)S(1)}, u32[]{:S(2)}, u32[]{:S(2)}) collective-permute-start(bf16[32,256]{1,0:T(8,128)(2,1)S(1)} %get-tuple-element.57), channel_id=1, source_target_pairs={{0,1},{1,0},{2,3},{3,2},{4,8},{5,9},{6,10},{7,11},{8,4},{9,5},{10,... | collective-permute-start | bytes 49160 | tf_op jit(solution)/shard_map/ppermute | solution.py:43
  30.6 4.5 %collective-permute-start.10 = (bf16[32,256]{1,0:T(8,128)(2,1)S(1)}, bf16[32,256]{1,0:T(8,128)(2,1)S(1)}, u32[]{:S(2)}, u32[]{:S(2)}) collective-permute-start(bf16[32,256]{1,0:T(8,128)(2,1)S(1)} %get-tuple-element.58), channel_id=1, source_target_pairs={{0,4},{4,0},{8,12},{12,8},{16,20},{20,16},{24,28},{28,24},{1,5},{5... | collective-permute-start | bytes 49160 | tf_op jit(solution)/shard_map/ppermute | solution.py:31
  30.6 4.5 %collective-permute-start.11 = (f32[8,128]{1,0:T(8,128)S(1)}, f32[8,128]{1,0:T(8,128)S(1)}, u32[]{:S(2)}, u32[]{:S(2)}) collective-permute-start(f32[8,128]{1,0:T(8,128)S(1)} %get-tuple-element.54.part_ref), channel_id=1, source_target_pairs={{0,2},{1,3},{2,0},{3,1},{4,6},{5,7},{6,4},{7,5},{8,10},{9,11},{10,... | collective-permute-start | bytes 12296 | tf_op jit(solution)/shard_map/ppermute | solution.py:544

commit v7 on v6

--- a/solution.py
+++ b/solution.py
@@ -362,38 +362,6 @@
     out_ref[...] = jnp.concatenate([both_ref[i] for i in range(2 * n)], axis=1)
 
 
-def sector_kernel(prim, depth, width, up, mine_ref, got_ref, wide_ref):
-    slabs = lax.axis_size("gx")
-    rows = slabs * up
-    half = prim // 2
-    top = (lax.axis_index("gx") * 2) // slabs
-    low = jnp.where(top == 0, mine_ref[...].astype(F32), got_ref[...].astype(F32))
-    high = jnp.where(top == 0, got_ref[...].astype(F32), mine_ref[...].astype(F32))
-    pieces = []
-    for part in range(2):
-        for h in range(slabs):
-            source = low if h < slabs // 2 else high
-            at = h % (slabs // 2) * 2 * width + part * width
-            pieces.append(source[:, at : at + width])
-    flat = jnp.concatenate(pieces, axis=1)
-    empty = jnp.zeros((up - prim, flat.shape[1]), F32)
-    parts = []
-    for g in range(slabs):
-        parts += [flat[g * prim : (g + 1) * prim], empty]
-    wide_ref[0:rows, :] = jnp.concatenate(parts, axis=0).astype(BF16)
-    shape = (wide_ref.shape[0] - rows, wide_ref.shape[1])
-    row = lax.broadcasted_iota(jnp.int32, shape, 0)
-    lane = lax.broadcasted_iota(jnp.int32, shape, 1)
-    part = lane // (slabs * width)
-    at = lane % depth
-    slab = lane // width % slabs
-    sector = lane % width // depth
-    sums = jnp.logical_and(at >= half, row == (at - half) * 2 + part)
-    mine = jnp.logical_and(sector == lax.axis_index("col"), at < half)
-    own = jnp.logical_and(mine, row == 16 + slab * up + part * half + at)
-    wide_ref[rows:, :] = jnp.where(jnp.logical_or(sums, own), 1.0, 0.0).astype(BF16)
-
-
 def near_rhs_kernel(rows, sectors, perm_ref, image_ref, r0, r1, r2, r3, weight_ref, basis_ref, rhs_ref, curv_ref,
                     scaled_ref, resid_ref, neumann_ref, assembled_ref, sol_r_ref, sol_q_ref, out_ref):
     for at, part in received_blocks(perm_ref, (r0, r1, r2, r3), image_ref.shape[1] // BLK):
@@ -424,31 +392,52 @@
         out_ref[i * step : (i + 1) * step] = several
 
 
-def weigh_kernel(weight_ref, r_ref, q_ref, r_out, q_out):
+def frame_kernel(depth, weight_ref, r_ref, q_ref, basis_ref, r_out, q_out, picks_ref, basis_out):
     r_out[...] = weight_ref[0:1, :] * r_ref[...]
     q_out[...] = weight_ref[0:1, :] * q_ref[...]
-
-
-def near_solve_kernel(perm_ref, gathered_ref, wide_ref, prev_ref, weight_ref, basis_ref, sol_r_ref, sol_q_ref,
-                      step_out, weighted_out, base_out, part_out, f0, f1, f2, f3, sol_ref):
+    prim = basis_ref.shape[0]
+    half = prim // 2
+    rows = basis_out.shape[0]
+    slabs, sectors = lax.axis_size("gx"), lax.axis_size("col")
+    width = sectors * depth
+    row = lax.broadcasted_iota(jnp.int32, picks_ref.shape, 0)
+    lane = lax.broadcasted_iota(jnp.int32, picks_ref.shape, 1)
+    part = lane // width % 2
+    at = lane % depth
+    sums = jnp.logical_and(at >= half, row == (at - half) * 2 + part)
+    mine = jnp.logical_and(lane % width // depth == lax.axis_index("col"), at < half)
+    own = jnp.logical_and(mine, row == 16 + lane // (2 * width) * prim + part * half + at)
+    picks_ref[...] = jnp.where(jnp.logical_or(sums, own), 1.0, 0.0).astype(BF16)
+    row = lax.broadcasted_iota(jnp.int32, (rows, prim), 0)
+    lane = lax.broadcasted_iota(jnp.int32, (rows, prim), 1)
+    here = jnp.where(row == lax.axis_index("gx") * prim + lane, 1.0, 0.0).astype(BF16)
+    basis_out[...] = jnp.dot(here, basis_ref[...], preferred_element_type=F32).astype(BF16)
+
+
+def near_solve_kernel(perm_ref, gathered_ref, mine_ref, got_ref, picks_ref, prev_ref, weight_ref, basis_ref,
+                      sol_r_ref, sol_q_ref, step_out, weighted_out, base_out, part_out, f0, f1, f2, f3, rhs_ref):
     n = prev_ref.shape[1]
-    prim = basis_ref.shape[0]
     slabs = lax.axis_size("gx")
-    rows = (wide_ref.shape[0] - 16) // 2
-    up = rows // slabs
-    halves = jnp.concatenate([gathered_ref[:, : 2 * n], gathered_ref[:, 2 * n :]], axis=0)
-    total = jnp.dot(wide_ref[...], halves, preferred_element_type=F32)
-    curvature, first, second, third = (
-        total[rows + i : rows + i + 1, 0:n] + total[rows + i : rows + i + 1, n : 2 * n] for i in range(4)
-    )
+    width = gathered_ref.shape[0] // slabs
+    for h in range(slabs):
+        part = gathered_ref[h * width : (h + 1) * width]
+        rhs_ref[2 * h * width : (2 * h + 1) * width] = part[:, : 2 * n]
+        rhs_ref[(2 * h + 1) * width : (2 * h + 2) * width] = part[:, 2 * n :]
+    count = slabs * width
+    top = (lax.axis_index("gx") * 2) // slabs
+    mine = rhs_ref[pl.ds(pl.multiple_of(top * count, 16), count), :]
+    got = rhs_ref[pl.ds(pl.multiple_of((1 - top) * count, 16), count), :]
+    picked = jnp.dot(picks_ref[...], rhs_ref[...], preferred_element_type=F32)
+    total = jnp.dot(mine_ref[...], mine, preferred_element_type=F32) + jnp.dot(
+        got_ref[...], got, preferred_element_type=F32
+    )
+    curvature, first, second, third = (picked[i : i + 1, 0:n] + picked[i : i + 1, n : 2 * n] for i in range(4))
     step = prev_ref[...] / curvature
-    sol = (total[0:rows, 0:n] - step * total[0:rows, n : 2 * n]).astype(BF16).astype(F32)
-    sol_ref[...] = sol
-    rhs = total[rows + 16 :, 0:n] - step * total[rows + 16 :, n : 2 * n]
-    high, low = split(jnp.sum(sol * rhs, axis=0, keepdims=True))
-    own = sol_ref[pl.ds(pl.multiple_of(lax.axis_index("gx") * up, 8), up), :].astype(BF16)
+    sol = (total[:, 0:n] - step * total[:, n : 2 * n]).astype(BF16)
+    rhs = picked[16:, 0:n] - step * picked[16:, n : 2 * n]
+    high, low = split(jnp.sum(sol.astype(F32) * rhs, axis=0, keepdims=True))
     correction = lax.dot_general(
-        own[0:prim], basis_ref[...], (((0,), (0,)), ((), ())), preferred_element_type=F32
+        sol, basis_ref[...], (((0,), (0,)), ((), ())), preferred_element_type=F32
     )
     step_col = to_column(step)
     step_out[...] = jnp.broadcast_to(step_col, step_out.shape)
@@ -466,7 +455,7 @@
     f1[n:, :] = lines
 
 
-def near_direction_kernel(perm_ref, rz_ref, dir_ref, weighted_ref, base_ref, part_ref, r0, r1, r2, r3, far_ref,
+def near_direction_kernel(perm_ref, rz_ref, dir_ref, weighted_ref, base_ref, part_ref, far_ref, r0, r1, r2, r3,
                           out_ref, rz_out):
     n = rz_ref.shape[1]
     sector = lax.axis_index("col")
@@ -493,7 +482,6 @@
     rhs, width = resid.shape
     prim = basis_t.shape[0]
     slabs, sectors = lax.axis_size("gx"), lax.axis_size("col")
-    up = -(-prim // 8) * 8
     vmem = pl.BlockSpec(memory_space=VMEM)
     full = jax.ShapeDtypeStruct((rhs, width), F32)
     line = jax.ShapeDtypeStruct((8, BLK), F32)
@@ -523,29 +511,33 @@
         blocks, swap_bit(blocks, 1), after=(packed,), scratch=[pltpu.VMEM((4,) + shard, BF16)],
         estimate=cost(2000 * rhs * width * width, 1 << 16),
     )
-    (wide,) = call(
-        functools.partial(sector_kernel, prim, rows, shard[1] // 2, up),
-        (jax.ShapeDtypeStruct((2 * slabs * up + 16, slabs * shard[1]), BF16),), blocks, swap_bit(blocks, 2),
-    )
+    got = swap_bit(blocks, 2)
     packed = packed.reshape(slabs * sectors, rows // 2, 2, BLK)
     gathered = lax.all_to_all(packed, ("gx", "col"), 0, 0).reshape(slabs * sectors * rows, BLK)
-    sol_r, sol_q = call(
-        weigh_kernel, (full, full), weight, sol_r, sol_q,
+    sol_r, sol_q, picks, placed = call(
+        functools.partial(frame_kernel, rows),
+        (
+            full,
+            full,
+            jax.ShapeDtypeStruct((16 + slabs * prim, slabs * shard[1]), BF16),
+            jax.ShapeDtypeStruct((slabs * prim, width), BF16),
+        ),
+        weight, sol_r, sol_q, basis_t,
     )
     face = jax.ShapeDtypeStruct((rhs, 2 * BLK), BF16)
     tall = jax.ShapeDtypeStruct((rhs + 16, 2 * BLK), BF16)
     step, weighted, base, part, *faces = call(
         near_solve_kernel,
-        (jax.ShapeDtypeStruct((rhs, BLK), F32), full, line, line, tall, tall, face, face),
-        perm, gathered, wide, rz_row, weight, basis_t, sol_r, sol_q,
-        scratch=[pltpu.VMEM((slabs * up, rhs), F32)],
-    )
+        (jax.ShapeDtypeStruct((rhs, BLK), F32), full, line, jax.ShapeDtypeStruct((64, BLK), F32), tall, tall, face, face),
+        perm, gathered, blocks, got, picks, rz_row, weight, placed, sol_r, sol_q,
+        scratch=[pltpu.VMEM((slabs * shard[1], 2 * rhs), BF16)],
+    )
+    far = lax.ppermute(part, "col", [(i, i ^ 2) for i in range(sectors)])
     received = swap_faces(faces)
-    far = lax.ppermute(part, "col", [(i, i ^ 2) for i in range(sectors)])
     (resid_new,) = call(resid_kernel, (full,), step, resid, assembled)
     direction_new, rz_next = call(
         near_direction_kernel, (full, jax.ShapeDtypeStruct((1, rhs), F32)),
-        perm, rz_row, direction, weighted, base, part, *received, far,
+        perm, rz_row, direction, weighted, base, part, far, *received,
     )
     return (resid_new[None, None], direction_new[None, None], rz_next[0])
 

time: 36.2 us -> 34.1 us (0.942)
  waiting for transfers between devices: 8.51 us -> 7.33 us
  starting transfers between devices: 19.4 us -> 18.8 us
    all_to_all x1, waiting for transfers between devices: 0.86 us -> 5.55 us  [near_rest(): lax.all_to_all(packed, ('gx', 'col'), 0, 0)]
    ppermute x3, waiting for transfers between devices: 4.41 us -> 0.01 us  [swap_bit(): return lax.ppermute(value, 'gx', [(i, i ^ 1 << k) for i in range(count)])]
    ppermute x1, waiting for transfers between devices: 3.22 us -> 0.01 us  [near_rest(): far = lax.ppermute(part, 'col', [(i, i ^ 2) for i in range(sectors)])]
    ppermute x2, waiting for transfers between devices: 0.01 us -> 1.75 us  [swap_second(): return lax.ppermute(value, ('gx', 'col'), pairs)]
    ppermute x1, starting transfers between devices: 0.56 us -> 1.35 us  [near_rest(): far = lax.ppermute(part, 'col', [(i, i ^ 2) for i in range(sectors)])]
    ppermute x2, starting transfers between devices: 4.05 us -> 3.27 us  [swap_second(): return lax.ppermute(value, ('gx', 'col'), pairs)]
    ppermute x6, starting transfers between devices: 7.56 us -> 6.89 us  [swap(): return lax.ppermute(value, axis, pairs)]
    pallas_call x8 -> x7, Pallas kernels: 4.61 us -> 4.36 us  [call(): pl.pallas_call(kernel, out_shape=outs, in_specs=[pl.BlockSpec(memory_spac...]
  transfers between devices with their start and end apart: 13 -> 13, of which waited for: 3 -> 2; matrix products, arithmetic and copies ran while one was open for 1% -> 1% of each run, Pallas kernels for 9% -> 9%
where the time goes in v7:
time: 34.1 us; the launch traced here: 33.9 us
  starting transfers between devices  18.8 us (55%)
  waiting for transfers between devices  7.33 us (21%)
  Pallas kernels  6.64 us (19%)
  between operations  0.79 us (2%)
  local copies, waits for them, and re-layouts  0.37 us (1%)
    ppermute x6, starting transfers between devices, swap(): return lax.ppermute(value, axis, pairs)  6.89 us
    all_to_all x1, waiting for transfers between devices, near_rest(): lax.all_to_all(packed, ('gx', 'col'), 0, 0)  5.55 us
    pallas_call x7, Pallas kernels, call(): pl.pallas_call(kernel, out_shape=outs, in_specs=[pl.BlockSpec(memory_spac...  4.36 us
    all_to_all x1, starting transfers between devices, near_rest(): lax.all_to_all(packed, ('gx', 'col'), 0, 0)  3.75 us
    ppermute x3, starting transfers between devices, swap_bit(): return lax.ppermute(value, 'gx', [(i, i ^ 1 << k) for i in range(count)])  3.49 us
    ppermute x2, starting transfers between devices, swap_second(): return lax.ppermute(value, ('gx', 'col'), pairs)  3.27 us
    pallas_call x1, Pallas kernels, body(): pl.pallas_call(image_kernel, out_shape=(full,) + (face,) * 4 + (full, ful...  2.02 us
    ppermute x2, waiting for transfers between devices, swap_second(): return lax.ppermute(value, ('gx', 'col'), pairs)  1.75 us
  transfers between devices with their start and end apart: 13, of which 2 were waited for; matrix products, arithmetic and copies ran while one was open for 1% of the time, Pallas kernels for 9%

profile of v7, /device:TPU:0, one launch (start us, length us, event | category | flops | bytes accessed | tf_op | source)
XLA Modules:
  0.0 33.9 jit_solution(12428916854363371530)
XLA Ops:
  0.6 0.0 copy-start
  0.6 0.0 copy-start.3
  0.7 2.0 %shard_map.112 = (f32[32,1024]{1,0:T(8,128)S(1)}, bf16[32,256]{1,0:T(8,128)(2,1)S(1)}, bf16[32,256]{1,0:T(8,128)(2,1)S(1)}, bf16[32,256]{1,0:T(8,128)(2,1)S(1)},...) custom-call(s32[1,8]{1,0:T(1,128)} %bitcast.16, ...), custom_call_target="tpu_custom_call" | custom-call | flops 67108864 | bytes 2097152 | tf_op jit(solution)/shard_map/pallas_call | solution.py:570
  2.7 0.5 %collective-permute-start.4 = (bf16[8,20,4,20]{3,2,1,0:T(4,128)(2,1)S(1)}, bf16[8,20,4,20]{3,2,1,0:T(4,128)(2,1)S(1)}, u32[]{:S(2)}, u32[]{:S(2)}) collective-permute-start(bf16[8,20,4,20]{3,2,1,0:T(4,128)(2,1)S(1)} %get-tuple-element.47), channel_id=1, source_target_pairs={{0,4},{4,0},{8,12},{12,8},{16,20},{20,16},{24,28},{28,24},{1,5},{5... | collective-permute-start | bytes 76808 | tf_op jit(solution)/shard_map/ppermute | solution.py:123
  3.2 4.7 %collective-permute-start = (bf16[32,256]{1,0:T(8,128)(2,1)S(1)}, bf16[32,256]{1,0:T(8,128)(2,1)S(1)}, u32[]{:S(2)}, u32[]{:S(2)}) collective-permute-start(bf16[32,256]{1,0:T(8,128)(2,1)S(1)} %get-tuple-element.35), channel_id=1, source_target_pairs={{1,2},{2,1},{3,0},{0,3},{5,6},{6,5},{7,4},{4,7},{9,10},{10,9},{11,... | collective-permute-start | bytes 49160 | tf_op jit(solution)/shard_map/ppermute | solution.py:31
  7.9 0.0 collective-permute-start.1
  7.9 2.0 %collective-permute-start.2 = (bf16[32,256]{1,0:T(8,128)(2,1)S(1)}, bf16[32,256]{1,0:T(8,128)(2,1)S(1)}, u32[]{:S(2)}, u32[]{:S(2)}) collective-permute-start(bf16[32,256]{1,0:T(8,128)(2,1)S(1)} %get-tuple-element.37), channel_id=1, source_target_pairs={{0,1},{1,0},{2,3},{3,2},{4,8},{5,9},{6,10},{7,11},{8,4},{9,5},{10,... | collective-permute-start | bytes 49160 | tf_op jit(solution)/shard_map/ppermute | solution.py:43
  9.9 0.0 collective-permute-start.3
  9.9 0.1 reshape.20.own_ref
  10.0 0.0 copy-done.3
  10.1 0.1 copy.12.conduct_ref
  10.1 0.0 collective-permute-done.4
  10.1 0.1 reshape.21.mate_ref
  10.3 0.0 copy-done
  10.3 0.0 copy-start.2
  10.3 0.3 shard_map.113
  10.6 0.2 shard_map.115.mine_ref
  10.8 1.1 %collective-permute-start.5 = (bf16[2,160,96]{2,1,0:T(8,128)(2,1)S(1)}, bf16[2,160,96]{2,1,0:T(8,128)(2,1)S(1)}, u32[]{:S(2)}, u32[]{:S(2)}) collective-permute-start(bf16[2,160,96]{2,1,0:T(8,128)(2,1)S(1)} %shard_map.115.mine_ref), channel_id=1, source_target_pairs={{0,8},{4,12},{8,0},{12,4},{16,24},{20,28},{24,16},{28,20},{1,9},{5... | collective-permute-start | bytes 184328 | tf_op jit(solution)/shard_map/ppermute | solution.py:123
  11.9 0.0 collective-permute-done.r0
  11.9 0.0 collective-permute-done.1.r1
  11.9 0.0 collective-permute-done.2.r2
  11.9 0.0 collective-permute-done.3.r3
  11.9 0.0 copy-done.2
  11.9 1.4 %shard_map.114 = (f32[32,1024]{1,0:T(8,128)S(1)}, f32[32,1024]{1,0:T(8,128)S(1)}, f32[32,1024]{1,0:T(8,128)S(1)}, bf16[384,128]{1,0:T(8,128)(2,1)}) custom-call(s32[1,8]{1,0:T(1,128)S(1)} %bitcast.19, f32[32,1024]{1,0:T(8,128)S(1)} %get-tuple-element.34.image_ref, bf16[32,256]{1,0:T(8,128)(2,1)S(1)} %collective-permute-done.r0, ...), custom_call_target="tpu_custom_call" | custom-call | flops 67108864000 | bytes 65536 | tf_op jit(solution)/shard_map/pallas_call | solution.py:491
  13.3 3.8 %all-to-all-start = ((bf16[32,6,2,128]{3,2,1,0:T(2,128)(2,1)}), bf16[32,6,2,128]{3,2,1,0:T(2,128)(2,1)S(1)}, u32[]{:S(2)}, u32[]{:S(2)}) async-start(bf16[32,6,2,128]{3,2,1,0:T(2,128)(2,1)} %bitcast.8), calls=%async_computation | async-start | bytes 196608 | tf_op jit(solution)/shard_map/all_to_all | solution.py:516
  17.1 0.0 copy-start.1
  17.1 0.0 collective-permute-done.5.got_ref
  17.1 0.1 shard_map.116.mine_ref
  17.2 1.8 %collective-permute-start.6 = (bf16[160,384]{1,0:T(8,128)(2,1)S(1)}, bf16[160,384]{1,0:T(8,128)(2,1)S(1)}, u32[]{:S(2)}, u32[]{:S(2)}) collective-permute-start(bf16[160,384]{1,0:T(8,128)(2,1)S(1)} %shard_map.116.mine_ref), channel_id=1, source_target_pairs={{0,16},{4,20},{8,24},{12,28},{16,0},{20,4},{24,8},{28,12},{1,17},{... | collective-permute-start | bytes 368648 | tf_op jit(solution)/shard_map/ppermute | solution.py:123
  19.1 0.4 %shard_map.117 = (f32[32,1024]{1,0:T(8,128)S(1)}, f32[32,1024]{1,0:T(8,128)S(1)}, bf16[176,768]{1,0:T(8,128)(2,1)S(1)}, bf16[160,1024]{1,0:T(8,128)(2,1)S(1)}) custom-call(f32[8,1024]{1,0:T(8,128)S(1)} %get-tuple-element.42.weight_ref, f32[32,1024]{1,0:T(8,128)S(1)} %get-tuple-element.48.r_ref, f32[32,1024]{1,0:T(8,128)S(1)} %get-tuple-element.49.q_ref, ...), custom_call_target="tpu_custom_call" | custom-call | flops 1024 | bytes 65536 | tf_op jit(solution)/shard_map/pallas_call | solution.py:491
  19.5 5.5 %all-to-all-done = bf16[32,6,2,128]{3,2,1,0:T(2,128)(2,1)S(1)} async-done(((bf16[32,6,2,128]{3,2,1,0:T(2,128)(2,1)}), bf16[32,6,2,128]{3,2,1,0:T(2,128)(2,1)S(1)}, u32[]{:S(2)}, u32[]{:S(2)}) %all-to-all-start) | async-done | bytes 98336 | tf_op jit(solution)/shard_map/all_to_all | solution.py:516
  25.0 0.0 collective-permute-done.6.got_ref
  25.0 0.0 copy-done.1
  25.0 0.7 %shard_map.118 = (f32[32,128]{1,0:T(8,128)S(1)}, f32[32,1024]{1,0:T(8,128)S(1)}, f32[8,128]{1,0:T(8,128)S(1)}, f32[64,128]{1,0:T(8,128)S(1)}, bf16[48,256]{1,0:T...) custom-call(s32[1,8]{1,0:T(1,128)S(1)} %bitcast.20, ...), custom_call_target="tpu_custom_call" | custom-call | flops 1024 | bytes 65536 | tf_op jit(solution)/shard_map/pallas_call | solution.py:491
  25.7 1.3 %collective-permute-start.7 = (f32[64,128]{1,0:T(8,128)S(1)}, f32[64,128]{1,0:T(8,128)S(1)}, u32[]{:S(2)}, u32[]{:S(2)}) collective-permute-start(f32[64,128]{1,0:T(8,128)S(1)} %get-tuple-element.58.part_ref), channel_id=1, source_target_pairs={{0,2},{1,3},{2,0},{3,1},{4,6},{5,7},{6,4},{7,5},{8,10},{9,11},{10,... | collective-permute-start | bytes 98312 | tf_op jit(solution)/shard_map/ppermute | solution.py:535
  27.1 1.4 %collective-permute-start.8 = (bf16[48,256]{1,0:T(8,128)(2,1)S(1)}, bf16[48,256]{1,0:T(8,128)(2,1)S(1)}, u32[]{:S(2)}, u32[]{:S(2)}) collective-permute-start(bf16[48,256]{1,0:T(8,128)(2,1)S(1)} %get-tuple-element.59), channel_id=1, source_target_pairs={{1,2},{2,1},{3,0},{0,3},{5,6},{6,5},{7,4},{4,7},{9,10},{10,9},{11,... | collective-permute-start | bytes 73736 | tf_op jit(solution)/shard_map/ppermute | solution.py:31
  28.5 0.8 %collective-permute-start.9 = (bf16[48,256]{1,0:T(8,128)(2,1)S(1)}, bf16[48,256]{1,0:T(8,128)(2,1)S(1)}, u32[]{:S(2)}, u32[]{:S(2)}) collective-permute-start(bf16[48,256]{1,0:T(8,128)(2,1)S(1)} %get-tuple-element.60), channel_id=1, source_target_pairs={{0,1},{1,0},{2,3},{3,2},{4,5},{5,4},{6,7},{7,6},{8,9},{9,8},{10,11... | collective-permute-start | bytes 73736 | tf_op jit(solution)/shard_map/ppermute | solution.py:31
  29.3 1.2 %collective-permute-start.10 = (bf16[32,256]{1,0:T(8,128)(2,1)S(1)}, bf16[32,256]{1,0:T(8,128)(2,1)S(1)}, u32[]{:S(2)}, u32[]{:S(2)}) collective-permute-start(bf16[32,256]{1,0:T(8,128)(2,1)S(1)} %get-tuple-element.61), channel_id=1, source_target_pairs={{0,1},{1,0},{2,3},{3,2},{4,8},{5,9},{6,10},{7,11},{8,4},{9,5},{10,... | collective-permute-start | bytes 49160 | tf_op jit(solution)/shard_map/ppermute | solution.py:43
  30.5 0.0 collective-permute-start.11
  30.5 0.7 %shard_map.119 = f32[32,1024]{1,0:T(8,128)} custom-call(f32[32,128]{1,0:T(8,128)S(1)} %get-tuple-element.54.step_ref, f32[32,1024]{1,0:T(8,128)S(1)} %get-tuple-element.40.resid_ref, f32[32,1024]{1,0:T(8,128)S(1)} %get-tuple-element.55.assembled_ref), custom_call_target="tpu_custom_call" | custom-call | flops 1024 | bytes 65536 | tf_op jit(solution)/shard_map/pallas_call | solution.py:491
  31.3 1.8 %collective-permute-done.10.r2 = bf16[32,256]{1,0:T(8,128)(2,1)S(1)} collective-permute-done((bf16[32,256]{1,0:T(8,128)(2,1)S(1)}, bf16[32,256]{1,0:T(8,128)(2,1)S(1)}, u32[]{:S(2)}, u32[]{:S(2)}) %collective-permute-start.10) | collective-permute-done | bytes 16416 | tf_op jit(solution)/shard_map/ppermute | solution.py:43
  33.0 0.0 collective-permute-done.11.r3
  33.0 0.0 collective-permute-done.8.r0
  33.0 0.0 collective-permute-done.9.r1
  33.0 0.0 collective-permute-done.7.far_ref
  33.1 0.8 %shard_map.120 = (f32[32,1024]{1,0:T(8,128)}, f32[1,32]{1,0:T(1,128)}) custom-call(s32[1,8]{1,0:T(1,128)S(1)} %bitcast.21, f32[1,32]{1,0:T(1,128)S(1)} %bitcast.23, f32[32,1024]{1,0:T(8,128)S(1)} %get-tuple-element.39.dir_ref, f32[32,1024]{1,0:T(8,128)S(1)} %get-tuple-element.56.weighted_ref, f32[8,128]{1,0:T(8,128)S(1)} %get-tuple-element.57.base_ref, ...), custom_call_target="tpu_custom_call" | custom-call | flops 1024 | bytes 65536 | tf_op jit(solution)/shard_map/pallas_call | solution.py:491
Async XLA Ops:
  0.6 9.6 %copy-start = (s32[1,1,8]{2,1,0:T(1,128)S(1)}, s32[1,1,8]{2,1,0:T(1,128)}, u32[]{:S(2)}) copy-start(s32[1,1,8]{2,1,0:T(1,128)} %param.17) | copy-start | bytes 100
  0.6 9.4 %copy-start.3 = (f32[8,4]{0,1:T(4,128)S(1)}, f32[8,4]{0,1:T(4,128)}, u32[]{:S(2)}) copy-start(f32[8,4]{0,1:T(4,128)} %param.16) | copy-start | bytes 388
  2.7 7.5 %collective-permute-start.4 = (bf16[8,20,4,20]{3,2,1,0:T(4,128)(2,1)S(1)}, bf16[8,20,4,20]{3,2,1,0:T(4,128)(2,1)S(1)}, u32[]{:S(2)}, u32[]{:S(2)}) collective-permute-start(bf16[8,20,4,20]{3,2,1,0:T(4,128)(2,1)S(1)} %get-tuple-element.47), channel_id=1, source_target_pairs={{0,4},{4,0},{8,12},{12,8},{16,20},{20,16},{24,28},{28,24},{1,5},{5... | collective-permute-start | bytes 76808 | tf_op jit(solution)/shard_map/ppermute | solution.py:123
  3.2 8.7 %collective-permute-start = (bf16[32,256]{1,0:T(8,128)(2,1)S(1)}, bf16[32,256]{1,0:T(8,128)(2,1)S(1)}, u32[]{:S(2)}, u32[]{:S(2)}) collective-permute-start(bf16[32,256]{1,0:T(8,128)(2,1)S(1)} %get-tuple-element.35), channel_id=1, source_target_pairs={{1,2},{2,1},{3,0},{0,3},{5,6},{6,5},{7,4},{4,7},{9,10},{10,9},{11,... | collective-permute-start | bytes 49160 | tf_op jit(solution)/shard_map/ppermute | solution.py:31
  7.9 4.0 %collective-permute-start.1 = (bf16[32,256]{1,0:T(8,128)(2,1)S(1)}, bf16[32,256]{1,0:T(8,128)(2,1)S(1)}, u32[]{:S(2)}, u32[]{:S(2)}) collective-permute-start(bf16[32,256]{1,0:T(8,128)(2,1)S(1)} %get-tuple-element.36), channel_id=1, source_target_pairs={{0,1},{1,0},{2,3},{3,2},{4,5},{5,4},{6,7},{7,6},{8,9},{9,8},{10,11... | collective-permute-start | bytes 49160 | tf_op jit(solution)/shard_map/ppermute | solution.py:31
  7.9 4.0 %collective-permute-start.2 = (bf16[32,256]{1,0:T(8,128)(2,1)S(1)}, bf16[32,256]{1,0:T(8,128)(2,1)S(1)}, u32[]{:S(2)}, u32[]{:S(2)}) collective-permute-start(bf16[32,256]{1,0:T(8,128)(2,1)S(1)} %get-tuple-element.37), channel_id=1, source_target_pairs={{0,1},{1,0},{2,3},{3,2},{4,8},{5,9},{6,10},{7,11},{8,4},{9,5},{10,... | collective-permute-start | bytes 49160 | tf_op jit(solution)/shard_map/ppermute | solution.py:43
  9.9 2.0 %collective-permute-start.3 = (bf16[32,256]{1,0:T(8,128)(2,1)S(1)}, bf16[32,256]{1,0:T(8,128)(2,1)S(1)}, u32[]{:S(2)}, u32[]{:S(2)}) collective-permute-start(bf16[32,256]{1,0:T(8,128)(2,1)S(1)} %get-tuple-element.38), channel_id=1, source_target_pairs={{0,4},{4,0},{8,12},{12,8},{16,20},{20,16},{24,28},{28,24},{1,5},{5... | collective-permute-start | bytes 49160 | tf_op jit(solution)/shard_map/ppermute | solution.py:31
  10.3 1.6 %copy-start.2 = (bf16[1,1,1024,1024]{3,2,1,0:T(8,128)(2,1)S(1)}, bf16[1,1,1024,1024]{3,2,1,0:T(8,128)(2,1)}, u32[]{:S(2)}) copy-start(bf16[1,1,1024,1024]{3,2,1,0:T(8,128)(2,1)} %param.13) | copy-start | bytes 6291460
  10.8 6.3 %collective-permute-start.5 = (bf16[2,160,96]{2,1,0:T(8,128)(2,1)S(1)}, bf16[2,160,96]{2,1,0:T(8,128)(2,1)S(1)}, u32[]{:S(2)}, u32[]{:S(2)}) collective-permute-start(bf16[2,160,96]{2,1,0:T(8,128)(2,1)S(1)} %shard_map.115.mine_ref), channel_id=1, source_target_pairs={{0,8},{4,12},{8,0},{12,4},{16,24},{20,28},{24,16},{28,20},{1,9},{5... | collective-permute-start | bytes 184328 | tf_op jit(solution)/shard_map/ppermute | solution.py:123
  13.3 11.7 %all-to-all-start = ((bf16[32,6,2,128]{3,2,1,0:T(2,128)(2,1)}), bf16[32,6,2,128]{3,2,1,0:T(2,128)(2,1)S(1)}, u32[]{:S(2)}, u32[]{:S(2)}) async-start(bf16[32,6,2,128]{3,2,1,0:T(2,128)(2,1)} %bitcast.8), calls=%async_computation | async-start | bytes 196608 | tf_op jit(solution)/shard_map/all_to_all | solution.py:516
  17.1 7.9 %copy-start.1 = (f32[32]{0:T(128)S(1)}, f32[32]{0:T(128)}, u32[]{:S(2)}) copy-start(f32[32]{0:T(128)} %param.11) | copy-start | bytes 388
  17.2 7.8 %collective-permute-start.6 = (bf16[160,384]{1,0:T(8,128)(2,1)S(1)}, bf16[160,384]{1,0:T(8,128)(2,1)S(1)}, u32[]{:S(2)}, u32[]{:S(2)}) collective-permute-start(bf16[160,384]{1,0:T(8,128)(2,1)S(1)} %shard_map.116.mine_ref), channel_id=1, source_target_pairs={{0,16},{4,20},{8,24},{12,28},{16,0},{20,4},{24,8},{28,12},{1,17},{... | collective-permute-start | bytes 368648 | tf_op jit(solution)/shard_map/ppermute | solution.py:123
  25.7 7.3 %collective-permute-start.7 = (f32[64,128]{1,0:T(8,128)S(1)}, f32[64,128]{1,0:T(8,128)S(1)}, u32[]{:S(2)}, u32[]{:S(2)}) collective-permute-start(f32[64,128]{1,0:T(8,128)S(1)} %get-tuple-element.58.part_ref), channel_id=1, source_target_pairs={{0,2},{1,3},{2,0},{3,1},{4,6},{5,7},{6,4},{7,5},{8,10},{9,11},{10,... | collective-permute-start | bytes 98312 | tf_op jit(solution)/shard_map/ppermute | solution.py:535
  27.1 6.0 %collective-permute-start.8 = (bf16[48,256]{1,0:T(8,128)(2,1)S(1)}, bf16[48,256]{1,0:T(8,128)(2,1)S(1)}, u32[]{:S(2)}, u32[]{:S(2)}) collective-permute-start(bf16[48,256]{1,0:T(8,128)(2,1)S(1)} %get-tuple-element.59), channel_id=1, source_target_pairs={{1,2},{2,1},{3,0},{0,3},{5,6},{6,5},{7,4},{4,7},{9,10},{10,9},{11,... | collective-permute-start | bytes 73736 | tf_op jit(solution)/shard_map/ppermute | solution.py:31
  28.5 4.5 %collective-permute-start.9 = (bf16[48,256]{1,0:T(8,128)(2,1)S(1)}, bf16[48,256]{1,0:T(8,128)(2,1)S(1)}, u32[]{:S(2)}, u32[]{:S(2)}) collective-permute-start(bf16[48,256]{1,0:T(8,128)(2,1)S(1)} %get-tuple-element.60), channel_id=1, source_target_pairs={{0,1},{1,0},{2,3},{3,2},{4,5},{5,4},{6,7},{7,6},{8,9},{9,8},{10,11... | collective-permute-start | bytes 73736 | tf_op jit(solution)/shard_map/ppermute | solution.py:31
  29.3 3.7 %collective-permute-start.10 = (bf16[32,256]{1,0:T(8,128)(2,1)S(1)}, bf16[32,256]{1,0:T(8,128)(2,1)S(1)}, u32[]{:S(2)}, u32[]{:S(2)}) collective-permute-start(bf16[32,256]{1,0:T(8,128)(2,1)S(1)} %get-tuple-element.61), channel_id=1, source_target_pairs={{0,1},{1,0},{2,3},{3,2},{4,8},{5,9},{6,10},{7,11},{8,4},{9,5},{10,... | collective-permute-start | bytes 49160 | tf_op jit(solution)/shard_map/ppermute | solution.py:43
  30.5 2.5 %collective-permute-start.11 = (bf16[32,256]{1,0:T(8,128)(2,1)S(1)}, bf16[32,256]{1,0:T(8,128)(2,1)S(1)}, u32[]{:S(2)}, u32[]{:S(2)}) collective-permute-start(bf16[32,256]{1,0:T(8,128)(2,1)S(1)} %get-tuple-element.62), channel_id=1, source_target_pairs={{0,4},{4,0},{8,12},{12,8},{16,20},{20,16},{24,28},{28,24},{1,5},{5... | collective-permute-start | bytes 49160 | tf_op jit(solution)/shard_map/ppermute | solution.py:31

commit v8 on v7

--- a/solution.py
+++ b/solution.py
@@ -43,13 +43,14 @@
     return lax.ppermute(value, ("gx", "col"), pairs)
 
 
-def swap_faces(faces):
-    return (
-        swap(faces[0], "col", 1),
-        swap(faces[1], "col", 0),
-        swap_second(faces[2]),
-        swap(faces[3], "gx", 0),
-    )
+def swap_faces(faces, first=0):
+    swaps = (
+        lambda face: swap(face, "col", 1),
+        lambda face: swap(face, "col", 0),
+        swap_second,
+        lambda face: swap(face, "gx", 0),
+    )
+    return [swaps[first + i](face) for i, face in enumerate(faces)]
 
 
 def swap_counts():
@@ -73,9 +74,9 @@
     return places
 
 
-def put_faces(perm_ref, source, outs):
+def put_faces(perm_ref, source, outs, first=0):
     blocks = [source[:, b * BLK : (b + 1) * BLK] for b in range(source.shape[1] // BLK)]
-    for i, place in enumerate(swapped_places(perm_ref)):
+    for i, place in enumerate(swapped_places(perm_ref)[2 * first : 2 * (first + len(outs))]):
         chosen = blocks[0]
         for b in range(1, len(blocks)):
             chosen = jnp.where(place == b, blocks[b], chosen)
@@ -94,6 +95,21 @@
     for b in range(blocks):
         chosen = parts[0]
         for place, part in zip(places[1:], parts[1:]):
+            chosen = jnp.where(place == b, part, chosen)
+        yield slice(b * BLK, (b + 1) * BLK), chosen
+
+
+def some_received_blocks(perm_ref, received, blocks, first):
+    places = swapped_places(perm_ref)[2 * first :]
+    parts = []
+    for i, got in enumerate(received):
+        counts = swap_counts()[first + i]
+        for j in range(2):
+            part = got[:, j * BLK : (j + 1) * BLK].astype(F32)
+            parts.append(part if counts is None else jnp.where(counts, part, 0.0))
+    for b in range(blocks):
+        chosen = jnp.zeros_like(parts[0])
+        for place, part in zip(places, parts):
             chosen = jnp.where(place == b, part, chosen)
         yield slice(b * BLK, (b + 1) * BLK), chosen
 
@@ -392,10 +408,16 @@
         out_ref[i * step : (i + 1) * step] = several
 
 
-def frame_kernel(depth, weight_ref, r_ref, q_ref, basis_ref, r_out, q_out, picks_ref, basis_out):
-    r_out[...] = weight_ref[0:1, :] * r_ref[...]
-    q_out[...] = weight_ref[0:1, :] * q_ref[...]
+def frame_kernel(depth, perm_ref, weight_ref, r_ref, q_ref, basis_ref, r_out, q_out, picks_ref, basis_out, f2, f3):
+    weighted_r = weight_ref[0:1, :] * r_ref[...]
+    weighted_q = weight_ref[0:1, :] * q_ref[...]
+    r_out[...] = weighted_r
+    q_out[...] = weighted_q
     prim = basis_ref.shape[0]
+    n = r_ref.shape[0]
+    weighted_basis = weight_ref[0:1, :] * basis_ref[...].astype(F32)
+    blank = jnp.zeros((f2.shape[0] - 2 * n - prim, r_ref.shape[1]), F32)
+    put_faces(perm_ref, jnp.concatenate([weighted_r, weighted_q, weighted_basis, blank], axis=0), (f2, f3), 2)
     half = prim // 2
     rows = basis_out.shape[0]
     slabs, sectors = lax.axis_size("gx"), lax.axis_size("col")
@@ -414,8 +436,8 @@
     basis_out[...] = jnp.dot(here, basis_ref[...], preferred_element_type=F32).astype(BF16)
 
 
-def near_solve_kernel(perm_ref, gathered_ref, mine_ref, got_ref, picks_ref, prev_ref, weight_ref, basis_ref,
-                      sol_r_ref, sol_q_ref, step_out, weighted_out, base_out, part_out, f0, f1, f2, f3, rhs_ref):
+def near_solve_kernel(r2, r3, perm_ref, gathered_ref, mine_ref, got_ref, picks_ref, prev_ref, weight_ref, basis_ref,
+                      sol_r_ref, sol_q_ref, step_out, weighted_out, base_out, part_out, sol_out, f0, f1, rhs_ref):
     n = prev_ref.shape[1]
     slabs = lax.axis_size("gx")
     width = gathered_ref.shape[0] // slabs
@@ -435,6 +457,7 @@
     step = prev_ref[...] / curvature
     sol = (total[:, 0:n] - step * total[:, n : 2 * n]).astype(BF16)
     rhs = picked[16:, 0:n] - step * picked[16:, n : 2 * n]
+    sol_out[...] = sol
     high, low = split(jnp.sum(sol.astype(F32) * rhs, axis=0, keepdims=True))
     correction = lax.dot_general(
         sol, basis_ref[...], (((0,), (0,)), ((), ())), preferred_element_type=F32
@@ -448,14 +471,34 @@
     base = first - step * (second - step * third)
     base_out[...] = jnp.broadcast_to(jnp.concatenate([base, blank], axis=1), base_out.shape)
     part_out[...] = jnp.broadcast_to(jnp.concatenate([high + low, blank], axis=1), part_out.shape)
-    put_faces(perm_ref, weighted, (f0, f1, f2, f3))
+    put_faces(perm_ref, weighted, (f0, f1))
     lines = jnp.concatenate([high, low, jnp.zeros((14, n), F32)], axis=0)
     lines = jnp.concatenate([lines, jnp.zeros((16, 2 * BLK - n), F32)], axis=1).astype(BF16)
-    f0[n:, :] = lines
-    f1[n:, :] = lines
-
-
-def near_direction_kernel(perm_ref, rz_ref, dir_ref, weighted_ref, base_ref, part_ref, far_ref, r0, r1, r2, r3,
+    f0[n : n + 16, :] = lines
+    f1[n : n + 16, :] = lines
+
+
+def beside_kernel(perm_ref, sol_ref, step_ref, weighted_ref, r2, r3, out_ref):
+    n = weighted_ref.shape[0]
+    slab, slabs = lax.axis_index("gx"), lax.axis_size("gx")
+    prim = sol_ref.shape[0] // slabs
+    received = []
+    for got, other in ((r2, jnp.where(slab % 2 == 1, slab + 1, slab - 1)), (r3, slab + 1 - 2 * (slab % 2))):
+        rows = got.shape[0] - 2 * n
+        row = lax.broadcasted_iota(jnp.int32, (rows, sol_ref.shape[0]), 0)
+        lane = lax.broadcasted_iota(jnp.int32, (rows, sol_ref.shape[0]), 1)
+        chosen = jnp.logical_and(row < prim, lane == other * prim + row)
+        sol = jnp.dot(jnp.where(chosen, 1.0, 0.0).astype(BF16), sol_ref[...], preferred_element_type=F32)
+        correction = lax.dot_general(
+            sol.astype(BF16), got[2 * n :, :], (((0,), (0,)), ((), ())), preferred_element_type=F32
+        )
+        step = step_ref[:, 0:1]
+        received.append(got[0:n, :].astype(F32) - step * got[n : 2 * n, :].astype(F32) + correction)
+    for at, part in some_received_blocks(perm_ref, received, weighted_ref.shape[1] // BLK, 2):
+        out_ref[:, at] = weighted_ref[:, at] + part
+
+
+def near_direction_kernel(perm_ref, rz_ref, dir_ref, weighted_ref, base_ref, part_ref, far_ref, r0, r1,
                           out_ref, rz_out):
     n = rz_ref.shape[1]
     sector = lax.axis_index("col")
@@ -472,8 +515,8 @@
         rz_next = rz_next + value
     rz_out[...] = rz_next
     factor = to_column(rz_next / rz_ref[...])
-    received = (r0[0:n, :], r1[0:n, :], r2[...], r3[...])
-    for at, part in received_blocks(perm_ref, received, dir_ref.shape[1] // BLK):
+    received = (r0[0:n, :], r1[0:n, :])
+    for at, part in some_received_blocks(perm_ref, received, dir_ref.shape[1] // BLK, 0):
         out_ref[:, at] = weighted_ref[:, at] + factor * dir_ref[:, at] + part
 
 
@@ -514,30 +557,42 @@
     got = swap_bit(blocks, 2)
     packed = packed.reshape(slabs * sectors, rows // 2, 2, BLK)
     gathered = lax.all_to_all(packed, ("gx", "col"), 0, 0).reshape(slabs * sectors * rows, BLK)
-    sol_r, sol_q, picks, placed = call(
+    face = jax.ShapeDtypeStruct((-(-(2 * rhs + prim) // 16) * 16, 2 * BLK), BF16)
+    sol_r, sol_q, picks, placed, f2, f3 = call(
         functools.partial(frame_kernel, rows),
         (
             full,
             full,
             jax.ShapeDtypeStruct((16 + slabs * prim, slabs * shard[1]), BF16),
             jax.ShapeDtypeStruct((slabs * prim, width), BF16),
+            face,
+            face,
         ),
-        weight, sol_r, sol_q, basis_t,
-    )
-    face = jax.ShapeDtypeStruct((rhs, 2 * BLK), BF16)
+        perm, weight, sol_r, sol_q, basis_t,
+    )
+    r2, r3 = swap_faces((f2, f3), 2)
     tall = jax.ShapeDtypeStruct((rhs + 16, 2 * BLK), BF16)
-    step, weighted, base, part, *faces = call(
+    step, weighted, base, part, sol, f0, f1 = call(
         near_solve_kernel,
-        (jax.ShapeDtypeStruct((rhs, BLK), F32), full, line, jax.ShapeDtypeStruct((64, BLK), F32), tall, tall, face, face),
+        (
+            jax.ShapeDtypeStruct((rhs, BLK), F32),
+            full,
+            line,
+            jax.ShapeDtypeStruct((8, BLK), F32),
+            jax.ShapeDtypeStruct((slabs * prim, rhs), BF16),
+            jax.ShapeDtypeStruct((64, 2 * BLK), BF16),
+            jax.ShapeDtypeStruct((48, 2 * BLK), BF16),
+        ),
         perm, gathered, blocks, got, picks, rz_row, weight, placed, sol_r, sol_q,
-        scratch=[pltpu.VMEM((slabs * shard[1], 2 * rhs), BF16)],
+        scratch=[pltpu.VMEM((slabs * shard[1], 2 * rhs), BF16)], after=(r2, r3),
     )
     far = lax.ppermute(part, "col", [(i, i ^ 2) for i in range(sectors)])
-    received = swap_faces(faces)
+    r0, r1 = swap_faces((f0, f1))
+    (weighted,) = call(beside_kernel, (full,), perm, sol, step, weighted, r2, r3)
     (resid_new,) = call(resid_kernel, (full,), step, resid, assembled)
     direction_new, rz_next = call(
         near_direction_kernel, (full, jax.ShapeDtypeStruct((1, rhs), F32)),
-        perm, rz_row, direction, weighted, base, part, far, *received,
+        perm, rz_row, direction, weighted, base, part, far, r0, r1,
     )
     return (resid_new[None, None], direction_new[None, None], rz_next[0])
 

time: 34.1 us -> 33.4 us (0.979)
  waiting for transfers between devices: 7.33 us -> 4.81 us
  starting transfers between devices: 18.8 us -> 20 us
  Pallas kernels: 6.64 us -> 7.23 us
    all_to_all x1, waiting for transfers between devices: 5.55 us -> 1.47 us  [near_rest(): lax.all_to_all(packed, ('gx', 'col'), 0, 0)]
    ppermute x1, starting transfers between devices: 1.35 us -> 2.51 us  [near_rest(): far = lax.ppermute(part, 'col', [(i, i ^ 2) for i in range(sectors)])]
    ppermute x2, waiting for transfers between devices: 1.75 us -> 2.58 us  [swap_second(): return lax.ppermute(value, ('gx', 'col'), pairs)]
    ppermute x1, waiting for transfers between devices: 0.01 us -> 0.74 us  [near_rest(): far = lax.ppermute(part, 'col', [(i, i ^ 2) for i in range(sectors)])]
    pallas_call x7 -> x8, Pallas kernels: 4.36 us -> 4.94 us  [call(): pl.pallas_call(kernel, out_shape=outs, in_specs=[pl.BlockSpec(memory_spac...]
  transfers between devices with their start and end apart: 13 -> 13, of which waited for: 2 -> 3; matrix products, arithmetic and copies ran while one was open for 1% -> 1% of each run, Pallas kernels for 9% -> 11%
where the time goes in v8:
time: 33.4 us; the launch traced here: 33.2 us
  starting transfers between devices  20 us (60%)
  Pallas kernels  7.23 us (22%)
  waiting for transfers between devices  4.81 us (14%)
  between operations  0.79 us (2%)
  local copies, waits for them, and re-layouts  0.37 us (1%)
    ppermute x6, starting transfers between devices, swap(): return lax.ppermute(value, axis, pairs)  6.73 us
    pallas_call x8, Pallas kernels, call(): pl.pallas_call(kernel, out_shape=outs, in_specs=[pl.BlockSpec(memory_spac...  4.94 us
    all_to_all x1, starting transfers between devices, near_rest(): lax.all_to_all(packed, ('gx', 'col'), 0, 0)  3.75 us
    ppermute x2, starting transfers between devices, swap_second(): return lax.ppermute(value, ('gx', 'col'), pairs)  3.55 us
    ppermute x3, starting transfers between devices, swap_bit(): return lax.ppermute(value, 'gx', [(i, i ^ 1 << k) for i in range(count)])  3.49 us
    ppermute x2, waiting for transfers between devices, swap_second(): return lax.ppermute(value, ('gx', 'col'), pairs)  2.58 us
    ppermute x1, starting transfers between devices, near_rest(): far = lax.ppermute(part, 'col', [(i, i ^ 2) for i in range(sectors)])  2.51 us
    pallas_call x1, Pallas kernels, body(): pl.pallas_call(image_kernel, out_shape=(full,) + (face,) * 4 + (full, ful...  2.02 us
  transfers between devices with their start and end apart: 13, of which 3 were waited for; matrix products, arithmetic and copies ran while one was open for 1% of the time, Pallas kernels for 11%

profile of v8, /device:TPU:0, one launch (start us, length us, event | category | flops | bytes accessed | tf_op | source)
XLA Modules:
  0.0 33.2 jit_solution(2868007103055051226)
XLA Ops:
  0.6 0.0 copy-start
  0.6 0.0 copy-start.3
  0.7 2.0 %shard_map.112 = (f32[32,1024]{1,0:T(8,128)S(1)}, bf16[32,256]{1,0:T(8,128)(2,1)S(1)}, bf16[32,256]{1,0:T(8,128)(2,1)S(1)}, bf16[32,256]{1,0:T(8,128)(2,1)S(1)},...) custom-call(s32[1,8]{1,0:T(1,128)} %bitcast.16, ...), custom_call_target="tpu_custom_call" | custom-call | flops 67108864 | bytes 2097152 | tf_op jit(solution)/shard_map/pallas_call | solution.py:625
  2.7 0.5 %collective-permute-start.6 = (bf16[8,20,4,20]{3,2,1,0:T(4,128)(2,1)S(1)}, bf16[8,20,4,20]{3,2,1,0:T(4,128)(2,1)S(1)}, u32[]{:S(2)}, u32[]{:S(2)}) collective-permute-start(bf16[8,20,4,20]{3,2,1,0:T(4,128)(2,1)S(1)} %get-tuple-element.52), channel_id=1, source_target_pairs={{0,4},{4,0},{8,12},{12,8},{16,20},{20,16},{24,28},{28,24},{1,5},{5... | collective-permute-start | bytes 76808 | tf_op jit(solution)/shard_map/ppermute | solution.py:139
  3.2 4.7 %collective-permute-start = (bf16[32,256]{1,0:T(8,128)(2,1)S(1)}, bf16[32,256]{1,0:T(8,128)(2,1)S(1)}, u32[]{:S(2)}, u32[]{:S(2)}) collective-permute-start(bf16[32,256]{1,0:T(8,128)(2,1)S(1)} %get-tuple-element.40), channel_id=1, source_target_pairs={{1,2},{2,1},{3,0},{0,3},{5,6},{6,5},{7,4},{4,7},{9,10},{10,9},{11,... | collective-permute-start | bytes 49160 | tf_op jit(solution)/shard_map/ppermute | solution.py:31
  7.9 0.0 collective-permute-start.1
  7.9 2.0 %collective-permute-start.2 = (bf16[32,256]{1,0:T(8,128)(2,1)S(1)}, bf16[32,256]{1,0:T(8,128)(2,1)S(1)}, u32[]{:S(2)}, u32[]{:S(2)}) collective-permute-start(bf16[32,256]{1,0:T(8,128)(2,1)S(1)} %get-tuple-element.42), channel_id=1, source_target_pairs={{0,1},{1,0},{2,3},{3,2},{4,8},{5,9},{6,10},{7,11},{8,4},{9,5},{10,... | collective-permute-start | bytes 49160 | tf_op jit(solution)/shard_map/ppermute | solution.py:43
  9.9 0.0 collective-permute-start.3
  9.9 0.1 reshape.20.own_ref
  10.0 0.0 copy-done.3
  10.1 0.1 copy.12.conduct_ref
  10.1 0.0 collective-permute-done.6
  10.1 0.1 reshape.21.mate_ref
  10.3 0.0 copy-done
  10.3 0.0 copy-start.2
  10.3 0.3 shard_map.113
  10.6 0.2 shard_map.116.mine_ref
  10.8 1.1 %collective-permute-start.7 = (bf16[2,160,96]{2,1,0:T(8,128)(2,1)S(1)}, bf16[2,160,96]{2,1,0:T(8,128)(2,1)S(1)}, u32[]{:S(2)}, u32[]{:S(2)}) collective-permute-start(bf16[2,160,96]{2,1,0:T(8,128)(2,1)S(1)} %shard_map.116.mine_ref), channel_id=1, source_target_pairs={{0,8},{4,12},{8,0},{12,4},{16,24},{20,28},{24,16},{28,20},{1,9},{5... | collective-permute-start | bytes 184328 | tf_op jit(solution)/shard_map/ppermute | solution.py:139
  11.9 0.0 collective-permute-done.r0
  11.9 0.0 collective-permute-done.1.r1
  11.9 0.0 collective-permute-done.2.r2
  11.9 0.0 collective-permute-done.3.r3
  11.9 0.0 copy-done.2
  11.9 1.4 %shard_map.114 = (f32[32,1024]{1,0:T(8,128)S(1)}, f32[32,1024]{1,0:T(8,128)S(1)}, f32[32,1024]{1,0:T(8,128)S(1)}, bf16[384,128]{1,0:T(8,128)(2,1)}) custom-call(s32[1,8]{1,0:T(1,128)S(1)} %bitcast.19, f32[32,1024]{1,0:T(8,128)S(1)} %get-tuple-element.36.image_ref, bf16[32,256]{1,0:T(8,128)(2,1)S(1)} %collective-permute-done.r0, ...), custom_call_target="tpu_custom_call" | custom-call | flops 67108864000 | bytes 65536 | tf_op jit(solution)/shard_map/pallas_call | solution.py:534
  13.3 3.8 %all-to-all-start = ((bf16[32,6,2,128]{3,2,1,0:T(2,128)(2,1)}), bf16[32,6,2,128]{3,2,1,0:T(2,128)(2,1)S(1)}, u32[]{:S(2)}, u32[]{:S(2)}) async-start(bf16[32,6,2,128]{3,2,1,0:T(2,128)(2,1)} %bitcast.8), calls=%async_computation | async-start | bytes 196608 | tf_op jit(solution)/shard_map/all_to_all | solution.py:559
  17.1 0.0 copy-start.1
  17.1 0.0 collective-permute-done.7.got_ref
  17.1 0.1 shard_map.117.mine_ref
  17.2 1.8 %collective-permute-start.8 = (bf16[160,384]{1,0:T(8,128)(2,1)S(1)}, bf16[160,384]{1,0:T(8,128)(2,1)S(1)}, u32[]{:S(2)}, u32[]{:S(2)}) collective-permute-start(bf16[160,384]{1,0:T(8,128)(2,1)S(1)} %shard_map.117.mine_ref), channel_id=1, source_target_pairs={{0,16},{4,20},{8,24},{12,28},{16,0},{20,4},{24,8},{28,12},{1,17},{... | collective-permute-start | bytes 368648 | tf_op jit(solution)/shard_map/ppermute | solution.py:139
  19.1 0.5 %shard_map.115 = (f32[32,1024]{1,0:T(8,128)S(1)}, f32[32,1024]{1,0:T(8,128)S(1)}, bf16[176,768]{1,0:T(8,128)(2,1)S(1)}, bf16[160,1024]{1,0:T(8,128)(2,1)S(1)}, b...) custom-call(s32[1,8]{1,0:T(1,128)S(1)} %bitcast.20, f32[8,1024]{1,0:T(8,128)S(1)} %get-tuple-element.39.weight_ref, ...), custom_call_target="tpu_custom_call" | custom-call | flops 1024 | bytes 65536 | tf_op jit(solution)/shard_map/pallas_call | solution.py:534
  19.6 1.5 %collective-permute-start.4 = (bf16[96,256]{1,0:T(8,128)(2,1)S(1)}, bf16[96,256]{1,0:T(8,128)(2,1)S(1)}, u32[]{:S(2)}, u32[]{:S(2)}) collective-permute-start(bf16[96,256]{1,0:T(8,128)(2,1)S(1)} %get-tuple-element.49), channel_id=1, source_target_pairs={{0,1},{1,0},{2,3},{3,2},{4,8},{5,9},{6,10},{7,11},{8,4},{9,5},{10,... | collective-permute-start | bytes 147464 | tf_op jit(solution)/shard_map/ppermute | solution.py:43
  21.1 0.1 collective-permute-start.5
  21.2 2.6 %collective-permute-done.4.r2 = bf16[96,256]{1,0:T(8,128)(2,1)S(1)} collective-permute-done((bf16[96,256]{1,0:T(8,128)(2,1)S(1)}, bf16[96,256]{1,0:T(8,128)(2,1)S(1)}, u32[]{:S(2)}, u32[]{:S(2)}) %collective-permute-start.4) | collective-permute-done | bytes 49184 | tf_op jit(solution)/shard_map/ppermute | solution.py:43
  23.8 0.0 collective-permute-done.5.r3
  23.8 1.5 %all-to-all-done = bf16[32,6,2,128]{3,2,1,0:T(2,128)(2,1)S(1)} async-done(((bf16[32,6,2,128]{3,2,1,0:T(2,128)(2,1)}), bf16[32,6,2,128]{3,2,1,0:T(2,128)(2,1)S(1)}, u32[]{:S(2)}, u32[]{:S(2)}) %all-to-all-start) | async-done | bytes 98336 | tf_op jit(solution)/shard_map/all_to_all | solution.py:559
  25.3 0.0 collective-permute-done.8.got_ref
  25.3 0.0 copy-done.1
  25.3 0.7 %shard_map.118 = (f32[32,128]{1,0:T(8,128)S(1)}, f32[32,1024]{1,0:T(8,128)S(1)}, f32[8,128]{1,0:T(8,128)S(1)}, f32[8,128]{1,0:T(8,128)S(1)}, bf16[160,32]{1,0:T(...) custom-call(bf16[96,256]{1,0:T(8,128)(2,1)S(1)} %collective-permute-done.4.r2, ...), custom_call_target="tpu_custom_call" | custom-call | flops 1024 | bytes 65536 | tf_op jit(solution)/shard_map/pallas_call | solution.py:534
  26.0 1.9 %collective-permute-start.10 = (bf16[64,256]{1,0:T(8,128)(2,1)S(1)}, bf16[64,256]{1,0:T(8,128)(2,1)S(1)}, u32[]{:S(2)}, u32[]{:S(2)}) collective-permute-start(bf16[64,256]{1,0:T(8,128)(2,1)S(1)} %get-tuple-element.63), channel_id=1, source_target_pairs={{1,2},{2,1},{3,0},{0,3},{5,6},{6,5},{7,4},{4,7},{9,10},{10,9},{11,... | collective-permute-start | bytes 98312 | tf_op jit(solution)/shard_map/ppermute | solution.py:31
  27.9 0.0 collective-permute-start.11
  27.9 2.5 %collective-permute-start.9 = (f32[8,128]{1,0:T(8,128)S(1)}, f32[8,128]{1,0:T(8,128)S(1)}, u32[]{:S(2)}, u32[]{:S(2)}) collective-permute-start(f32[8,128]{1,0:T(8,128)S(1)} %get-tuple-element.62.part_ref), channel_id=1, source_target_pairs={{0,2},{1,3},{2,0},{3,1},{4,6},{5,7},{6,4},{7,5},{8,10},{9,11},{10,... | collective-permute-start | bytes 12296 | tf_op jit(solution)/shard_map/ppermute | solution.py:589
  30.4 0.7 %shard_map.119 = f32[32,1024]{1,0:T(8,128)} custom-call(f32[32,128]{1,0:T(8,128)S(1)} %get-tuple-element.57.step_ref, f32[32,1024]{1,0:T(8,128)S(1)} %get-tuple-element.37.resid_ref, f32[32,1024]{1,0:T(8,128)S(1)} %get-tuple-element.58.assembled_ref), custom_call_target="tpu_custom_call" | custom-call | flops 1024 | bytes 65536 | tf_op jit(solution)/shard_map/pallas_call | solution.py:534
  31.2 0.5 %shard_map.120.weighted_ref = f32[32,1024]{1,0:T(8,128)S(1)} custom-call(s32[1,8]{1,0:T(1,128)S(1)} %bitcast.22, bf16[160,32]{1,0:T(8,128)(2,1)S(1)} %get-tuple-element.59.sol_ref, f32[32,128]{1,0:T(8,128)S(1)} %get-tuple-element.57.step_ref, f32[32,1024]{1,0:T(8,128)S(1)} %get-tuple-element.60.weighted_ref, bf16[96,256]{1,0:T(8,128)(2,1)S(1)} %collective-permute-done.4.r2, ...), custom_call_target="tpu_custom_call" | custom-call | flops 1024 | bytes 65536 | tf_op jit(solution)/shard_map/pallas_call | solution.py:534
  31.7 0.7 %collective-permute-done.9.far_ref = f32[8,128]{1,0:T(8,128)S(1)} collective-permute-done((f32[8,128]{1,0:T(8,128)S(1)}, f32[8,128]{1,0:T(8,128)S(1)}, u32[]{:S(2)}, u32[]{:S(2)}) %collective-permute-start.9) | collective-permute-done | bytes 4128 | tf_op jit(solution)/shard_map/ppermute | solution.py:589
  32.4 0.0 collective-permute-done.11.r1
  32.4 0.0 collective-permute-done.10.r0
  32.4 0.8 %shard_map.121 = (f32[32,1024]{1,0:T(8,128)}, f32[1,32]{1,0:T(1,128)}) custom-call(s32[1,8]{1,0:T(1,128)S(1)} %bitcast.23, f32[1,32]{1,0:T(1,128)S(1)} %bitcast.25, f32[32,1024]{1,0:T(8,128)S(1)} %get-tuple-element.35.dir_ref, f32[32,1024]{1,0:T(8,128)S(1)} %shard_map.120.weighted_ref, f32[8,128]{1,0:T(8,128)S(1)} %get-tuple-element.61.base_ref, ...), custom_call_target="tpu_custom_call" | custom-call | flops 1024 | bytes 65536 | tf_op jit(solution)/shard_map/pallas_call | solution.py:534
Async XLA Ops:
  0.6 9.6 %copy-start = (s32[1,1,8]{2,1,0:T(1,128)S(1)}, s32[1,1,8]{2,1,0:T(1,128)}, u32[]{:S(2)}) copy-start(s32[1,1,8]{2,1,0:T(1,128)} %param.17) | copy-start | bytes 100
  0.6 9.4 %copy-start.3 = (f32[8,4]{0,1:T(4,128)S(1)}, f32[8,4]{0,1:T(4,128)}, u32[]{:S(2)}) copy-start(f32[8,4]{0,1:T(4,128)} %param.16) | copy-start | bytes 388
  2.7 7.5 %collective-permute-start.6 = (bf16[8,20,4,20]{3,2,1,0:T(4,128)(2,1)S(1)}, bf16[8,20,4,20]{3,2,1,0:T(4,128)(2,1)S(1)}, u32[]{:S(2)}, u32[]{:S(2)}) collective-permute-start(bf16[8,20,4,20]{3,2,1,0:T(4,128)(2,1)S(1)} %get-tuple-element.52), channel_id=1, source_target_pairs={{0,4},{4,0},{8,12},{12,8},{16,20},{20,16},{24,28},{28,24},{1,5},{5... | collective-permute-start | bytes 76808 | tf_op jit(solution)/shard_map/ppermute | solution.py:139
  3.2 8.7 %collective-permute-start = (bf16[32,256]{1,0:T(8,128)(2,1)S(1)}, bf16[32,256]{1,0:T(8,128)(2,1)S(1)}, u32[]{:S(2)}, u32[]{:S(2)}) collective-permute-start(bf16[32,256]{1,0:T(8,128)(2,1)S(1)} %get-tuple-element.40), channel_id=1, source_target_pairs={{1,2},{2,1},{3,0},{0,3},{5,6},{6,5},{7,4},{4,7},{9,10},{10,9},{11,... | collective-permute-start | bytes 49160 | tf_op jit(solution)/shard_map/ppermute | solution.py:31
  7.9 4.0 %collective-permute-start.1 = (bf16[32,256]{1,0:T(8,128)(2,1)S(1)}, bf16[32,256]{1,0:T(8,128)(2,1)S(1)}, u32[]{:S(2)}, u32[]{:S(2)}) collective-permute-start(bf16[32,256]{1,0:T(8,128)(2,1)S(1)} %get-tuple-element.41), channel_id=1, source_target_pairs={{0,1},{1,0},{2,3},{3,2},{4,5},{5,4},{6,7},{7,6},{8,9},{9,8},{10,11... | collective-permute-start | bytes 49160 | tf_op jit(solution)/shard_map/ppermute | solution.py:31
  7.9 4.0 %collective-permute-start.2 = (bf16[32,256]{1,0:T(8,128)(2,1)S(1)}, bf16[32,256]{1,0:T(8,128)(2,1)S(1)}, u32[]{:S(2)}, u32[]{:S(2)}) collective-permute-start(bf16[32,256]{1,0:T(8,128)(2,1)S(1)} %get-tuple-element.42), channel_id=1, source_target_pairs={{0,1},{1,0},{2,3},{3,2},{4,8},{5,9},{6,10},{7,11},{8,4},{9,5},{10,... | collective-permute-start | bytes 49160 | tf_op jit(solution)/shard_map/ppermute | solution.py:43
  9.9 2.0 %collective-permute-start.3 = (bf16[32,256]{1,0:T(8,128)(2,1)S(1)}, bf16[32,256]{1,0:T(8,128)(2,1)S(1)}, u32[]{:S(2)}, u32[]{:S(2)}) collective-permute-start(bf16[32,256]{1,0:T(8,128)(2,1)S(1)} %get-tuple-element.43), channel_id=1, source_target_pairs={{0,4},{4,0},{8,12},{12,8},{16,20},{20,16},{24,28},{28,24},{1,5},{5... | collective-permute-start | bytes 49160 | tf_op jit(solution)/shard_map/ppermute | solution.py:31
  10.3 1.6 %copy-start.2 = (bf16[1,1,1024,1024]{3,2,1,0:T(8,128)(2,1)S(1)}, bf16[1,1,1024,1024]{3,2,1,0:T(8,128)(2,1)}, u32[]{:S(2)}) copy-start(bf16[1,1,1024,1024]{3,2,1,0:T(8,128)(2,1)} %param.13) | copy-start | bytes 6291460
  10.8 6.3 %collective-permute-start.7 = (bf16[2,160,96]{2,1,0:T(8,128)(2,1)S(1)}, bf16[2,160,96]{2,1,0:T(8,128)(2,1)S(1)}, u32[]{:S(2)}, u32[]{:S(2)}) collective-permute-start(bf16[2,160,96]{2,1,0:T(8,128)(2,1)S(1)} %shard_map.116.mine_ref), channel_id=1, source_target_pairs={{0,8},{4,12},{8,0},{12,4},{16,24},{20,28},{24,16},{28,20},{1,9},{5... | collective-permute-start | bytes 184328 | tf_op jit(solution)/shard_map/ppermute | solution.py:139
  13.3 12.0 %all-to-all-start = ((bf16[32,6,2,128]{3,2,1,0:T(2,128)(2,1)}), bf16[32,6,2,128]{3,2,1,0:T(2,128)(2,1)S(1)}, u32[]{:S(2)}, u32[]{:S(2)}) async-start(bf16[32,6,2,128]{3,2,1,0:T(2,128)(2,1)} %bitcast.8), calls=%async_computation | async-start | bytes 196608 | tf_op jit(solution)/shard_map/all_to_all | solution.py:559
  17.1 8.2 %copy-start.1 = (f32[32]{0:T(128)S(1)}, f32[32]{0:T(128)}, u32[]{:S(2)}) copy-start(f32[32]{0:T(128)} %param.11) | copy-start | bytes 388
  17.2 8.0 %collective-permute-start.8 = (bf16[160,384]{1,0:T(8,128)(2,1)S(1)}, bf16[160,384]{1,0:T(8,128)(2,1)S(1)}, u32[]{:S(2)}, u32[]{:S(2)}) collective-permute-start(bf16[160,384]{1,0:T(8,128)(2,1)S(1)} %shard_map.117.mine_ref), channel_id=1, source_target_pairs={{0,16},{4,20},{8,24},{12,28},{16,0},{20,4},{24,8},{28,12},{1,17},{... | collective-permute-start | bytes 368648 | tf_op jit(solution)/shard_map/ppermute | solution.py:139
  19.6 4.2 %collective-permute-start.4 = (bf16[96,256]{1,0:T(8,128)(2,1)S(1)}, bf16[96,256]{1,0:T(8,128)(2,1)S(1)}, u32[]{:S(2)}, u32[]{:S(2)}) collective-permute-start(bf16[96,256]{1,0:T(8,128)(2,1)S(1)} %get-tuple-element.49), channel_id=1, source_target_pairs={{0,1},{1,0},{2,3},{3,2},{4,8},{5,9},{6,10},{7,11},{8,4},{9,5},{10,... | collective-permute-start | bytes 147464 | tf_op jit(solution)/shard_map/ppermute | solution.py:43
  21.1 2.7 %collective-permute-start.5 = (bf16[96,256]{1,0:T(8,128)(2,1)S(1)}, bf16[96,256]{1,0:T(8,128)(2,1)S(1)}, u32[]{:S(2)}, u32[]{:S(2)}) collective-permute-start(bf16[96,256]{1,0:T(8,128)(2,1)S(1)} %get-tuple-element.50), channel_id=1, source_target_pairs={{0,4},{4,0},{8,12},{12,8},{16,20},{20,16},{24,28},{28,24},{1,5},{5... | collective-permute-start | bytes 147464 | tf_op jit(solution)/shard_map/ppermute | solution.py:31
  26.0 6.5 %collective-permute-start.10 = (bf16[64,256]{1,0:T(8,128)(2,1)S(1)}, bf16[64,256]{1,0:T(8,128)(2,1)S(1)}, u32[]{:S(2)}, u32[]{:S(2)}) collective-permute-start(bf16[64,256]{1,0:T(8,128)(2,1)S(1)} %get-tuple-element.63), channel_id=1, source_target_pairs={{1,2},{2,1},{3,0},{0,3},{5,6},{6,5},{7,4},{4,7},{9,10},{10,9},{11,... | collective-permute-start | bytes 98312 | tf_op jit(solution)/shard_map/ppermute | solution.py:31
  27.9 4.5 %collective-permute-start.11 = (bf16[48,256]{1,0:T(8,128)(2,1)S(1)}, bf16[48,256]{1,0:T(8,128)(2,1)S(1)}, u32[]{:S(2)}, u32[]{:S(2)}) collective-permute-start(bf16[48,256]{1,0:T(8,128)(2,1)S(1)} %get-tuple-element.64), channel_id=1, source_target_pairs={{0,1},{1,0},{2,3},{3,2},{4,5},{5,4},{6,7},{7,6},{8,9},{9,8},{10,11... | collective-permute-start | bytes 73736 | tf_op jit(solution)/shard_map/ppermute | solution.py:31
  27.9 4.5 %collective-permute-start.9 = (f32[8,128]{1,0:T(8,128)S(1)}, f32[8,128]{1,0:T(8,128)S(1)}, u32[]{:S(2)}, u32[]{:S(2)}) collective-permute-start(f32[8,128]{1,0:T(8,128)S(1)} %get-tuple-element.62.part_ref), channel_id=1, source_target_pairs={{0,2},{1,3},{2,0},{3,1},{4,6},{5,7},{6,4},{7,5},{8,10},{9,11},{10,... | collective-permute-start | bytes 12296 | tf_op jit(solution)/shard_map/ppermute | solution.py:589

commit v9 on v8

--- a/solution.py
+++ b/solution.py
@@ -139,29 +139,33 @@
     return lax.ppermute(value, "gx", [(i, i ^ (1 << k)) for i in range(count)])
 
 
-def image_kernel(perm_hbm, dir_hbm, schur_hbm, resid_hbm, basis_hbm, coarse_hbm,
-                 image_ref, f0, f1, f2, f3, dir_ref, resid_ref, basis_ref, coarse_ref, *rest):
-    *send_ref, perm_ref, schur_ref, sems = rest
+def image_kernel(perm_hbm, dir_hbm, schur_hbm, resid_hbm, basis_hbm, coarse_hbm, conduct_hbm,
+                 image_ref, f0, f1, f2, f3, dir_ref, resid_ref, basis_ref, coarse_ref, weight_ref, rhs_ref,
+                 scaled_ref, *rest):
+    *send_ref, perm_ref, conduct_ref, schur_ref, sems = rest
     rows = schur_ref.shape[0] // CHUNKS
     parts = [pl.ds(i * rows, rows) for i in range(CHUNKS)]
-    pairs = [(dir_hbm, dir_ref), (perm_hbm, perm_ref)]
+    pairs = [(dir_hbm, dir_ref), (perm_hbm, perm_ref), (conduct_hbm, conduct_ref)]
+    pairs += [(resid_hbm, resid_ref), (basis_hbm, basis_ref)]
+    small = len(pairs)
     pairs += [(schur_hbm.at[part], schur_ref.at[part]) for part in parts]
     for ref in send_ref:
         pairs += [(coarse_hbm.at[other_block(i, 0)], ref.at[i]) for i in range(ref.shape[0])]
-    pairs += [(resid_hbm, resid_ref), (basis_hbm, basis_ref), (coarse_hbm, coarse_ref)]
+    pairs += [(coarse_hbm, coarse_ref)]
     copies = [pltpu.make_async_copy(source, target, sems.at[i]) for i, (source, target) in enumerate(pairs)]
     for copy in copies:
         copy.start()
-    copies[0].wait()
+    for copy in copies[:small]:
+        copy.wait()
+    early_part(perm_ref, conduct_ref, resid_ref, basis_ref, weight_ref, rhs_ref, scaled_ref)
     total = None
     for i, part in enumerate(parts):
-        copies[2 + i].wait()
+        copies[small + i].wait()
         term = jnp.dot(dir_ref[:, part].astype(BF16), schur_ref[part], preferred_element_type=F32)
         total = term if total is None else total + term
     image_ref[...] = total
-    copies[1].wait()
     put_faces(perm_ref, total, (f0, f1, f2, f3))
-    for copy in copies[2 + CHUNKS :]:
+    for copy in copies[small + CHUNKS :]:
         copy.wait()
 
 
@@ -213,23 +217,20 @@
         send_ref[i] = blocks_ref[other_block(i, k)]
 
 
-def conduct_at(row, sector):
+def conduct_at(row, slab):
     lane = lax.broadcasted_iota(jnp.int32, row.shape, 1)
-    return jnp.sum(jnp.where(lane == sector, row, 0.0), axis=1, keepdims=True)
-
-
-def early_kernel(perm_ref, conduct_ref, dir_ref, image_ref, resid_ref, basis_ref,
-                 weight_ref, rhs_ref, curv_ref, scaled_ref):
+    return jnp.sum(jnp.where(lane == slab, row, 0.0), axis=1, keepdims=True)
+
+
+def early_part(perm_ref, conduct_ref, resid_ref, basis_ref, weight_ref, rhs_ref, scaled_ref):
     slab, sector = lax.axis_index("gx"), lax.axis_index("col")
     slabs, sectors = lax.axis_size("gx"), lax.axis_size("col")
-    row = conduct_ref[pl.ds(slab, 1), :]
-    own = conduct_at(row, sector)
-    below = conduct_at(conduct_ref[pl.ds(jnp.maximum(slab - 1, 0), 1), :], sector)
-    above = conduct_at(conduct_ref[pl.ds(jnp.minimum(slab + 1, slabs - 1), 1), :], sector)
-    below = jnp.where(slab > 0, below, 0.0)
-    above = jnp.where(slab < slabs - 1, above, 0.0)
-    left = conduct_at(row, (sector + sectors - 1) % sectors)
-    right = conduct_at(row, (sector + 1) % sectors)
+    row = conduct_ref[pl.ds(sector, 1), :]
+    own = conduct_at(row, slab)
+    below = jnp.where(slab > 0, conduct_at(row, slab - 1), 0.0)
+    above = jnp.where(slab < slabs - 1, conduct_at(row, slab + 1), 0.0)
+    left = conduct_at(conduct_ref[pl.ds((sector + sectors - 1) % sectors, 1), :], slab)
+    right = conduct_at(conduct_ref[pl.ds((sector + 1) % sectors, 1), :], slab)
     across = [jnp.broadcast_to(own / (own + other), (1, BLK)) for other in (below, above, left, right)]
     places = [slot_place(perm_ref, slot) for slot in range(8)]
     for b in range(weight_ref.shape[1] // BLK):
@@ -242,15 +243,15 @@
     rhs_ref[...] = lax.dot_general(
         basis_ref[...], scaled, (((1,), (1,)), ((), ())), preferred_element_type=F32
     )
+
+
+def curvature_part(dir_ref, image_ref):
     curv = to_row(jnp.sum(dir_ref[...] * image_ref[...], axis=1, keepdims=True))
     high = curv.astype(BF16).astype(F32)
-    n = curv.shape[1]
-    curv_ref[...] = jnp.zeros_like(curv_ref)
-    curv_ref[0:1, 0:n] = high
-    curv_ref[0:1, n : 2 * n] = curv - high
-
-
-def coarse_rhs_kernel(rows, sectors, perm_ref, image_ref, r0, r1, r2, r3, weight_ref, basis_ref, rhs_ref, curv_ref,
+    return high, curv - high
+
+
+def coarse_rhs_kernel(rows, sectors, perm_ref, image_ref, r0, r1, r2, r3, weight_ref, basis_ref, rhs_ref, dir_ref,
                       assembled_ref, scaled_ref, rhs_q_ref, out_ref):
     for at, part in received_blocks(perm_ref, (r0, r1, r2, r3), image_ref.shape[1] // BLK):
         assembled_ref[:, at] = image_ref[:, at] + part
@@ -263,8 +264,10 @@
     rhs_r = rhs_ref[...]
     half = rhs_r.shape[0] // 2
     packed = jnp.concatenate([rhs_r[:half], rhs_q[:half], rhs_r[half:], rhs_q[half:]], axis=1)
+    high, low = curvature_part(dir_ref, image_ref)
+    line = jnp.concatenate([high, low, jnp.zeros_like(high), jnp.zeros_like(high)], axis=1)
     packed = jnp.concatenate(
-        [packed, curv_ref[0:1, :], jnp.zeros((rows - half - 1, BLK), F32)], axis=0
+        [packed, line, jnp.zeros((rows - half - 1, BLK), F32)], axis=0
     )
     several = jnp.concatenate([packed] * sectors, axis=0).astype(BF16)
     step = several.shape[0]
@@ -378,7 +381,7 @@
     out_ref[...] = jnp.concatenate([both_ref[i] for i in range(2 * n)], axis=1)
 
 
-def near_rhs_kernel(rows, sectors, perm_ref, image_ref, r0, r1, r2, r3, weight_ref, basis_ref, rhs_ref, curv_ref,
+def near_rhs_kernel(rows, sectors, perm_ref, image_ref, r0, r1, r2, r3, weight_ref, basis_ref, rhs_ref, dir_ref,
                     scaled_ref, resid_ref, neumann_ref, assembled_ref, sol_r_ref, sol_q_ref, out_ref):
     for at, part in received_blocks(perm_ref, (r0, r1, r2, r3), image_ref.shape[1] // BLK):
         assembled_ref[:, at] = image_ref[:, at] + part
@@ -396,7 +399,7 @@
     sol_q_ref[...] = sol_q
     products = (weighted_r * sol_r, weighted_r * sol_q + weighted_q * sol_r, weighted_q * sol_q)
     sums = [to_row(jnp.sum(product, axis=1, keepdims=True)) for product in products]
-    first = jnp.concatenate([curv_ref[0:1, : 2 * n], *split(sums[0])], axis=1)
+    first = jnp.concatenate([*curvature_part(dir_ref, image_ref), *split(sums[0])], axis=1)
     second = jnp.concatenate([*split(sums[1]), *split(sums[2])], axis=1)
     rhs_r = rhs_ref[...]
     half = rhs_r.shape[0] // 2
@@ -520,7 +523,7 @@
         out_ref[:, at] = weighted_ref[:, at] + factor * dir_ref[:, at] + part
 
 
-def near_rest(perm, rz_row, neumann, image, received, weight, rhs_r, curv, scaled_r, direction, resid, basis_t,
+def near_rest(perm, rz_row, neumann, image, received, weight, rhs_r, scaled_r, direction, resid, basis_t,
               coarse, rows):
     rhs, width = resid.shape
     prim = basis_t.shape[0]
@@ -542,11 +545,12 @@
     (blocks,) = call(
         spread_pair_kernel, (jax.ShapeDtypeStruct((2,) + shard, BF16),),
         coarse.reshape(flat), mate.reshape(flat), after=(perm,),
+        estimate=cost(2000 * rhs * width * width, 1 << 16),
     )
     assembled, sol_r, sol_q, packed = call(
         functools.partial(near_rhs_kernel, rows, sectors),
         (full, full, full, jax.ShapeDtypeStruct((slabs * sectors * rows, BLK), BF16)),
-        perm, image, *received, weight, basis_t, rhs_r, curv, scaled_r, resid, neumann,
+        perm, image, *received, weight, basis_t, rhs_r, direction, scaled_r, resid, neumann,
         estimate=cost(2000 * rhs * width * width, 1 << 16),
     )
     (blocks,) = call(
@@ -621,33 +625,29 @@
 
     near = sectors == 4 and slabs == 8
     sends = () if near else (send_type,)
-    fetched = [pltpu.with_memory_space_constraint(x, pltpu.HBM) for x in (perm, direction, schur, resid, basis_t, coarse)]
-    image, f0, f1, f2, f3, direction, resid, basis_t, coarse, *send = pl.pallas_call(
+    fetched = [pltpu.with_memory_space_constraint(x, pltpu.HBM) for x in (perm, direction, schur, resid, basis_t, coarse, conduct.T)]
+    image, f0, f1, f2, f3, direction, resid, basis_t, coarse, weight, rhs_r, scaled_r, *send = pl.pallas_call(
         image_kernel,
         out_shape=(full,) + (face,) * 4
-        + (full, full, jax.ShapeDtypeStruct((prim, width), BF16), coarse_type) + sends,
-        in_specs=[hbm] * 6, out_specs=(vmem,) * (9 + len(sends)),
+        + (full, full, jax.ShapeDtypeStruct((prim, width), BF16), coarse_type)
+        + (
+            jax.ShapeDtypeStruct((8, width), F32),
+            jax.ShapeDtypeStruct((prim, rhs), F32),
+            jax.ShapeDtypeStruct((rhs, width), BF16),
+        )
+        + sends,
+        in_specs=[hbm] * 7, out_specs=(vmem,) * (12 + len(sends)),
         scratch_shapes=[
             pltpu.VMEM(perm.shape, jnp.int32),
+            pltpu.VMEM((sectors, slabs), F32),
             pltpu.VMEM((width, width), BF16),
-            pltpu.SemaphoreType.DMA((CHUNKS + 5 + len(sends) * (slabs // 2),)),
+            pltpu.SemaphoreType.DMA((CHUNKS + 6 + len(sends) * (slabs // 2),)),
         ],
         compiler_params=params(), cost_estimate=cost(flops, 2 * width * width),
     )(*fetched)
     received = swap_faces((f0, f1, f2, f3))
-    weight, rhs_r, curv, scaled_r = pl.pallas_call(
-        early_kernel,
-        out_shape=(
-            jax.ShapeDtypeStruct((8, width), F32),
-            jax.ShapeDtypeStruct((prim, rhs), F32),
-            jax.ShapeDtypeStruct((8, BLK), F32),
-            jax.ShapeDtypeStruct((rhs, width), BF16),
-        ),
-        in_specs=[vmem] * 6, out_specs=(vmem,) * 4, compiler_params=params(),
-        cost_estimate=cost(1000 * flops, 8 * rhs * width),
-    )(perm, conduct, direction, image, resid, basis_t)
     if near:
-        return near_rest(perm, rz_row, neumann, image, received, weight, rhs_r, curv, scaled_r, direction, resid,
+        return near_rest(perm, rz_row, neumann, image, received, weight, rhs_r, scaled_r, direction, resid,
                          basis_t, coarse, rows)
     send = send[0]
     for k in range(rounds - 1):
@@ -683,7 +683,7 @@
         ),
         in_specs=[vmem] + [vmem] * 9, out_specs=(vmem,) * 4, compiler_params=params(),
         cost_estimate=cost(2 * rhs * width * prim, 8 * rhs * width),
-    )(perm, image, *received, weight, basis_t, rhs_r, curv)
+    )(perm, image, *received, weight, basis_t, rhs_r, direction)
     packed = packed.reshape(slabs * sectors, rows // 2, 2, BLK)
     gathered = lax.all_to_all(packed, ("gx", "col"), 0, 0).reshape(slabs * sectors * rows, BLK)
     sol_r, sol_q, sums = pl.pallas_call(

time: 33.4 us -> 33.5 us (level)
  transfers between devices with their start and end apart: 13 -> 13, of which waited for: 3 -> 5; matrix products, arithmetic and copies ran while one was open for 1% -> 1% of each run, Pallas kernels for 11% -> 10%
where the time goes in v9:
time: 33.5 us; the launch traced here: 33.2 us
  starting transfers between devices  20.2 us (60%)
  Pallas kernels  6.95 us (21%)
  waiting for transfers between devices  5.06 us (15%)
  between operations  0.76 us (2%)
    ppermute x6, starting transfers between devices, swap(): return lax.ppermute(value, axis, pairs)  6.73 us
    pallas_call x8, Pallas kernels, call(): pl.pallas_call(kernel, out_shape=outs, in_specs=[pl.BlockSpec(memory_spac...  4.92 us
    all_to_all x1, starting transfers between devices, near_rest(): lax.all_to_all(packed, ('gx', 'col'), 0, 0)  3.89 us
    ppermute x2, starting transfers between devices, swap_second(): return lax.ppermute(value, ('gx', 'col'), pairs)  3.55 us
    ppermute x3, starting transfers between devices, swap_bit(): return lax.ppermute(value, 'gx', [(i, i ^ 1 << k) for i in range(count)])  3.49 us
    ppermute x2, waiting for transfers between devices, swap_second(): return lax.ppermute(value, ('gx', 'col'), pairs)  2.75 us
    ppermute x1, starting transfers between devices, near_rest(): far = lax.ppermute(part, 'col', [(i, i ^ 2) for i in range(sectors)])  2.51 us
    pallas_call x1, Pallas kernels, body(): pl.pallas_call(image_kernel, out_shape=(full,) + (face,) * 4 + (full, ful...  2.03 us
  transfers between devices with their start and end apart: 13, of which 5 were waited for; matrix products, arithmetic and copies ran while one was open for 1% of the time, Pallas kernels for 10%

profile of v9, /device:TPU:0, one launch (start us, length us, event | category | flops | bytes accessed | tf_op | source)
XLA Modules:
  0.0 33.2 jit_solution(18216957607609541978)
XLA Ops:
  0.6 0.0 copy-start
  0.6 2.0 %shard_map.112 = (f32[32,1024]{1,0:T(8,128)S(1)}, bf16[32,256]{1,0:T(8,128)(2,1)S(1)}, bf16[32,256]{1,0:T(8,128)(2,1)S(1)}, bf16[32,256]{1,0:T(8,128)(2,1)S(1)},...) custom-call(s32[1,8]{1,0:T(1,128)} %bitcast.17, ...), custom_call_target="tpu_custom_call" | custom-call | flops 67108864 | bytes 2097152 | tf_op jit(solution)/shard_map/pallas_call | solution.py:629
  2.7 0.5 %collective-permute-start.6 = (bf16[8,20,4,20]{3,2,1,0:T(4,128)(2,1)S(1)}, bf16[8,20,4,20]{3,2,1,0:T(4,128)(2,1)S(1)}, u32[]{:S(2)}, u32[]{:S(2)}) collective-permute-start(bf16[8,20,4,20]{3,2,1,0:T(4,128)(2,1)S(1)} %get-tuple-element.50), channel_id=1, source_target_pairs={{0,4},{4,0},{8,12},{12,8},{16,20},{20,16},{24,28},{28,24},{1,5},{5... | collective-permute-start | bytes 76808 | tf_op jit(solution)/shard_map/ppermute | solution.py:139
  3.2 4.7 %collective-permute-start = (bf16[32,256]{1,0:T(8,128)(2,1)S(1)}, bf16[32,256]{1,0:T(8,128)(2,1)S(1)}, u32[]{:S(2)}, u32[]{:S(2)}) collective-permute-start(bf16[32,256]{1,0:T(8,128)(2,1)S(1)} %get-tuple-element.36), channel_id=1, source_target_pairs={{1,2},{2,1},{3,0},{0,3},{5,6},{6,5},{7,4},{4,7},{9,10},{10,9},{11,... | collective-permute-start | bytes 49160 | tf_op jit(solution)/shard_map/ppermute | solution.py:31
  7.9 0.0 collective-permute-start.1
  7.9 2.0 %collective-permute-start.2 = (bf16[32,256]{1,0:T(8,128)(2,1)S(1)}, bf16[32,256]{1,0:T(8,128)(2,1)S(1)}, u32[]{:S(2)}, u32[]{:S(2)}) collective-permute-start(bf16[32,256]{1,0:T(8,128)(2,1)S(1)} %get-tuple-element.38), channel_id=1, source_target_pairs={{0,1},{1,0},{2,3},{3,2},{4,8},{5,9},{6,10},{7,11},{8,4},{9,5},{10,... | collective-permute-start | bytes 49160 | tf_op jit(solution)/shard_map/ppermute | solution.py:43
  9.9 0.0 collective-permute-start.3
  9.9 0.1 reshape.20.own_ref
  10.0 0.0 collective-permute-done.6
  10.1 0.1 reshape.21.mate_ref
  10.2 0.0 copy-done
  10.2 0.0 copy-start.2
  10.2 0.2 shard_map.115.mine_ref
  10.4 1.1 %collective-permute-start.7 = (bf16[2,160,96]{2,1,0:T(8,128)(2,1)S(1)}, bf16[2,160,96]{2,1,0:T(8,128)(2,1)S(1)}, u32[]{:S(2)}, u32[]{:S(2)}) collective-permute-start(bf16[2,160,96]{2,1,0:T(8,128)(2,1)S(1)} %shard_map.115.mine_ref), channel_id=1, source_target_pairs={{0,8},{4,12},{8,0},{12,4},{16,24},{20,28},{24,16},{28,20},{1,9},{5... | collective-permute-start | bytes 184328 | tf_op jit(solution)/shard_map/ppermute | solution.py:139
  11.5 0.0 collective-permute-done.r0
  11.5 0.1 collective-permute-done.1.r1
  11.6 0.2 collective-permute-done.2.r2
  11.8 0.0 collective-permute-done.3.r3
  11.8 0.0 copy-done.2
  11.8 1.4 %shard_map.113 = (f32[32,1024]{1,0:T(8,128)S(1)}, f32[32,1024]{1,0:T(8,128)S(1)}, f32[32,1024]{1,0:T(8,128)S(1)}, bf16[384,128]{1,0:T(8,128)(2,1)}) custom-call(s32[1,8]{1,0:T(1,128)S(1)} %bitcast.19, f32[32,1024]{1,0:T(8,128)S(1)} %get-tuple-element.35.image_ref, bf16[32,256]{1,0:T(8,128)(2,1)S(1)} %collective-permute-done.r0, ...), custom_call_target="tpu_custom_call" | custom-call | flops 67108864000 | bytes 65536 | tf_op jit(solution)/shard_map/pallas_call | solution.py:537
  13.2 3.9 %all-to-all-start = ((bf16[32,6,2,128]{3,2,1,0:T(2,128)(2,1)}), bf16[32,6,2,128]{3,2,1,0:T(2,128)(2,1)S(1)}, u32[]{:S(2)}, u32[]{:S(2)}) async-start(bf16[32,6,2,128]{3,2,1,0:T(2,128)(2,1)} %bitcast.9), calls=%async_computation | async-start | bytes 196608 | tf_op jit(solution)/shard_map/all_to_all | solution.py:563
  17.1 0.0 copy-start.1
  17.1 0.0 collective-permute-done.7.got_ref
  17.1 0.1 shard_map.116.mine_ref
  17.3 1.8 %collective-permute-start.8 = (bf16[160,384]{1,0:T(8,128)(2,1)S(1)}, bf16[160,384]{1,0:T(8,128)(2,1)S(1)}, u32[]{:S(2)}, u32[]{:S(2)}) collective-permute-start(bf16[160,384]{1,0:T(8,128)(2,1)S(1)} %shard_map.116.mine_ref), channel_id=1, source_target_pairs={{0,16},{4,20},{8,24},{12,28},{16,0},{20,4},{24,8},{28,12},{1,17},{... | collective-permute-start | bytes 368648 | tf_op jit(solution)/shard_map/ppermute | solution.py:139
  19.1 0.5 %shard_map.114 = (f32[32,1024]{1,0:T(8,128)S(1)}, f32[32,1024]{1,0:T(8,128)S(1)}, bf16[176,768]{1,0:T(8,128)(2,1)S(1)}, bf16[160,1024]{1,0:T(8,128)(2,1)S(1)}, b...) custom-call(s32[1,8]{1,0:T(1,128)S(1)} %bitcast.20, f32[8,1024]{1,0:T(8,128)S(1)} %get-tuple-element.34.weight_ref, ...), custom_call_target="tpu_custom_call" | custom-call | flops 1024 | bytes 65536 | tf_op jit(solution)/shard_map/pallas_call | solution.py:537
  19.6 1.5 %collective-permute-start.4 = (bf16[96,256]{1,0:T(8,128)(2,1)S(1)}, bf16[96,256]{1,0:T(8,128)(2,1)S(1)}, u32[]{:S(2)}, u32[]{:S(2)}) collective-permute-start(bf16[96,256]{1,0:T(8,128)(2,1)S(1)} %get-tuple-element.47), channel_id=1, source_target_pairs={{0,1},{1,0},{2,3},{3,2},{4,8},{5,9},{6,10},{7,11},{8,4},{9,5},{10,... | collective-permute-start | bytes 147464 | tf_op jit(solution)/shard_map/ppermute | solution.py:43
  21.1 0.1 collective-permute-start.5
  21.2 2.6 %collective-permute-done.4.r2 = bf16[96,256]{1,0:T(8,128)(2,1)S(1)} collective-permute-done((bf16[96,256]{1,0:T(8,128)(2,1)S(1)}, bf16[96,256]{1,0:T(8,128)(2,1)S(1)}, u32[]{:S(2)}, u32[]{:S(2)}) %collective-permute-start.4) | collective-permute-done | bytes 49184 | tf_op jit(solution)/shard_map/ppermute | solution.py:43
  23.8 0.0 collective-permute-done.5.r3
  23.8 1.5 %all-to-all-done = bf16[32,6,2,128]{3,2,1,0:T(2,128)(2,1)S(1)} async-done(((bf16[32,6,2,128]{3,2,1,0:T(2,128)(2,1)}), bf16[32,6,2,128]{3,2,1,0:T(2,128)(2,1)S(1)}, u32[]{:S(2)}, u32[]{:S(2)}) %all-to-all-start) | async-done | bytes 98336 | tf_op jit(solution)/shard_map/all_to_all | solution.py:563
  25.3 0.0 collective-permute-done.8.got_ref
  25.3 0.0 copy-done.1
  25.3 0.7 %shard_map.117 = (f32[32,128]{1,0:T(8,128)S(1)}, f32[32,1024]{1,0:T(8,128)S(1)}, f32[8,128]{1,0:T(8,128)S(1)}, f32[8,128]{1,0:T(8,128)S(1)}, bf16[160,32]{1,0:T(...) custom-call(bf16[96,256]{1,0:T(8,128)(2,1)S(1)} %collective-permute-done.4.r2, ...), custom_call_target="tpu_custom_call" | custom-call | flops 1024 | bytes 65536 | tf_op jit(solution)/shard_map/pallas_call | solution.py:537
  26.0 1.9 %collective-permute-start.10 = (bf16[64,256]{1,0:T(8,128)(2,1)S(1)}, bf16[64,256]{1,0:T(8,128)(2,1)S(1)}, u32[]{:S(2)}, u32[]{:S(2)}) collective-permute-start(bf16[64,256]{1,0:T(8,128)(2,1)S(1)} %get-tuple-element.61), channel_id=1, source_target_pairs={{1,2},{2,1},{3,0},{0,3},{5,6},{6,5},{7,4},{4,7},{9,10},{10,9},{11,... | collective-permute-start | bytes 98312 | tf_op jit(solution)/shard_map/ppermute | solution.py:31
  27.9 0.0 collective-permute-start.11
  27.9 2.5 %collective-permute-start.9 = (f32[8,128]{1,0:T(8,128)S(1)}, f32[8,128]{1,0:T(8,128)S(1)}, u32[]{:S(2)}, u32[]{:S(2)}) collective-permute-start(f32[8,128]{1,0:T(8,128)S(1)} %get-tuple-element.60.part_ref), channel_id=1, source_target_pairs={{0,2},{1,3},{2,0},{3,1},{4,6},{5,7},{6,4},{7,5},{8,10},{9,11},{10,... | collective-permute-start | bytes 12296 | tf_op jit(solution)/shard_map/ppermute | solution.py:593
  30.4 0.7 %shard_map.118 = f32[32,1024]{1,0:T(8,128)} custom-call(f32[32,128]{1,0:T(8,128)S(1)} %get-tuple-element.55.step_ref, f32[32,1024]{1,0:T(8,128)S(1)} %get-tuple-element.44.resid_ref, f32[32,1024]{1,0:T(8,128)S(1)} %get-tuple-element.56.assembled_ref), custom_call_target="tpu_custom_call" | custom-call | flops 1024 | bytes 65536 | tf_op jit(solution)/shard_map/pallas_call | solution.py:537
  31.2 0.5 %shard_map.119.weighted_ref = f32[32,1024]{1,0:T(8,128)S(1)} custom-call(s32[1,8]{1,0:T(1,128)S(1)} %bitcast.22, bf16[160,32]{1,0:T(8,128)(2,1)S(1)} %get-tuple-element.57.sol_ref, f32[32,128]{1,0:T(8,128)S(1)} %get-tuple-element.55.step_ref, f32[32,1024]{1,0:T(8,128)S(1)} %get-tuple-element.58.weighted_ref, bf16[96,256]{1,0:T(8,128)(2,1)S(1)} %collective-permute-done.4.r2, ...), custom_call_target="tpu_custom_call" | custom-call | flops 1024 | bytes 65536 | tf_op jit(solution)/shard_map/pallas_call | solution.py:537
  31.7 0.7 %collective-permute-done.9.far_ref = f32[8,128]{1,0:T(8,128)S(1)} collective-permute-done((f32[8,128]{1,0:T(8,128)S(1)}, f32[8,128]{1,0:T(8,128)S(1)}, u32[]{:S(2)}, u32[]{:S(2)}) %collective-permute-start.9) | collective-permute-done | bytes 4128 | tf_op jit(solution)/shard_map/ppermute | solution.py:593
  32.4 0.0 collective-permute-done.11.r1
  32.4 0.0 collective-permute-done.10.r0
  32.4 0.8 %shard_map.120 = (f32[32,1024]{1,0:T(8,128)}, f32[1,32]{1,0:T(1,128)}) custom-call(s32[1,8]{1,0:T(1,128)S(1)} %bitcast.23, f32[1,32]{1,0:T(1,128)S(1)} %bitcast.25, f32[32,1024]{1,0:T(8,128)S(1)} %get-tuple-element.42.dir_ref, f32[32,1024]{1,0:T(8,128)S(1)} %shard_map.119.weighted_ref, f32[8,128]{1,0:T(8,128)S(1)} %get-tuple-element.59.base_ref, ...), custom_call_target="tpu_custom_call" | custom-call | flops 1024 | bytes 65536 | tf_op jit(solution)/shard_map/pallas_call | solution.py:537
Async XLA Ops:
  0.6 9.6 %copy-start = (s32[1,1,8]{2,1,0:T(1,128)S(1)}, s32[1,1,8]{2,1,0:T(1,128)}, u32[]{:S(2)}) copy-start(s32[1,1,8]{2,1,0:T(1,128)} %param.17) | copy-start | bytes 100
  2.7 7.4 %collective-permute-start.6 = (bf16[8,20,4,20]{3,2,1,0:T(4,128)(2,1)S(1)}, bf16[8,20,4,20]{3,2,1,0:T(4,128)(2,1)S(1)}, u32[]{:S(2)}, u32[]{:S(2)}) collective-permute-start(bf16[8,20,4,20]{3,2,1,0:T(4,128)(2,1)S(1)} %get-tuple-element.50), channel_id=1, source_target_pairs={{0,4},{4,0},{8,12},{12,8},{16,20},{20,16},{24,28},{28,24},{1,5},{5... | collective-permute-start | bytes 76808 | tf_op jit(solution)/shard_map/ppermute | solution.py:139
  3.2 8.3 %collective-permute-start = (bf16[32,256]{1,0:T(8,128)(2,1)S(1)}, bf16[32,256]{1,0:T(8,128)(2,1)S(1)}, u32[]{:S(2)}, u32[]{:S(2)}) collective-permute-start(bf16[32,256]{1,0:T(8,128)(2,1)S(1)} %get-tuple-element.36), channel_id=1, source_target_pairs={{1,2},{2,1},{3,0},{0,3},{5,6},{6,5},{7,4},{4,7},{9,10},{10,9},{11,... | collective-permute-start | bytes 49160 | tf_op jit(solution)/shard_map/ppermute | solution.py:31
  7.9 3.7 %collective-permute-start.1 = (bf16[32,256]{1,0:T(8,128)(2,1)S(1)}, bf16[32,256]{1,0:T(8,128)(2,1)S(1)}, u32[]{:S(2)}, u32[]{:S(2)}) collective-permute-start(bf16[32,256]{1,0:T(8,128)(2,1)S(1)} %get-tuple-element.37), channel_id=1, source_target_pairs={{0,1},{1,0},{2,3},{3,2},{4,5},{5,4},{6,7},{7,6},{8,9},{9,8},{10,11... | collective-permute-start | bytes 49160 | tf_op jit(solution)/shard_map/ppermute | solution.py:31
  7.9 3.9 %collective-permute-start.2 = (bf16[32,256]{1,0:T(8,128)(2,1)S(1)}, bf16[32,256]{1,0:T(8,128)(2,1)S(1)}, u32[]{:S(2)}, u32[]{:S(2)}) collective-permute-start(bf16[32,256]{1,0:T(8,128)(2,1)S(1)} %get-tuple-element.38), channel_id=1, source_target_pairs={{0,1},{1,0},{2,3},{3,2},{4,8},{5,9},{6,10},{7,11},{8,4},{9,5},{10,... | collective-permute-start | bytes 49160 | tf_op jit(solution)/shard_map/ppermute | solution.py:43
  9.9 1.9 %collective-permute-start.3 = (bf16[32,256]{1,0:T(8,128)(2,1)S(1)}, bf16[32,256]{1,0:T(8,128)(2,1)S(1)}, u32[]{:S(2)}, u32[]{:S(2)}) collective-permute-start(bf16[32,256]{1,0:T(8,128)(2,1)S(1)} %get-tuple-element.39), channel_id=1, source_target_pairs={{0,4},{4,0},{8,12},{12,8},{16,20},{20,16},{24,28},{28,24},{1,5},{5... | collective-permute-start | bytes 49160 | tf_op jit(solution)/shard_map/ppermute | solution.py:31
  10.2 1.6 %copy-start.2 = (bf16[1,1,1024,1024]{3,2,1,0:T(8,128)(2,1)S(1)}, bf16[1,1,1024,1024]{3,2,1,0:T(8,128)(2,1)}, u32[]{:S(2)}) copy-start(bf16[1,1,1024,1024]{3,2,1,0:T(8,128)(2,1)} %param.13) | copy-start | bytes 6291460
  10.4 6.7 %collective-permute-start.7 = (bf16[2,160,96]{2,1,0:T(8,128)(2,1)S(1)}, bf16[2,160,96]{2,1,0:T(8,128)(2,1)S(1)}, u32[]{:S(2)}, u32[]{:S(2)}) collective-permute-start(bf16[2,160,96]{2,1,0:T(8,128)(2,1)S(1)} %shard_map.115.mine_ref), channel_id=1, source_target_pairs={{0,8},{4,12},{8,0},{12,4},{16,24},{20,28},{24,16},{28,20},{1,9},{5... | collective-permute-start | bytes 184328 | tf_op jit(solution)/shard_map/ppermute | solution.py:139
  13.2 12.1 %all-to-all-start = ((bf16[32,6,2,128]{3,2,1,0:T(2,128)(2,1)}), bf16[32,6,2,128]{3,2,1,0:T(2,128)(2,1)S(1)}, u32[]{:S(2)}, u32[]{:S(2)}) async-start(bf16[32,6,2,128]{3,2,1,0:T(2,128)(2,1)} %bitcast.9), calls=%async_computation | async-start | bytes 196608 | tf_op jit(solution)/shard_map/all_to_all | solution.py:563
  17.1 8.2 %copy-start.1 = (f32[32]{0:T(128)S(1)}, f32[32]{0:T(128)}, u32[]{:S(2)}) copy-start(f32[32]{0:T(128)} %param.11) | copy-start | bytes 388
  17.3 8.0 %collective-permute-start.8 = (bf16[160,384]{1,0:T(8,128)(2,1)S(1)}, bf16[160,384]{1,0:T(8,128)(2,1)S(1)}, u32[]{:S(2)}, u32[]{:S(2)}) collective-permute-start(bf16[160,384]{1,0:T(8,128)(2,1)S(1)} %shard_map.116.mine_ref), channel_id=1, source_target_pairs={{0,16},{4,20},{8,24},{12,28},{16,0},{20,4},{24,8},{28,12},{1,17},{... | collective-permute-start | bytes 368648 | tf_op jit(solution)/shard_map/ppermute | solution.py:139
  19.6 4.2 %collective-permute-start.4 = (bf16[96,256]{1,0:T(8,128)(2,1)S(1)}, bf16[96,256]{1,0:T(8,128)(2,1)S(1)}, u32[]{:S(2)}, u32[]{:S(2)}) collective-permute-start(bf16[96,256]{1,0:T(8,128)(2,1)S(1)} %get-tuple-element.47), channel_id=1, source_target_pairs={{0,1},{1,0},{2,3},{3,2},{4,8},{5,9},{6,10},{7,11},{8,4},{9,5},{10,... | collective-permute-start | bytes 147464 | tf_op jit(solution)/shard_map/ppermute | solution.py:43
  21.1 2.7 %collective-permute-start.5 = (bf16[96,256]{1,0:T(8,128)(2,1)S(1)}, bf16[96,256]{1,0:T(8,128)(2,1)S(1)}, u32[]{:S(2)}, u32[]{:S(2)}) collective-permute-start(bf16[96,256]{1,0:T(8,128)(2,1)S(1)} %get-tuple-element.48), channel_id=1, source_target_pairs={{0,4},{4,0},{8,12},{12,8},{16,20},{20,16},{24,28},{28,24},{1,5},{5... | collective-permute-start | bytes 147464 | tf_op jit(solution)/shard_map/ppermute | solution.py:31
  26.0 6.5 %collective-permute-start.10 = (bf16[64,256]{1,0:T(8,128)(2,1)S(1)}, bf16[64,256]{1,0:T(8,128)(2,1)S(1)}, u32[]{:S(2)}, u32[]{:S(2)}) collective-permute-start(bf16[64,256]{1,0:T(8,128)(2,1)S(1)} %get-tuple-element.61), channel_id=1, source_target_pairs={{1,2},{2,1},{3,0},{0,3},{5,6},{6,5},{7,4},{4,7},{9,10},{10,9},{11,... | collective-permute-start | bytes 98312 | tf_op jit(solution)/shard_map/ppermute | solution.py:31
  27.9 4.5 %collective-permute-start.11 = (bf16[48,256]{1,0:T(8,128)(2,1)S(1)}, bf16[48,256]{1,0:T(8,128)(2,1)S(1)}, u32[]{:S(2)}, u32[]{:S(2)}) collective-permute-start(bf16[48,256]{1,0:T(8,128)(2,1)S(1)} %get-tuple-element.62), channel_id=1, source_target_pairs={{0,1},{1,0},{2,3},{3,2},{4,5},{5,4},{6,7},{7,6},{8,9},{9,8},{10,11... | collective-permute-start | bytes 73736 | tf_op jit(solution)/shard_map/ppermute | solution.py:31
  27.9 4.5 %collective-permute-start.9 = (f32[8,128]{1,0:T(8,128)S(1)}, f32[8,128]{1,0:T(8,128)S(1)}, u32[]{:S(2)}, u32[]{:S(2)}) collective-permute-start(f32[8,128]{1,0:T(8,128)S(1)} %get-tuple-element.60.part_ref), channel_id=1, source_target_pairs={{0,2},{1,3},{2,0},{3,1},{4,6},{5,7},{6,4},{7,5},{8,10},{9,11},{10,... | collective-permute-start | bytes 12296 | tf_op jit(solution)/shard_map/ppermute | solution.py:593
